TPU v7x, 32 devices: a whole 2x2x4 slice. The times are simulated.
32 devices in a mesh: section: 2 (over x), shard: 16 (over z, y, core).
Axes of the slice: x: 2, y: 2, z: 4, core: 2. Of those that a mesh axis runs over, the one named last changes fastest.
Arguments:
- boundary: bfloat16 [2, 2, 8192, 768], P('section', None, 'shard'), may hold values from -6 to 6
- ln1_gain: bfloat16 [2, 768], P('section', 'shard'), may hold values from 0.099609375 to 1.8984375
- ln1_bias: bfloat16 [2, 768], P('section', 'shard'), may hold values from -3 to 3
- w_qkv: bfloat16 [2, 768, 2304], P('section', 'shard'), may hold values from -0.21875 to 0.21875
- qv_bias: bfloat16 [2, 1536], P('section', 'shard'), may hold values from -3 to 3
- w_out: bfloat16 [2, 768, 768], P('section', 'shard'), may hold values from -3.5 to 3.5
- out_bias: bfloat16 [2, 768], P('section', 'shard'), may hold values from -3 to 3
- ln2_gain: bfloat16 [2, 768], P('section', 'shard'), may hold values from 0.099609375 to 1.8984375
- ln2_bias: bfloat16 [2, 768], P('section', 'shard'), may hold values from -3 to 3
- w_up: bfloat16 [2, 768, 3072], P('section', 'shard'), may hold values from -0.21875 to 0.21875
- up_bias: bfloat16 [2, 3072], P('section', 'shard'), may hold values from -3 to 3
- w_down: bfloat16 [2, 3072, 768], P('section', 'shard'), may hold values from -0.109375 to 0.109375
- down_bias: bfloat16 [2, 768], P('section', 'shard'), may hold values from -3 to 3
Outputs:
- section_outputs: bfloat16 [2, 2, 8192, 768], P('section', None, 'shard')
- section_grads: bfloat16 [2, 2, 8192, 768], P('section', None, 'shard')
- ln1_gain_grad: float32 [2, 768], P('section', 'shard')
- ln1_bias_grad: float32 [2, 768], P('section', 'shard')
- w_qkv_grad: float32 [2, 768, 2304], P('section', 'shard')
- qv_bias_grad: float32 [2, 1536], P('section', 'shard')
- w_out_grad: float32 [2, 768, 768], P('section', 'shard')
- out_bias_grad: float32 [2, 768], P('section', 'shard')
- ln2_gain_grad: float32 [2, 768], P('section', 'shard')
- ln2_bias_grad: float32 [2, 768], P('section', 'shard')
- w_up_grad: float32 [2, 768, 3072], P('section', 'shard')
- up_bias_grad: float32 [2, 3072], P('section', 'shard')
- w_down_grad: float32 [2, 3072, 768], P('section', 'shard')
- down_bias_grad: float32 [2, 768], P('section', 'shard')
All inputs are finite; a program needn't handle non-finite values.
Results may differ from a plain program's by a relative error of at most 0.015.
Values may be sent and summed in bfloat16 or wider, within the bound.
No kernel may reach another device: no remote copies, remote signals or barrier semaphores. Data moves between devices by JAX's collectives and lax.ppermute only.
A program may use at most 192 MiB of HBM per device.

v0:
```python
import jax
import jax.numpy as jnp
from jax import lax
from jax.sharding import PartitionSpec as P

D = 768
HEADS = 12
HEAD_DIM = 64


def from_behind(value, axis, steps):
    count = lax.axis_size(axis)
    first, last = (max(0, -steps), min(count, count - steps))
    return lax.ppermute(value, axis, [(source, source + steps) for source in range(first, last)])


def norm_affine(values, gain, bias):
    row_mean = jnp.mean(values, axis=-1, keepdims=True)
    centred = values - row_mean
    variance = jnp.mean(centred * centred, axis=-1, keepdims=True)
    return centred * lax.rsqrt(variance + 1e-05) * gain + bias


def key_mask(rows):
    query_pos = jnp.arange(rows)[:, None]
    key_pos = jnp.arange(rows)[None, :]
    return key_pos <= query_pos


def head_groups(matrix):
    return matrix.reshape(matrix.shape[0], HEADS // 2, 2 * HEAD_DIM).transpose(1, 0, 2)


def split_heads(block):
    return block.reshape(block.shape[0], 2, HEAD_DIM)


def ungroup(stacked):
    return stacked.transpose(1, 0, 2).reshape(stacked.shape[1], HEADS * HEAD_DIM)


def masked_scores(head_q, head_k, allowed):
    scores = jnp.einsum(
        "qhd,khd->hqk", head_q, head_k, preferred_element_type=jnp.float32
    ) * HEAD_DIM ** (-0.5)
    return jnp.where(allowed[None], scores, -1e30)


def attend_forward(queries, key_rows, value_rows):
    rows = queries.shape[0]
    allowed = key_mask(rows)

    def one_group(inputs):
        group_q, group_k, group_v = inputs
        scores = masked_scores(split_heads(group_q), split_heads(group_k), allowed)
        row_max = jnp.max(scores, axis=-1, keepdims=True)
        exponent = jnp.exp(scores - row_max)
        row_sum = jnp.sum(exponent, axis=-1, keepdims=True)
        weights = (exponent / row_sum).astype(jnp.bfloat16)
        attended = jnp.einsum(
            "hqk,khd->qhd", weights, split_heads(group_v), preferred_element_type=jnp.float32
        )
        return (attended.reshape(rows, 2 * HEAD_DIM), row_max + jnp.log(row_sum))

    attended, log_sums = lax.map(
        one_group, (head_groups(queries), head_groups(key_rows), head_groups(value_rows))
    )
    return (ungroup(attended), log_sums)


def attend_backward(queries, key_rows, value_rows, grad_attended, log_sums):
    rows = queries.shape[0]
    allowed = key_mask(rows)

    def one_group(inputs):
        group_q, group_k, group_v, group_g, group_lse = inputs
        head_q = split_heads(group_q)
        head_k = split_heads(group_k)
        head_g = split_heads(group_g)
        scores = masked_scores(head_q, head_k, allowed)
        weights = jnp.exp(scores - group_lse)
        grad_prob = jnp.einsum(
            "qhd,khd->hqk", head_g, split_heads(group_v), preferred_element_type=jnp.float32
        )
        centre = jnp.sum(weights * grad_prob, axis=-1, keepdims=True)
        grad_scores = (weights * (grad_prob - centre)).astype(jnp.bfloat16)
        grad_q = jnp.einsum(
            "hqk,khd->qhd", grad_scores, head_k, preferred_element_type=jnp.float32
        ) * HEAD_DIM ** (-0.5)
        grad_k = jnp.einsum(
            "hqk,qhd->khd", grad_scores, head_q, preferred_element_type=jnp.float32
        ) * HEAD_DIM ** (-0.5)
        grad_v = jnp.einsum(
            "hqk,qhd->khd", weights.astype(jnp.bfloat16), head_g, preferred_element_type=jnp.float32
        )
        return (
            grad_q.reshape(rows, 2 * HEAD_DIM),
            grad_k.reshape(rows, 2 * HEAD_DIM),
            grad_v.reshape(rows, 2 * HEAD_DIM),
        )

    grad_q, grad_k, grad_v = lax.map(
        one_group,
        (
            head_groups(queries),
            head_groups(key_rows),
            head_groups(value_rows),
            head_groups(grad_attended),
            log_sums,
        ),
    )
    return (ungroup(grad_q), ungroup(grad_k), ungroup(grad_v))


def forward_layer(hidden, weights):
    (
        ln1_gain,
        ln1_bias,
        w_qkv,
        qv_bias,
        w_out,
        out_bias,
        ln2_gain,
        ln2_bias,
        w_up,
        up_bias,
        w_down,
        down_bias,
    ) = weights
    h_float = hidden.astype(jnp.float32)
    normed = norm_affine(
        h_float, ln1_gain.astype(jnp.float32), ln1_bias.astype(jnp.float32)
    ).astype(jnp.bfloat16)
    joined = jnp.dot(normed, w_qkv, preferred_element_type=jnp.float32)
    bias_float = qv_bias.astype(jnp.float32)
    queries = (joined[:, :D] + bias_float[:D]).astype(jnp.bfloat16)
    key_rows = joined[:, D : 2 * D].astype(jnp.bfloat16)
    value_rows = (joined[:, 2 * D :] + bias_float[D:]).astype(jnp.bfloat16)
    attended, log_sums = attend_forward(queries, key_rows, value_rows)
    attended = attended.astype(jnp.bfloat16)
    residual = (
        h_float
        + jnp.dot(attended, w_out, preferred_element_type=jnp.float32)
        + out_bias.astype(jnp.float32)
    )
    normed_two = norm_affine(
        residual, ln2_gain.astype(jnp.float32), ln2_bias.astype(jnp.float32)
    ).astype(jnp.bfloat16)
    before = jnp.dot(normed_two, w_up, preferred_element_type=jnp.float32) + up_bias.astype(
        jnp.float32
    )
    activated = jax.nn.gelu(before).astype(jnp.bfloat16)
    layer_out = (
        residual
        + jnp.dot(activated, w_down, preferred_element_type=jnp.float32)
        + down_bias.astype(jnp.float32)
    )
    kept = (
        hidden,
        normed,
        queries,
        key_rows,
        value_rows,
        attended,
        log_sums,
        residual,
        normed_two,
        before,
        activated,
    )
    return (layer_out, kept)


def backward_layer(kept, grad_out, weights):
    (
        ln1_gain,
        ln1_bias,
        w_qkv,
        qv_bias,
        w_out,
        out_bias,
        ln2_gain,
        ln2_bias,
        w_up,
        up_bias,
        w_down,
        down_bias,
    ) = weights
    (
        hidden,
        normed,
        queries,
        key_rows,
        value_rows,
        attended,
        log_sums,
        residual,
        normed_two,
        before,
        activated,
    ) = kept
    down_bias_grad = jnp.sum(grad_out, axis=0)
    grad_low = grad_out.astype(jnp.bfloat16)
    w_down_grad = jnp.einsum("tf,td->fd", activated, grad_low, preferred_element_type=jnp.float32)
    grad_act = jnp.einsum("td,fd->tf", grad_low, w_down, preferred_element_type=jnp.float32)
    _, gelu_back = jax.vjp(jax.nn.gelu, before)
    (grad_before,) = gelu_back(grad_act)
    up_bias_grad = jnp.sum(grad_before, axis=0)
    before_low = grad_before.astype(jnp.bfloat16)
    w_up_grad = jnp.einsum("td,tf->df", normed_two, before_low, preferred_element_type=jnp.float32)
    grad_normed_two = jnp.einsum("tf,df->td", before_low, w_up, preferred_element_type=jnp.float32)
    _, norm_back_two = jax.vjp(
        norm_affine, residual, ln2_gain.astype(jnp.float32), ln2_bias.astype(jnp.float32)
    )
    grad_res_norm, ln2_gain_grad, ln2_bias_grad = norm_back_two(grad_normed_two)
    grad_residual = grad_out + grad_res_norm
    out_bias_grad = jnp.sum(grad_residual, axis=0)
    residual_low = grad_residual.astype(jnp.bfloat16)
    w_out_grad = jnp.einsum("td,te->de", attended, residual_low, preferred_element_type=jnp.float32)
    grad_attended = jnp.einsum(
        "te,de->td", residual_low, w_out, preferred_element_type=jnp.float32
    ).astype(jnp.bfloat16)
    grad_q, grad_keys, grad_values = attend_backward(
        queries, key_rows, value_rows, grad_attended, log_sums
    )
    key_low = grad_keys.astype(jnp.bfloat16)
    value_low = grad_values.astype(jnp.bfloat16)
    query_low = grad_q.astype(jnp.bfloat16)
    qv_bias_grad = jnp.concatenate(
        [
            jnp.sum(query_low.astype(jnp.float32), axis=0),
            jnp.sum(value_low.astype(jnp.float32), axis=0),
        ]
    )
    grad_joined = jnp.concatenate([query_low, key_low, value_low], axis=1)
    w_qkv_grad = jnp.einsum("td,te->de", normed, grad_joined, preferred_element_type=jnp.float32)
    grad_normed = jnp.einsum("te,de->td", grad_joined, w_qkv, preferred_element_type=jnp.float32)
    _, norm_back_one = jax.vjp(
        norm_affine,
        hidden.astype(jnp.float32),
        ln1_gain.astype(jnp.float32),
        ln1_bias.astype(jnp.float32),
    )
    grad_h_norm, ln1_gain_grad, ln1_bias_grad = norm_back_one(grad_normed)
    grad_hidden = grad_residual + grad_h_norm
    layer_grads = [
        ln1_gain_grad,
        ln1_bias_grad,
        w_qkv_grad,
        qv_bias_grad,
        w_out_grad,
        out_bias_grad,
        ln2_gain_grad,
        ln2_bias_grad,
        w_up_grad,
        up_bias_grad,
        w_down_grad,
        down_bias_grad,
    ]
    return (grad_hidden, layer_grads)


def on_device(
    boundary,
    ln1_gain,
    ln1_bias,
    w_qkv,
    qv_bias,
    w_out,
    out_bias,
    ln2_gain,
    ln2_bias,
    w_up,
    up_bias,
    w_down,
    down_bias,
):
    is_first = lax.axis_index("section") == 0
    batches = boundary.shape[1]
    gathered = (
        lax.all_gather(ln1_gain, "shard", axis=1, tiled=True),
        lax.all_gather(ln1_bias, "shard", axis=1, tiled=True),
        lax.all_gather(w_qkv, "shard", axis=1, tiled=True),
        lax.all_gather(qv_bias, "shard", axis=1, tiled=True),
        lax.all_gather(w_out, "shard", axis=1, tiled=True),
        lax.all_gather(out_bias, "shard", axis=1, tiled=True),
        lax.all_gather(ln2_gain, "shard", axis=1, tiled=True),
        lax.all_gather(ln2_bias, "shard", axis=1, tiled=True),
        lax.all_gather(w_up, "shard", axis=1, tiled=True),
        lax.all_gather(up_bias, "shard", axis=1, tiled=True),
        lax.all_gather(w_down, "shard", axis=1, tiled=True),
        lax.all_gather(down_bias, "shard", axis=1, tiled=True),
    )
    weights = [item[0] for item in gathered]
    zero_rows = jnp.zeros(boundary.shape[2:], jnp.bfloat16)
    received = zero_rows
    outputs = []
    kept_all = []
    for moment in range(batches + 1):
        hidden = jnp.where(is_first, boundary[0, min(moment, batches - 1)], received)
        layer_out, kept = forward_layer(hidden, weights)
        layer_low = layer_out.astype(jnp.bfloat16)
        outputs.append(layer_low)
        kept_all.append(kept)
        if moment < batches:
            received = from_behind(layer_low, "section", 1)
    section_outputs = jnp.where(is_first, jnp.stack(outputs[:batches]), jnp.stack(outputs[1:]))[
        None
    ]
    gathered = (
        lax.all_gather(ln1_gain, "shard", axis=1, tiled=True),
        lax.all_gather(ln1_bias, "shard", axis=1, tiled=True),
        lax.all_gather(w_qkv, "shard", axis=1, tiled=True),
        lax.all_gather(qv_bias, "shard", axis=1, tiled=True),
        lax.all_gather(w_out, "shard", axis=1, tiled=True),
        lax.all_gather(out_bias, "shard", axis=1, tiled=True),
        lax.all_gather(ln2_gain, "shard", axis=1, tiled=True),
        lax.all_gather(ln2_bias, "shard", axis=1, tiled=True),
        lax.all_gather(w_up, "shard", axis=1, tiled=True),
        lax.all_gather(up_bias, "shard", axis=1, tiled=True),
        lax.all_gather(w_down, "shard", axis=1, tiled=True),
        lax.all_gather(down_bias, "shard", axis=1, tiled=True),
    )
    weights = [item[0] for item in gathered]
    totals = [jnp.zeros(item.shape, jnp.float32) for item in weights]
    received = zero_rows
    input_grads = []
    for moment in range(batches + 1):
        cotangent = jnp.where(is_first, received, boundary[0, min(moment, batches - 1)])
        earlier = kept_all[max(moment - 1, 0)]
        later = kept_all[min(moment + 1, batches)]
        kept = jax.tree.map(
            lambda lower_part, upper_part: jnp.where(is_first, lower_part, upper_part),
            earlier,
            later,
        )
        grad_hidden, layer_grads = backward_layer(kept, cotangent.astype(jnp.float32), weights)
        is_valid = jnp.where(is_first, jnp.float32(moment >= 1), jnp.float32(moment < batches))
        masked = [item * is_valid for item in layer_grads]
        totals = [running + share for running, share in zip(totals, masked)]
        grad_low = grad_hidden.astype(jnp.bfloat16)
        input_grads.append(grad_low)
        if moment < batches:
            received = from_behind(grad_low, "section", -1)
    section_grads = jnp.where(
        is_first, jnp.stack(input_grads[1:]), jnp.stack(input_grads[:batches])
    )[None]
    finals = (
        lax.psum_scatter(totals[0][None], "shard", scatter_dimension=1, tiled=True),
        lax.psum_scatter(totals[1][None], "shard", scatter_dimension=1, tiled=True),
        lax.psum_scatter(totals[2][None], "shard", scatter_dimension=1, tiled=True),
        lax.psum_scatter(totals[3][None], "shard", scatter_dimension=1, tiled=True),
        lax.psum_scatter(totals[4][None], "shard", scatter_dimension=1, tiled=True),
        lax.psum_scatter(totals[5][None], "shard", scatter_dimension=1, tiled=True),
        lax.psum_scatter(totals[6][None], "shard", scatter_dimension=1, tiled=True),
        lax.psum_scatter(totals[7][None], "shard", scatter_dimension=1, tiled=True),
        lax.psum_scatter(totals[8][None], "shard", scatter_dimension=1, tiled=True),
        lax.psum_scatter(totals[9][None], "shard", scatter_dimension=1, tiled=True),
        lax.psum_scatter(totals[10][None], "shard", scatter_dimension=1, tiled=True),
        lax.psum_scatter(totals[11][None], "shard", scatter_dimension=1, tiled=True),
    )
    return (
        section_outputs,
        section_grads,
        finals[0],
        finals[1],
        finals[2],
        finals[3],
        finals[4],
        finals[5],
        finals[6],
        finals[7],
        finals[8],
        finals[9],
        finals[10],
        finals[11],
    )


def solution(mesh):
    placed = (
        P("section", None, "shard", None),
        P("section", "shard"),
        P("section", "shard"),
        P("section", "shard", None),
        P("section", "shard"),
        P("section", "shard", None),
        P("section", "shard"),
        P("section", "shard"),
        P("section", "shard"),
        P("section", "shard", None),
        P("section", "shard"),
        P("section", "shard", None),
        P("section", "shard"),
    )
    return jax.shard_map(
        on_device,
        mesh=mesh,
        in_specs=placed,
        out_specs=(
            P("section", None, "shard", None),
            P("section", None, "shard", None),
            P("section", "shard"),
            P("section", "shard"),
            P("section", "shard", None),
            P("section", "shard"),
            P("section", "shard", None),
            P("section", "shard"),
            P("section", "shard"),
            P("section", "shard"),
            P("section", "shard", None),
            P("section", "shard"),
            P("section", "shard", None),
            P("section", "shard"),
        ),
        check_vma=False,
    )
```

profile of v0, /device:TPU:0, one launch (start us, length us, event | category | flops | bytes accessed | tf_op | source)
XLA Modules:
  0.0 1515.0 jit_solution(10081789766072236981)
XLA Ops:
  16.4 64.1 %all-reduce.8 = (bf16[768]{0:T(1024)(128)(2,1)S(1)}, bf16[768]{0:T(1024)(128)(2,1)S(1)}, bf16[1536]{0:T(1024)(128)(2,1)S(1)}, bf16[768]{0:T(1024)(128)(2,1)S(1)}...) all-reduce(bf16[768]{0:T(1024)(128)(2,1)S(1)} %dynamic-update-slice, ...), channel_id=1, replica_groups=mesh['section'=2,'shard'=16] {'shard'}, use_global_device_ids=true, to_apply=%add.1 | all-reduce | flops 9216 | bytes 36864
  92.2 23.7 %while.84 = (s32[]{:T(128)}, bf16[6,512,128]{1,2,0:T(8,128)(2,1)S(1)}, f32[6,2,512,1]{2,1,3,0:T(2,128)S(1)}, bf16[6,512,128]{1,2,0:T(8,128)(2,1)}, bf16[6,512,12...) while((s32[]{:T(128)}, bf16[6,512,128]{1,2,0:T(8,128)(2,1)S(1)}, ...), condition=%wide.region_5.6_spmd.clone, body=%wide.region_2.5_spmd.clone.sunk | while | flops 140770304 | bytes 8945757 | solution.py:65
  119.6 35.5 %all-gather.9.cloned.1.call-done = bf16[1,768,3072]{2,1,0:T(8,128)(2,1)} async-done(((bf16[1,48,3072]{2,1,0:T(8,128)(2,1)}), bf16[1,768,3072]{2,1,0:T(8,128)(2,1)}) %all-gather.9.cloned.1.call-update) | async-done | bytes 4718608 | tf_op jit(solution)/shard_map/all_gather | solution.py:289
  163.9 45.2 %all-gather.11.cloned.1.call-done = bf16[1,3072,768]{2,1,0:T(8,128)(2,1)} async-done(((bf16[1,192,768]{2,1,0:T(8,128)(2,1)}), bf16[1,3072,768]{2,1,0:T(8,128)(2,1)}) %all-gather.11.cloned.1.call-update) | async-done | bytes 4718608 | tf_op jit(solution)/shard_map/all_gather | solution.py:291
  219.5 17.3 %collective-permute-done = bf16[512,768]{1,0:T(8,128)(2,1)S(1)} collective-permute-done((bf16[512,768]{1,0:T(8,128)(2,1)}, bf16[512,768]{1,0:T(8,128)(2,1)S(1)}, u32[]{:S(2)}, u32[]{:S(2)}) %collective-permute-start) | collective-permute-done | bytes 786464 | tf_op jit(solution)/shard_map/ppermute | solution.py:14
  251.4 23.7 %while.85 = (s32[]{:T(128)}, bf16[6,512,128]{1,2,0:T(8,128)(2,1)S(1)}, f32[6,2,512,1]{2,1,3,0:T(2,128)S(1)}, bf16[6,512,128]{1,2,0:T(8,128)(2,1)}, bf16[6,512,12...) while((s32[]{:T(128)}, bf16[6,512,128]{1,2,0:T(8,128)(2,1)S(1)}, ...), condition=%wide.region_13.14_spmd.clone, body=%wide.region_10.13_spmd.clone.sunk | while | flops 140770304 | bytes 8945757 | solution.py:65
  329.7 27.9 %while.86 = (s32[]{:T(128)}, bf16[6,512,128]{1,2,0:T(8,128)(2,1)}, f32[6,2,512,1]{2,1,3,0:T(2,128)S(1)}, bf16[6,512,128]{1,2,0:T(8,128)(2,1)}, bf16[6,512,128]{1...) while((s32[]{:T(128)}, bf16[6,512,128]{1,2,0:T(8,128)(2,1)}, ...), condition=%wide.region_21.22_spmd.clone, body=%wide.region_18.21_spmd.clone.sunk | while | flops 140770304 | bytes 8946265 | solution.py:65
  379.4 46.5 %while.87 = (s32[]{:T(128)}, bf16[6,512,128]{1,2,0:T(8,128)(2,1)S(1)}, bf16[6,512,128]{1,2,0:T(8,128)(2,1)}, bf16[6,512,128]{1,2,0:T(8,128)(2,1)}, bf16[6,512,12...) while((s32[]{:T(128)}, ...), condition=%wide.region_30.31_spmd.clone, body=%wide.region_28.30_spmd.clone.sunk | while | flops 340786176 | bytes 19419772 | solution.py:102
  464.4 9.3 fusion.277
  485.1 50.5 %while.88 = (s32[]{:T(128)}, bf16[6,512,128]{1,2,0:T(8,128)(2,1)}, bf16[6,512,128]{1,2,0:T(8,128)(2,1)}, bf16[6,512,128]{1,2,0:T(8,128)(2,1)}, bf16[6,512,128]{1...) while((s32[]{:T(128)}, bf16[6,512,128]{1,2,0:T(8,128)(2,1)}, ...), condition=%wide.region_41.42_spmd.clone, body=%wide.region_39.41_spmd.clone.sunk | while | flops 340786176 | bytes 19420280 | solution.py:102
  548.4 17.4 %collective-permute-done.3 = bf16[512,768]{1,0:T(8,128)(2,1)S(1)} collective-permute-done((bf16[512,768]{1,0:T(8,128)(2,1)S(1)}, bf16[512,768]{1,0:T(8,128)(2,1)S(1)}, u32[]{:S(2)}, u32[]{:S(2)}) %collective-permute-start.3) | collective-permute-done | bytes 786464 | tf_op jit(solution)/shard_map/ppermute | solution.py:14
  565.9 10.6 fusion.276
  587.7 50.1 %while.89 = (s32[]{:T(128)}, bf16[6,512,128]{1,2,0:T(8,128)(2,1)}, bf16[6,512,128]{1,2,0:T(8,128)(2,1)}, bf16[6,512,128]{1,2,0:T(8,128)(2,1)}, bf16[6,512,128]{1...) while((s32[]{:T(128)}, bf16[6,512,128]{1,2,0:T(8,128)(2,1)}, ...), condition=%wide.region_52.53_spmd.clone, body=%wide.region_50.52_spmd.clone.sunk | while | flops 340786176 | bytes 19420280 | solution.py:102
  734.3 27.0 %reduce-scatter.47.cloned.1.call-done = f32[48,1]{1,0:T(8,128)} async-done(((f32[768,1]{1,0:T(8,128)}), f32[48,1]{1,0:T(8,128)}) %reduce-scatter.47.cloned.1.call-update) | async-done | bytes 208
  762.6 56.8 %reduce-scatter.45.cloned.1.call-done = f32[48,1]{1,0:T(8,128)} async-done(((f32[768,1]{1,0:T(8,128)}), f32[48,1]{1,0:T(8,128)}) %reduce-scatter.45.cloned.1.call-update) | async-done | bytes 208
  820.7 57.3 %reduce-scatter.43.cloned.1.call-done = f32[48,1]{1,0:T(8,128)} async-done(((f32[768,1]{1,0:T(8,128)}), f32[48,1]{1,0:T(8,128)}) %reduce-scatter.43.cloned.1.call-update) | async-done | bytes 208
  879.3 56.8 %reduce-scatter.39.cloned.1.call-done = f32[48,1]{1,0:T(8,128)} async-done(((f32[768,1]{1,0:T(8,128)}), f32[48,1]{1,0:T(8,128)}) %reduce-scatter.39.cloned.1.call-update) | async-done | bytes 208
  937.5 57.1 %reduce-scatter.37.cloned.1.call-done = f32[48,1]{1,0:T(8,128)} async-done(((f32[768,1]{1,0:T(8,128)}), f32[48,1]{1,0:T(8,128)}) %reduce-scatter.37.cloned.1.call-update) | async-done | bytes 208
  995.9 57.8 %reduce-scatter.41.cloned.1.call-done = f32[96,1]{1,0:T(8,128)} async-done(((f32[1536,1]{1,0:T(8,128)}), f32[96,1]{1,0:T(8,128)}) %reduce-scatter.41.cloned.1.call-update) | async-done | bytes 400
  1055.0 61.1 %reduce-scatter.49.cloned.1.call-done = f32[192,1]{1,0:T(8,128)} async-done(((f32[3072,1]{1,0:T(8,128)}), f32[192,1]{1,0:T(8,128)}) %reduce-scatter.49.cloned.1.call-update) | async-done | bytes 784
  1117.7 64.8 %reduce-scatter.31.cloned.1.call-done = f32[1,48,768]{2,1,0:T(8,128)} async-done(((f32[1,768,768]{2,1,0:T(8,128)}), f32[1,48,768]{2,1,0:T(8,128)}) %reduce-scatter.31.cloned.1.call-update) | async-done | bytes 147472 | tf_op jit(solution)/shard_map/reduce_scatter | solution.py:353
  1182.5 94.1 %reduce-scatter.29.cloned.1.call-done = f32[1,48,2304]{2,1,0:T(8,128)} async-done(((f32[1,768,2304]{2,1,0:T(8,128)}), f32[1,48,2304]{2,1,0:T(8,128)}) %reduce-scatter.29.cloned.1.call-update) | async-done | bytes 442384 | tf_op jit(solution)/shard_map/reduce_scatter | solution.py:351
  1276.5 115.4 %reduce-scatter.35.cloned.1.call-done = f32[1,192,768]{2,1,0:T(8,128)} async-done(((f32[1,3072,768]{2,1,0:T(8,128)}), f32[1,192,768]{2,1,0:T(8,128)}) %reduce-scatter.35.cloned.1.call-update) | async-done | bytes 589840 | tf_op jit(solution)/shard_map/reduce_scatter | solution.py:359
  1391.9 116.3 %reduce-scatter.33.cloned.1.call-done = f32[1,48,3072]{2,1,0:T(8,128)} async-done(((f32[1,768,3072]{2,1,0:T(8,128)}), f32[1,48,3072]{2,1,0:T(8,128)}) %reduce-scatter.33.cloned.1.call-update) | async-done | bytes 589840 | tf_op jit(solution)/shard_map/reduce_scatter | solution.py:357
  (894 shorter events, 530.3 us)
Async XLA Ops:
  7.3 73.4 %all-gather.5.cloned.1.call-start = ((), (), s32[]{:S(2)}) async-start(), calls=%async_computation.12 | async-start | bytes 3760128 | tf_op jit(solution)/shard_map/all_gather | solution.py:283
  8.0 107.9 %all-gather.7.cloned.1.call-start = ((), (), s32[]{:S(2)}) async-start(), calls=%async_computation.13 | async-start | bytes 1253376 | tf_op jit(solution)/shard_map/all_gather | solution.py:285
  8.8 146.2 %all-gather.9.cloned.1.call-start = ((), (), s32[]{:S(2)}) async-start(), calls=%async_computation.14 | async-start | bytes 5013504 | tf_op jit(solution)/shard_map/all_gather | solution.py:289
  9.5 199.6 %all-gather.11.cloned.1.call-start = ((), (), s32[]{:S(2)}) async-start(), calls=%async_computation.15 | async-start | bytes 5013504 | tf_op jit(solution)/shard_map/all_gather | solution.py:291
  10.1 722.9 %reduce-scatter.51.cloned.1.call-start = ((), (), s32[]{:S(2)}) async-start(), calls=%async_computation.27 | async-start | bytes 417792
  80.5 231.4 %copy-start.68 = (f32[768]{0:T(1024)}, f32[768]{0:T(1024)S(1)}, u32[]{:S(2)}) copy-start(f32[768]{0:T(1024)S(1)} %add.779) | copy-start | bytes 9220
  80.6 283.0 %copy-start.66 = (f32[768]{0:T(1024)}, f32[768]{0:T(1024)S(1)}, u32[]{:S(2)}) copy-start(f32[768]{0:T(1024)S(1)} %add.781) | copy-start | bytes 9220
  80.6 204.1 %copy-start.92 = (f32[768]{0:T(1024)}, f32[768]{0:T(1024)S(1)}, u32[]{:S(2)}) copy-start(f32[768]{0:T(1024)S(1)} %add.783) | copy-start | bytes 9220
  215.9 20.9 %collective-permute-start = (bf16[512,768]{1,0:T(8,128)(2,1)}, bf16[512,768]{1,0:T(8,128)(2,1)S(1)}, u32[]{:S(2)}, u32[]{:S(2)}) collective-permute-start(bf16[512,768]{1,0:T(8,128)(2,1)} %add_convert_fusion.7), channel_id=1, source_target_pairs={{0,16},{1,17},{2,18},{3,19},{4,20},{5,21},{6,22},{7,23},{8,24},{9,... | collective-permute-start | bytes 2359304 | tf_op jit(solution)/shard_map/ppermute | solution.py:14
  288.6 21.0 %collective-permute-start.1 = (bf16[512,768]{1,0:T(8,128)(2,1)}, bf16[512,768]{1,0:T(8,128)(2,1)}, u32[]{:S(2)}, u32[]{:S(2)}) collective-permute-start(bf16[512,768]{1,0:T(8,128)(2,1)} %add_convert_fusion.5), channel_id=1, source_target_pairs={{0,16},{1,17},{2,18},{3,19},{4,20},{5,21},{6,22},{7,23},{8,24},{9,... | collective-permute-start | bytes 2359304 | tf_op jit(solution)/shard_map/ppermute | solution.py:14
  311.4 122.0 %copy-start.1 = (bf16[512,768]{1,0:T(8,128)(2,1)}, bf16[512,768]{1,0:T(8,128)(2,1)S(1)}, u32[]{:S(2)}) copy-start(bf16[512,768]{1,0:T(8,128)(2,1)S(1)} %get-tuple-element.539) | copy-start | bytes 2359300
  436.1 26.5 %collective-permute-start.2 = (bf16[512,768]{1,0:T(8,128)(2,1)}, bf16[512,768]{1,0:T(8,128)(2,1)}, u32[]{:S(2)}, u32[]{:S(2)}) collective-permute-start(bf16[512,768]{1,0:T(8,128)(2,1)} %get-tuple-element.603), channel_id=1, source_target_pairs={{16,0},{17,1},{18,2},{19,3},{20,4},{21,5},{22,6},{23,7},{24,8},{25... | collective-permute-start | bytes 2359304 | tf_op jit(solution)/shard_map/ppermute | solution.py:14
  543.0 22.8 %collective-permute-start.3 = (bf16[512,768]{1,0:T(8,128)(2,1)S(1)}, bf16[512,768]{1,0:T(8,128)(2,1)S(1)}, u32[]{:S(2)}, u32[]{:S(2)}) collective-permute-start(bf16[512,768]{1,0:T(8,128)(2,1)S(1)} %get-tuple-element.604), channel_id=1, source_target_pairs={{16,0},{17,1},{18,2},{19,3},{20,4},{21,5},{22,6},{23,7},{24,8},{25... | collective-permute-start | bytes 2359304 | tf_op jit(solution)/shard_map/ppermute | solution.py:14
  649.4 111.8 %reduce-scatter.47.cloned.1.call-start = ((), (), s32[]{:S(2)}) async-start(), calls=%async_computation.25 | async-start | bytes 417792
  650.5 168.9 %reduce-scatter.45.cloned.1.call-start = ((), (), s32[]{:S(2)}) async-start(), calls=%async_computation.24 | async-start | bytes 417792
  651.5 226.5 %reduce-scatter.43.cloned.1.call-start = ((), (), s32[]{:S(2)}) async-start(), calls=%async_computation.23 | async-start | bytes 417792
  652.5 283.7 %reduce-scatter.39.cloned.1.call-start = ((), (), s32[]{:S(2)}) async-start(), calls=%async_computation.21 | async-start | bytes 417792
  653.5 341.0 %reduce-scatter.37.cloned.1.call-start = ((), (), s32[]{:S(2)}) async-start(), calls=%async_computation.20 | async-start | bytes 417792
  654.5 399.1 %reduce-scatter.41.cloned.1.call-start = ((), (), s32[]{:S(2)}) async-start(), calls=%async_computation.22 | async-start | bytes 835584
  655.9 460.3 %reduce-scatter.49.cloned.1.call-start = ((), (), s32[]{:S(2)}) async-start(), calls=%async_computation.26 | async-start | bytes 1671168
  657.6 524.8 %reduce-scatter.31.cloned.1.call-start = ((), (), s32[]{:S(2)}) async-start(), calls=%async_computation.17 | async-start | bytes 2506752 | tf_op jit(solution)/shard_map/reduce_scatter | solution.py:353
  663.1 613.4 %reduce-scatter.29.cloned.1.call-start = ((), (), s32[]{:S(2)}) async-start(), calls=%async_computation.16 | async-start | bytes 7520256 | tf_op jit(solution)/shard_map/reduce_scatter | solution.py:351
  679.5 712.4 %reduce-scatter.35.cloned.1.call-start = ((), (), s32[]{:S(2)}) async-start(), calls=%async_computation.19 | async-start | bytes 10027008 | tf_op jit(solution)/shard_map/reduce_scatter | solution.py:359
  697.5 810.6 %reduce-scatter.33.cloned.1.call-start = ((), (), s32[]{:S(2)}) async-start(), calls=%async_computation.18 | async-start | bytes 10027008 | tf_op jit(solution)/shard_map/reduce_scatter | solution.py:357
  (121 other events, 984.1 us)
Sparse Core Ops, SparseCore 0:
  10.4 50.2 all-gather.4
  63.0 37.3 all-gather.6
  102.6 52.3 all-gather.8
  157.1 51.9 all-gather.10
  649.6 53.2 reduce-scatter.50
  706.6 54.6 reduce-scatter.46
  764.8 54.6 reduce-scatter.44
  823.3 54.6 reduce-scatter.42
  881.5 54.6 reduce-scatter.38
  939.9 54.6 reduce-scatter.36
  998.1 55.4 reduce-scatter.40
  1057.6 58.4 reduce-scatter.48
  1120.5 61.9 reduce-scatter.30
  1187.4 89.0 reduce-scatter.28
  1281.0 110.8 reduce-scatter.34
  1397.0 111.1 reduce-scatter.32
where the time goes:
time: 1520 us; the launch traced here: 1510 us
  waiting for transfers between devices  884 us (58%)
  matrix products  250 us (16%)
  local copies, waits for them, and re-layouts  214 us (14%)
  other arithmetic  69.8 us (5%)
  blocking collectives  64.1 us (4%)
  between operations  18.1 us (1%)
    unnamed x24, waiting for transfers between devices  377 us
    reduce_scatter x1, waiting for transfers between devices, on_device(): lax.psum_scatter(totals[8][None], 'shard', scatter_dimension=1, tiled=True)  116 us
    reduce_scatter x1, waiting for transfers between devices, on_device(): lax.psum_scatter(totals[10][None], 'shard', scatter_dimension=1, tiled=True)  115 us
    dynamic_slice x108, local copies, waits for them, and re-layouts, attend_forward(): lax.map(one_group, (head_groups(queries), head_groups(key_rows), head_gro...  101 us
    reduce_scatter x1, waiting for transfers between devices, on_device(): lax.psum_scatter(totals[2][None], 'shard', scatter_dimension=1, tiled=True)  94.1 us
    reduce_scatter x1, waiting for transfers between devices, on_device(): lax.psum_scatter(totals[4][None], 'shard', scatter_dimension=1, tiled=True)  64.8 us
    unnamed x1, blocking collectives  64.1 us
    all_gather x1, waiting for transfers between devices, on_device(): lax.all_gather(w_down, 'shard', axis=1, tiled=True)  45.2 us
  transfers between devices with their start and end apart: 20, of which 16 were waited for; matrix products, arithmetic and copies ran while one was open for 12% of the time, Pallas kernels for 0%

commit v1 on v0

--- a/solution.py
+++ b/solution.py
@@ -260,6 +260,214 @@
     return (grad_hidden, layer_grads)
 
 
+LOW = jnp.bfloat16
+FLOAT = jnp.float32
+
+
+def hop(value, axis, target):
+    count = lax.axis_size(axis)
+    return lax.ppermute(value, axis, [(source, target(source)) for source in range(count)])
+
+
+def over_section(value):
+    return hop(value, "section", lambda source: 1 - source)
+
+
+def over_core(value):
+    return hop(value, "shard", lambda source: source ^ 1)
+
+
+def over_y(value):
+    return hop(value, "shard", lambda source: source ^ 2)
+
+
+def over_z(value, steps):
+    count = lax.axis_size("shard")
+    return hop(value, "shard", lambda source: (source + 4 * steps) % count)
+
+
+def place(buffer, block, index, dim):
+    starts = [0] * buffer.ndim
+    starts[dim] = index
+    return lax.dynamic_update_slice(buffer, block, starts)
+
+
+def take(value, index, size, dim):
+    return lax.dynamic_slice_in_dim(value, index * size, size, dim)
+
+
+def place_of():
+    shard = lax.axis_index("shard")
+    return (lax.axis_index("section"), shard // 4, (shard // 2) % 2, shard % 2)
+
+
+def spread_z(block):
+    _, z, _, _ = place_of()
+    count = lax.axis_size("shard") // 4
+    buffer = jnp.zeros((count,) + block.shape, block.dtype)
+    buffer = place(buffer, block[None], z, 0)
+    for steps in range(1, count):
+        arrived = over_z(block, steps)
+        buffer = place(buffer, arrived[None], (z - steps) % count, 0)
+    return buffer
+
+
+def pair(own, arrived, index, dim):
+    own, arrived = jnp.expand_dims(own, dim), jnp.expand_dims(arrived, dim)
+    is_low = index == 0
+    return jnp.concatenate(
+        [jnp.where(is_low, own, arrived), jnp.where(is_low, arrived, own)], axis=dim
+    )
+
+
+def spread_y(blocks):
+    _, _, y, _ = place_of()
+    return pair(blocks, over_y(blocks), y, 1)
+
+
+def spread_x(blocks):
+    x, _, _, _ = place_of()
+    dim = blocks.ndim - 1
+    arrived = over_section(blocks)
+    is_low = x == 0
+    return jnp.concatenate(
+        [jnp.where(is_low, blocks, arrived), jnp.where(is_low, arrived, blocks)], axis=dim
+    )
+
+
+def spread_core(blocks):
+    _, _, _, core = place_of()
+    return pair(blocks, over_core(blocks), core, 2)
+
+
+def finish_gather(stacked, x_last):
+    if x_last:
+        stacked = spread_x(spread_y(stacked))
+    else:
+        stacked = spread_y(spread_x(stacked))
+    stacked = spread_core(stacked)
+    return stacked.reshape(-1, stacked.shape[-1])
+
+
+def halves_of_both(shard):
+    x, _, _, _ = place_of()
+    half = shard.shape[1] // 2
+    own = take(shard, x, half, 1)
+    arrived = over_section(take(shard, 1 - x, half, 1))
+    is_low = x == 0
+    return (jnp.where(is_low, own, arrived), jnp.where(is_low, arrived, own))
+
+
+def gather_vectors(packed):
+    x, _, y, core = place_of()
+    stacked = spread_z(packed)
+    stacked = pair(stacked, over_y(stacked), y, 1)
+    stacked = pair(stacked, over_core(stacked), core, 2)
+    stacked = stacked.reshape((-1,) + packed.shape)
+    arrived = over_section(stacked)
+    return (jnp.where(x == 0, stacked, arrived), jnp.where(x == 0, arrived, stacked))
+
+
+def reduce_core(total):
+    _, _, _, core = place_of()
+    sent = lax.dynamic_index_in_dim(total, 1 - core, 2, keepdims=False)
+    kept = lax.dynamic_index_in_dim(total, core, 2, keepdims=False)
+    return (kept.astype(FLOAT) + over_core(sent).astype(FLOAT)).astype(LOW)
+
+
+def reduce_y(total):
+    _, _, y, _ = place_of()
+    sent = lax.dynamic_index_in_dim(total, 1 - y, 1, keepdims=False)
+    kept = lax.dynamic_index_in_dim(total, y, 1, keepdims=False)
+    return (kept.astype(FLOAT) + over_y(sent).astype(FLOAT)).astype(LOW)
+
+
+def reduce_x(total):
+    x, _, _, _ = place_of()
+    dim = total.ndim - 1
+    half = total.shape[dim] // 2
+    sent = take(total, 1 - x, half, dim)
+    kept = take(total, x, half, dim)
+    return (kept.astype(FLOAT) + over_section(sent).astype(FLOAT)).astype(LOW)
+
+
+def reduce_z(total):
+    _, z, _, _ = place_of()
+    count = total.shape[0]
+    result = lax.dynamic_index_in_dim(total, z, 0, keepdims=False).astype(FLOAT)
+    for steps in range(1, count):
+        sent = lax.dynamic_index_in_dim(total, (z + steps) % count, 0, keepdims=False)
+        result = result + over_z(sent, steps).astype(FLOAT)
+    return result
+
+
+def reduce_matrix(total, x_last):
+    count = lax.axis_size("shard")
+    columns = total.shape[1]
+    if x_last is None:
+        return total
+    total = total.reshape(count // 4, 2, 2, total.shape[0] // count, columns)
+    total = reduce_core(total)
+    total = reduce_y(reduce_x(total)) if x_last else reduce_x(reduce_y(total))
+    return reduce_z(total)
+
+
+def join_halves(first_layer, second_layer):
+    x, _, _, _ = place_of()
+    is_low = x == 0
+    kept = jnp.where(is_low, first_layer, second_layer)
+    arrived = over_section(jnp.where(is_low, second_layer, first_layer).astype(LOW)).astype(FLOAT)
+    return jnp.concatenate(
+        [jnp.where(is_low, kept, arrived), jnp.where(is_low, arrived, kept)], axis=1
+    )
+
+
+def scatter_vectors(first_layer, second_layer):
+    x, z, y, core = place_of()
+    count = lax.axis_size("shard")
+    is_low = x == 0
+    kept = jnp.where(is_low, first_layer, second_layer)
+    total = kept + over_section(jnp.where(is_low, second_layer, first_layer))
+    total = total.reshape((count // 4, 2, 2) + total.shape[1:])
+    sent = lax.dynamic_index_in_dim(total, 1 - core, 2, keepdims=False)
+    total = lax.dynamic_index_in_dim(total, core, 2, keepdims=False) + over_core(sent)
+    sent = lax.dynamic_index_in_dim(total, 1 - y, 1, keepdims=False)
+    total = lax.dynamic_index_in_dim(total, y, 1, keepdims=False) + over_y(sent)
+    return reduce_z(total)
+
+
+def both_gathered(shard, x_last, direct):
+    if direct:
+        first, second = halves_of_both(shard)
+        return [finish_gather(spread_z(item), x_last) for item in (first, second)]
+    own = lax.all_gather(shard, "shard", axis=0, tiled=True)
+    arrived = over_section(own)
+    is_low = lax.axis_index("section") == 0
+    return [jnp.where(is_low, own, arrived), jnp.where(is_low, arrived, own)]
+
+
+def both_reduced(first, second, x_last, direct):
+    if direct:
+        return join_halves(reduce_matrix(first, x_last), reduce_matrix(second, x_last))
+    is_low = lax.axis_index("section") == 0
+    kept = jnp.where(is_low, first, second).astype(FLOAT)
+    arrived = over_section(jnp.where(is_low, second, first)).astype(FLOAT)
+    return lax.psum_scatter(kept + arrived, "shard", scatter_dimension=0, tiled=True)
+
+
+def unpack_vectors(stacked):
+    rows = stacked.shape[0]
+    singles = [stacked[:, item].reshape(-1) for item in range(6)]
+    return singles + [stacked[:, 6:8].reshape(-1), stacked[:, 8:12].reshape(-1)]
+
+
+def pack_vectors(singles, pair_vector, quad_vector, count):
+    parts = [item.reshape(count, 1, -1) for item in singles]
+    parts.append(pair_vector.reshape(count, 2, -1))
+    parts.append(quad_vector.reshape(count, 4, -1))
+    return jnp.concatenate(parts, axis=1)
+
+
 def on_device(
     boundary,
     ln1_gain,
@@ -275,105 +483,76 @@
     w_down,
     down_bias,
 ):
-    is_first = lax.axis_index("section") == 0
-    batches = boundary.shape[1]
-    gathered = (
-        lax.all_gather(ln1_gain, "shard", axis=1, tiled=True),
-        lax.all_gather(ln1_bias, "shard", axis=1, tiled=True),
-        lax.all_gather(w_qkv, "shard", axis=1, tiled=True),
-        lax.all_gather(qv_bias, "shard", axis=1, tiled=True),
-        lax.all_gather(w_out, "shard", axis=1, tiled=True),
-        lax.all_gather(out_bias, "shard", axis=1, tiled=True),
-        lax.all_gather(ln2_gain, "shard", axis=1, tiled=True),
-        lax.all_gather(ln2_bias, "shard", axis=1, tiled=True),
-        lax.all_gather(w_up, "shard", axis=1, tiled=True),
-        lax.all_gather(up_bias, "shard", axis=1, tiled=True),
-        lax.all_gather(w_down, "shard", axis=1, tiled=True),
-        lax.all_gather(down_bias, "shard", axis=1, tiled=True),
-    )
-    weights = [item[0] for item in gathered]
-    zero_rows = jnp.zeros(boundary.shape[2:], jnp.bfloat16)
-    received = zero_rows
-    outputs = []
-    kept_all = []
-    for moment in range(batches + 1):
-        hidden = jnp.where(is_first, boundary[0, min(moment, batches - 1)], received)
-        layer_out, kept = forward_layer(hidden, weights)
-        layer_low = layer_out.astype(jnp.bfloat16)
-        outputs.append(layer_low)
-        kept_all.append(kept)
-        if moment < batches:
-            received = from_behind(layer_low, "section", 1)
-    section_outputs = jnp.where(is_first, jnp.stack(outputs[:batches]), jnp.stack(outputs[1:]))[
-        None
+    x = lax.axis_index("section")
+    is_first = x == 0
+    count = lax.axis_size("shard")
+    direct = count <= 16
+    packed = pack_vectors(
+        [ln1_gain, ln1_bias, out_bias, ln2_gain, ln2_bias, down_bias], qv_bias, up_bias, 1
+    )[0]
+    other = over_section(jnp.where(is_first, boundary[0, 1], boundary[0, 0]))
+    hidden = jnp.where(is_first, boundary[0, 0], other)
+    cotangent = jnp.where(is_first, other, boundary[0, 1])
+    vectors = gather_vectors(packed)
+    qk_both = both_gathered(w_qkv[0, :, : 2 * D], True, direct)
+    vo_both = both_gathered(jnp.concatenate([w_qkv[0, :, 2 * D :], w_out[0]], axis=1), False, direct)
+    up_both = both_gathered(w_up[0], True, direct)
+    down_both = both_gathered(w_down[0], False, direct)
+    layers = []
+    for index in range(2):
+        singles = unpack_vectors(vectors[index])
+        g1, b1, ob, g2, b2, db, qvb, ub = singles
+        qkv = jnp.concatenate([qk_both[index], vo_both[index][:, :D]], axis=1)
+        layers.append(
+            (g1, b1, qkv, qvb, vo_both[index][:, D:], ob, g2, b2, up_both[index], ub, down_both[index], db)
+        )
+    first_out, kept_first = forward_layer(hidden, layers[0])
+    first_low = first_out.astype(LOW)
+    second_out, kept_second = forward_layer(first_low, layers[1])
+    second_low = second_out.astype(LOW)
+    grad_mid, grads_second = backward_layer(kept_second, cotangent.astype(FLOAT), layers[1])
+    mid_low = grad_mid.astype(LOW)
+    grad_in, grads_first = backward_layer(kept_first, mid_low.astype(FLOAT), layers[0])
+    in_low = grad_in.astype(LOW)
+    returned = over_section(jnp.stack([jnp.where(is_first, second_low, first_low), jnp.where(is_first, mid_low, in_low)]))
+    own_out = jnp.where(is_first, first_low, second_low)
+    own_grad = jnp.where(is_first, in_low, mid_low)
+    section_outputs = jnp.where(is_first, jnp.stack([own_out, returned[0]]), jnp.stack([returned[0], own_out]))[None]
+    section_grads = jnp.where(is_first, jnp.stack([own_grad, returned[1]]), jnp.stack([returned[1], own_grad]))[None]
+    low_grads = []
+    packed_grads = []
+    for grads in (grads_first, grads_second):
+        g1, b1, qkv, qvb, out, ob, g2, b2, up, ub, down, db = grads
+        low_grads.append(
+            (
+                qkv[:, : 2 * D].astype(LOW),
+                jnp.concatenate([qkv[:, 2 * D :], out], axis=1).astype(LOW),
+                up.astype(LOW),
+                down.astype(LOW),
+            )
+        )
+        packed_grads.append(pack_vectors([g1, b1, ob, g2, b2, db], qvb, ub, count))
+    x_orders = (True, False, True, False)
+    qk, vo, up, down = [
+        both_reduced(low_first, low_second, x_last, direct)
+        for low_first, low_second, x_last in zip(low_grads[0], low_grads[1], x_orders)
     ]
-    gathered = (
-        lax.all_gather(ln1_gain, "shard", axis=1, tiled=True),
-        lax.all_gather(ln1_bias, "shard", axis=1, tiled=True),
-        lax.all_gather(w_qkv, "shard", axis=1, tiled=True),
-        lax.all_gather(qv_bias, "shard", axis=1, tiled=True),
-        lax.all_gather(w_out, "shard", axis=1, tiled=True),
-        lax.all_gather(out_bias, "shard", axis=1, tiled=True),
-        lax.all_gather(ln2_gain, "shard", axis=1, tiled=True),
-        lax.all_gather(ln2_bias, "shard", axis=1, tiled=True),
-        lax.all_gather(w_up, "shard", axis=1, tiled=True),
-        lax.all_gather(up_bias, "shard", axis=1, tiled=True),
-        lax.all_gather(w_down, "shard", axis=1, tiled=True),
-        lax.all_gather(down_bias, "shard", axis=1, tiled=True),
-    )
-    weights = [item[0] for item in gathered]
-    totals = [jnp.zeros(item.shape, jnp.float32) for item in weights]
-    received = zero_rows
-    input_grads = []
-    for moment in range(batches + 1):
-        cotangent = jnp.where(is_first, received, boundary[0, min(moment, batches - 1)])
-        earlier = kept_all[max(moment - 1, 0)]
-        later = kept_all[min(moment + 1, batches)]
-        kept = jax.tree.map(
-            lambda lower_part, upper_part: jnp.where(is_first, lower_part, upper_part),
-            earlier,
-            later,
-        )
-        grad_hidden, layer_grads = backward_layer(kept, cotangent.astype(jnp.float32), weights)
-        is_valid = jnp.where(is_first, jnp.float32(moment >= 1), jnp.float32(moment < batches))
-        masked = [item * is_valid for item in layer_grads]
-        totals = [running + share for running, share in zip(totals, masked)]
-        grad_low = grad_hidden.astype(jnp.bfloat16)
-        input_grads.append(grad_low)
-        if moment < batches:
-            received = from_behind(grad_low, "section", -1)
-    section_grads = jnp.where(
-        is_first, jnp.stack(input_grads[1:]), jnp.stack(input_grads[:batches])
-    )[None]
-    finals = (
-        lax.psum_scatter(totals[0][None], "shard", scatter_dimension=1, tiled=True),
-        lax.psum_scatter(totals[1][None], "shard", scatter_dimension=1, tiled=True),
-        lax.psum_scatter(totals[2][None], "shard", scatter_dimension=1, tiled=True),
-        lax.psum_scatter(totals[3][None], "shard", scatter_dimension=1, tiled=True),
-        lax.psum_scatter(totals[4][None], "shard", scatter_dimension=1, tiled=True),
-        lax.psum_scatter(totals[5][None], "shard", scatter_dimension=1, tiled=True),
-        lax.psum_scatter(totals[6][None], "shard", scatter_dimension=1, tiled=True),
-        lax.psum_scatter(totals[7][None], "shard", scatter_dimension=1, tiled=True),
-        lax.psum_scatter(totals[8][None], "shard", scatter_dimension=1, tiled=True),
-        lax.psum_scatter(totals[9][None], "shard", scatter_dimension=1, tiled=True),
-        lax.psum_scatter(totals[10][None], "shard", scatter_dimension=1, tiled=True),
-        lax.psum_scatter(totals[11][None], "shard", scatter_dimension=1, tiled=True),
-    )
+    vector = scatter_vectors(packed_grads[0], packed_grads[1])
     return (
         section_outputs,
         section_grads,
-        finals[0],
-        finals[1],
-        finals[2],
-        finals[3],
-        finals[4],
-        finals[5],
-        finals[6],
-        finals[7],
-        finals[8],
-        finals[9],
-        finals[10],
-        finals[11],
+        vector[0:1],
+        vector[1:2],
+        jnp.concatenate([qk, vo[:, :D]], axis=1)[None],
+        vector[6:8].reshape(1, -1),
+        vo[:, D:][None],
+        vector[2:3],
+        vector[3:4],
+        vector[4:5],
+        up[None],
+        vector[8:12].reshape(1, -1),
+        down[None],
+        vector[5:6],
     )
 
 

time: 1520 us -> 872 us (0.57)
  waiting for transfers between devices: 884 us -> 308 us
  starting transfers between devices: 12.6 us -> 140 us
  matrix products: 250 us -> 134 us
  blocking collectives: 64.1 us -> 0 us
  local copies, waits for them, and re-layouts: 214 us -> 187 us
  other arithmetic: 69.8 us -> 88.7 us
    reduce_scatter x4 -> x0, waiting for transfers between devices: 391 us -> none  [the longest x1 116 us: on_device(): lax.psum_scatter(totals[8][None], 'shard', scatter_dimension=1, tiled=True)]
    unnamed x24 -> x0, waiting for transfers between devices: 377 us -> none
    ppermute x4 -> x118, waiting for transfers between devices: 35.8 us -> 308 us  [hop(): lax.ppermute(value, axis, [(source, target(source)) for source in range(c...]
    ppermute x4 -> x118, starting transfers between devices: 11.4 us -> 140 us  [hop(): lax.ppermute(value, axis, [(source, target(source)) for source in range(c...]
    all_gather x4 -> x0, waiting for transfers between devices: 80.7 us -> none  [the longest x1 45.2 us: on_device(): lax.all_gather(w_down, 'shard', axis=1, tiled=True)]
    unnamed x1 -> x0, blocking collectives: 64.1 us -> none
    dynamic_slice x108 -> x72, local copies, waits for them, and re-layouts: 101 us -> 61.6 us  [attend_forward(): lax.map(one_group, (head_groups(queries), head_groups(key_rows), head_gro...]
    dynamic_slice x0 -> x25, local copies, waits for them, and re-layouts: none -> 25.3 us  [the longest x3 14.4 us: reduce_core(): kept = lax.dynamic_index_in_dim(total, core, 2, keepdims=False)]
  transfers between devices with their start and end apart: 20 -> 118, of which waited for: 16 -> 50; matrix products, arithmetic and copies ran while one was open for 12% -> 23% of each run, Pallas kernels for 0% -> 0%
where the time goes in v1:
time: 872 us; the launch traced here: 864 us
  waiting for transfers between devices  308 us (35%)
  local copies, waits for them, and re-layouts  187 us (21%)
  starting transfers between devices  140 us (16%)
  matrix products  134 us (15%)
  other arithmetic  88.7 us (10%)
    ppermute x118, waiting for transfers between devices, hop(): lax.ppermute(value, axis, [(source, target(source)) for source in range(c...  308 us
    ppermute x118, starting transfers between devices, hop(): lax.ppermute(value, axis, [(source, target(source)) for source in range(c...  140 us
    dynamic_slice x72, local copies, waits for them, and re-layouts, attend_forward(): lax.map(one_group, (head_groups(queries), head_groups(key_rows), head_gro...  61.6 us
    unnamed x292, local copies, waits for them, and re-layouts  22.7 us
    dynamic_update_slice x36, local copies, waits for them, and re-layouts, attend_forward(): lax.map(one_group, (head_groups(queries), head_groups(key_rows), head_gro...  20.5 us
    dot_general x24, matrix products, masked_scores(): jnp.einsum('qhd,khd->hqk', head_q, head_k, preferred_element_type=jnp.flo...  18.4 us
  transfers between devices with their start and end apart: 118, of which 50 were waited for; matrix products, arithmetic and copies ran while one was open for 23% of the time, Pallas kernels for 0%

profile of v1, /device:TPU:0, one launch (start us, length us, event | category | flops | bytes accessed | tf_op | source)
XLA Modules:
  0.0 863.8 jit_solution(10607693507281418956)
XLA Ops:
  22.1 16.4 %collective-permute-done.6 = bf16[16,12,48]{2,0,1:T(8,128)(2,1)S(1)} collective-permute-done((bf16[16,12,48]{2,0,1:T(8,128)(2,1)S(1)}, bf16[16,12,48]{2,0,1:T(8,128)(2,1)S(1)}, u32[]{:S(2)}, u32[]{:S(2)}) %collective-permute-start.6) | collective-permute-done | bytes 18464 | tf_op jit(solution)/shard_map/ppermute | solution.py:269
  113.1 7.2 collective-permute-done.47
  128.0 8.9 %collective-permute-done.49 = bf16[48,1536]{1,0:T(8,128)(2,1)S(1)} collective-permute-done((bf16[48,1536]{1,0:T(8,128)(2,1)S(1)}, bf16[48,1536]{1,0:T(8,128)(2,1)S(1)}, u32[]{:S(2)}, u32[]{:S(2)}) %collective-permute-start.49) | collective-permute-done | bytes 147488 | tf_op jit(solution)/shard_map/ppermute | solution.py:269
  174.5 11.0 %collective-permute-done.50 = bf16[4,48,1536]{2,1,0:T(8,128)(2,1)S(1)} collective-permute-done((bf16[4,48,1536]{2,1,0:T(8,128)(2,1)S(1)}, bf16[4,48,1536]{2,1,0:T(8,128)(2,1)S(1)}, u32[]{:S(2)}, u32[]{:S(2)}) %collective-permute-start.50) | collective-permute-done | bytes 589856 | tf_op jit(solution)/shard_map/ppermute | solution.py:269
  188.3 9.9 %collective-permute-done.19 = bf16[4,48,1536]{2,1,0:T(8,128)(2,1)S(1)} collective-permute-done((bf16[4,48,1536]{2,1,0:T(8,128)(2,1)S(1)}, bf16[4,48,1536]{2,1,0:T(8,128)(2,1)S(1)}, u32[]{:S(2)}, u32[]{:S(2)}) %collective-permute-start.19) | collective-permute-done | bytes 589856 | tf_op jit(solution)/shard_map/ppermute | solution.py:269
  198.9 11.9 %collective-permute-done.45 = bf16[4,48,1536]{2,1,0:T(8,128)(2,1)S(1)} collective-permute-done((bf16[4,48,1536]{2,1,0:T(8,128)(2,1)S(1)}, bf16[4,48,1536]{2,1,0:T(8,128)(2,1)S(1)}, u32[]{:S(2)}, u32[]{:S(2)}) %collective-permute-start.45) | collective-permute-done | bytes 589856 | tf_op jit(solution)/shard_map/ppermute | solution.py:269
  216.2 17.4 %collective-permute-done.26 = bf16[4,2,48,1536]{3,2,0,1:T(8,128)(2,1)S(1)} collective-permute-done((bf16[4,2,48,1536]{3,2,0,1:T(8,128)(2,1)S(1)}, bf16[4,2,48,1536]{3,2,0,1:T(8,128)(2,1)S(1)}, u32[]{:S(2)}, u32[]{:S(2)}) %collective-permute-start.26) | collective-permute-done | bytes 1179680 | tf_op jit(solution)/shard_map/ppermute | solution.py:269
  236.6 14.4 %collective-permute-done.57 = bf16[4,192,768]{2,1,0:T(8,128)(2,1)S(1)} collective-permute-done((bf16[4,192,768]{2,1,0:T(8,128)(2,1)S(1)}, bf16[4,192,768]{2,1,0:T(8,128)(2,1)S(1)}, u32[]{:S(2)}, u32[]{:S(2)}) %collective-permute-start.57) | collective-permute-done | bytes 1179680 | tf_op jit(solution)/shard_map/ppermute | solution.py:269
  274.3 27.7 %while.56 = (s32[]{:T(128)}, bf16[6,512,128]{1,2,0:T(8,128)(2,1)}, f32[6,2,512,1]{2,1,3,0:T(2,128)S(1)}, bf16[6,512,128]{1,2,0:T(8,128)(2,1)}, bf16[6,512,128]{1...) while((s32[]{:T(128)}, bf16[6,512,128]{1,2,0:T(8,128)(2,1)}, ...), condition=%wide.region_5.6_spmd.clone, body=%wide.region_2.5_spmd.clone.sunk | while | flops 140770304 | bytes 8945765 | solution.py:65
  342.1 31.0 %while.57 = (s32[]{:T(128)}, bf16[6,512,128]{1,2,0:T(8,128)(2,1)}, f32[6,2,512,1]{2,1,3,0:T(2,128)}, bf16[6,512,128]{1,2,0:T(8,128)(2,1)}, bf16[6,512,128]{1,2,0...) while((s32[]{:T(128)}, bf16[6,512,128]{1,2,0:T(8,128)(2,1)}, ...), condition=%wide.region_13.14_spmd.clone, body=%wide.region_10.13_spmd.clone.sunk | while | flops 140770304 | bytes 8945765 | solution.py:65
  386.2 7.2 fusion.164
  400.5 44.5 %while.58 = (s32[]{:T(128)}, bf16[6,512,128]{1,2,0:T(8,128)(2,1)S(1)}, bf16[6,512,128]{1,2,0:T(8,128)(2,1)}, bf16[6,512,128]{1,2,0:T(8,128)(2,1)S(1)}, bf16[6,51...) while((s32[]{:T(128)}, ...), condition=%wide.region_20.21_spmd.clone, body=%wide.region_18.20_spmd.clone.sunk | while | flops 340786176 | bytes 19419272 | solution.py:102
  453.2 9.7 %fusion.162 = (f32[3072]{0:T(1024)S(1)}, bf16[512,3072]{1,0:T(8,128)(2,1)S(1)}) fusion(f32[512,3072]{1,0:T(8,128)} %copy-done.122, f32[3072]{0:T(1024)S(1)} %copy-done.105, bf16[512,768]{1,0:T(8,128)(2,1)S(1)} %get-tuple-element.436, bf16[3072,768]{1,0:T(8,128)(2,1)} %bitcast.758), kind=kOutput, calls=%fused_computation.577 | convolution fusion | flops 2450519040 | bytes 14966784 | tf_op jit(solution)/shard_map/td,fd->tf/dot_general | solution.py:205
  472.9 54.4 %while.59 = (s32[]{:T(128)}, bf16[6,512,128]{1,2,0:T(8,128)(2,1)}, bf16[6,512,128]{1,2,0:T(8,128)(2,1)}, bf16[6,512,128]{1,2,0:T(8,128)(2,1)}, bf16[6,512,128]{1...) while((s32[]{:T(128)}, bf16[6,512,128]{1,2,0:T(8,128)(2,1)}, ...), condition=%wide.region_27.28_spmd.clone, body=%wide.region_25.27_spmd.clone.sunk | while | flops 340786176 | bytes 19419272 | solution.py:102
  554.6 5.9 convolution_convert_fusion
  587.6 26.7 %collective-permute-done.60 = f32[16,12,48]{2,0,1:T(8,128)S(1)} collective-permute-done((f32[16,12,48]{2,0,1:T(8,128)S(1)}, f32[16,12,48]{2,0,1:T(8,128)S(1)}, u32[]{:S(2)}, u32[]{:S(2)}) %collective-permute-start.60) | collective-permute-done | bytes 36896 | tf_op jit(solution)/shard_map/ppermute | solution.py:269
  628.2 6.8 constant_dynamic-slice_fusion.16
  667.3 10.7 %collective-permute-done.86 = bf16[4,48,1536]{2,1,0:T(8,128)(2,1)S(1)} collective-permute-done((bf16[4,48,1536]{2,1,0:T(8,128)(2,1)S(1)}, bf16[4,48,1536]{2,1,0:T(8,128)(2,1)S(1)}, u32[]{:S(2)}, u32[]{:S(2)}) %collective-permute-start.86) | collective-permute-done | bytes 589856 | tf_op jit(solution)/shard_map/ppermute | solution.py:269
  742.8 20.7 %collective-permute-done.93 = bf16[4,2,48,1536]{3,2,0,1:T(8,128)(2,1)S(1)} collective-permute-done((bf16[4,2,48,1536]{3,2,0,1:T(8,128)(2,1)S(1)}, bf16[4,2,48,1536]{3,2,0,1:T(8,128)(2,1)S(1)}, u32[]{:S(2)}, u32[]{:S(2)}) %collective-permute-start.93) | collective-permute-done | bytes 1179680 | tf_op jit(solution)/shard_map/ppermute | solution.py:269
  765.1 19.5 %collective-permute-done.99 = bf16[4,2,48,1536]{3,2,0,1:T(8,128)(2,1)S(1)} collective-permute-done((bf16[4,2,48,1536]{3,2,0,1:T(8,128)(2,1)S(1)}, bf16[4,2,48,1536]{3,2,0,1:T(8,128)(2,1)S(1)}, u32[]{:S(2)}, u32[]{:S(2)}) %collective-permute-start.99) | collective-permute-done | bytes 1179680 | tf_op jit(solution)/shard_map/ppermute | solution.py:269
  794.7 11.6 %collective-permute-done.94 = bf16[4,48,1536]{2,1,0:T(8,128)(2,1)S(1)} collective-permute-done((bf16[4,48,1536]{2,1,0:T(8,128)(2,1)S(1)}, bf16[4,48,1536]{2,1,0:T(8,128)(2,1)S(1)}, u32[]{:S(2)}, u32[]{:S(2)}) %collective-permute-start.94) | collective-permute-done | bytes 589856 | tf_op jit(solution)/shard_map/ppermute | solution.py:269
  808.2 6.6 collective-permute-done.100
  823.9 6.8 collective-permute-start.109
  833.7 9.1 %collective-permute-done.102 = bf16[48,1536]{1,0:T(8,128)(2,1)S(1)} collective-permute-done((bf16[48,1536]{1,0:T(8,128)(2,1)S(1)}, bf16[48,1536]{1,0:T(8,128)(2,1)S(1)}, u32[]{:S(2)}, u32[]{:S(2)}) %collective-permute-start.102) | collective-permute-done | bytes 147488 | tf_op jit(solution)/shard_map/ppermute | solution.py:269
  (1131 shorter events, 619.5 us)
Async XLA Ops:
  12.7 150.0 %collective-permute-start = (bf16[512,768]{1,0:T(8,128)(2,1)S(1)}, bf16[512,768]{1,0:T(8,128)(2,1)S(1)}, u32[]{:S(2)}, u32[]{:S(2)}) collective-permute-start(bf16[512,768]{1,0:T(8,128)(2,1)S(1)} %bitcast_select_fusion.1), channel_id=1, source_target_pairs={{0,16},{16,0},{1,17},{17,1},{2,18},{18,2},{3,19},{19,3},{4,20},{20... | collective-permute-start | bytes 2359304 | tf_op jit(solution)/shard_map/ppermute | solution.py:269
  14.3 42.3 %collective-permute-start.14 = (bf16[48,768]{1,0:T(8,128)(2,1)S(1)}, bf16[48,768]{1,0:T(8,128)(2,1)S(1)}, u32[]{:S(2)}, u32[]{:S(2)}) collective-permute-start(bf16[48,768]{1,0:T(8,128)(2,1)S(1)} %fusion.126), channel_id=1, source_target_pairs={{0,16},{16,0},{1,17},{17,1},{2,18},{18,2},{3,19},{19,3},{4,20},{20... | collective-permute-start | bytes 221192 | tf_op jit(solution)/shard_map/ppermute | solution.py:269
  16.9 40.7 %collective-permute-start.7 = (bf16[48,768]{1,0:T(8,128)(2,1)S(1)}, bf16[48,768]{1,0:T(8,128)(2,1)S(1)}, u32[]{:S(2)}, u32[]{:S(2)}) collective-permute-start(bf16[48,768]{1,0:T(8,128)(2,1)S(1)} %dynamic-slice_bitcast_fusion.36), channel_id=1, source_target_pairs={{0,16},{16,0},{1,17},{17,1},{2,18},{18,2},{3,19},{19,3},{4,20},{20... | collective-permute-start | bytes 221192 | tf_op jit(solution)/shard_map/ppermute | solution.py:269
  19.2 41.9 %collective-permute-start.28 = (bf16[192,384]{1,0:T(8,128)(2,1)S(1)}, bf16[192,384]{1,0:T(8,128)(2,1)S(1)}, u32[]{:S(2)}, u32[]{:S(2)}) collective-permute-start(bf16[192,384]{1,0:T(8,128)(2,1)S(1)} %dynamic-slice_bitcast_fusion.22), channel_id=1, source_target_pairs={{0,16},{16,0},{1,17},{17,1},{2,18},{18,2},{3,19},{19,3},{4,20},{20... | collective-permute-start | bytes 442376 | tf_op jit(solution)/shard_map/ppermute | solution.py:269
  84.2 54.1 %collective-permute-start.29 = (bf16[192,384]{1,0:T(8,128)(2,1)S(1)}, bf16[192,384]{1,0:T(8,128)(2,1)S(1)}, u32[]{:S(2)}, u32[]{:S(2)}) collective-permute-start(bf16[192,384]{1,0:T(8,128)(2,1)S(1)} %get-tuple-element.387), channel_id=1, source_target_pairs={{0,4},{1,5},{2,6},{3,7},{4,8},{5,9},{6,10},{7,11},{8,12},{9,13},{1... | collective-permute-start | bytes 442376 | tf_op jit(solution)/shard_map/ppermute | solution.py:269
  86.4 52.1 %collective-permute-start.30 = (bf16[192,384]{1,0:T(8,128)(2,1)S(1)}, bf16[192,384]{1,0:T(8,128)(2,1)S(1)}, u32[]{:S(2)}, u32[]{:S(2)}) collective-permute-start(bf16[192,384]{1,0:T(8,128)(2,1)S(1)} %get-tuple-element.387), channel_id=1, source_target_pairs={{0,8},{1,9},{2,10},{3,11},{4,12},{5,13},{6,14},{7,15},{8,0},{9,1},... | collective-permute-start | bytes 442376 | tf_op jit(solution)/shard_map/ppermute | solution.py:269
  89.1 52.4 %collective-permute-start.31 = (bf16[192,384]{1,0:T(8,128)(2,1)S(1)}, bf16[192,384]{1,0:T(8,128)(2,1)S(1)}, u32[]{:S(2)}, u32[]{:S(2)}) collective-permute-start(bf16[192,384]{1,0:T(8,128)(2,1)S(1)} %get-tuple-element.387), channel_id=1, source_target_pairs={{0,12},{1,13},{2,14},{3,15},{4,0},{5,1},{6,2},{7,3},{8,4},{9,5},{1... | collective-permute-start | bytes 442376 | tf_op jit(solution)/shard_map/ppermute | solution.py:269
  170.5 41.1 %collective-permute-start.12 = (bf16[4,2,48,768]{3,2,0,1:T(8,128)(2,1)S(1)}, bf16[4,2,48,768]{3,2,0,1:T(8,128)(2,1)S(1)}, u32[]{:S(2)}, u32[]{:S(2)}) collective-permute-start(bf16[4,2,48,768]{3,2,0,1:T(8,128)(2,1)S(1)} %pad_maximum_fusion.33), channel_id=1, source_target_pairs={{0,16},{16,0},{1,17},{17,1},{2,18},{18,2},{3,19},{19,3},{4,20},{20... | collective-permute-start | bytes 1769480 | tf_op jit(solution)/shard_map/ppermute | solution.py:269
  186.5 49.6 %collective-permute-start.33 = (bf16[4,192,768]{2,1,0:T(8,128)(2,1)S(1)}, bf16[4,192,768]{2,1,0:T(8,128)(2,1)S(1)}, u32[]{:S(2)}, u32[]{:S(2)}) collective-permute-start(bf16[4,192,768]{2,1,0:T(8,128)(2,1)S(1)} %pad_maximum_fusion.24), channel_id=1, source_target_pairs={{0,2},{1,3},{2,0},{3,1},{4,6},{5,7},{6,4},{7,5},{8,10},{9,11},{10,... | collective-permute-start | bytes 3538952 | tf_op jit(solution)/shard_map/ppermute | solution.py:269
  210.8 45.6 %collective-permute-start.51 = (bf16[4,2,48,1536]{3,2,0,1:T(8,128)(2,1)S(1)}, bf16[4,2,48,1536]{3,2,0,1:T(8,128)(2,1)S(1)}, u32[]{:S(2)}, u32[]{:S(2)}) collective-permute-start(bf16[4,2,48,1536]{3,2,0,1:T(8,128)(2,1)S(1)} %pad_maximum_fusion.27), channel_id=1, source_target_pairs={{0,16},{16,0},{1,17},{17,1},{2,18},{18,2},{3,19},{19,3},{4,20},{20... | collective-permute-start | bytes 3538952 | tf_op jit(solution)/shard_map/ppermute | solution.py:269
  213.4 45.8 %collective-permute-start.20 = (bf16[4,2,48,1536]{3,2,0,1:T(8,128)(2,1)S(1)}, bf16[4,2,48,1536]{3,2,0,1:T(8,128)(2,1)S(1)}, u32[]{:S(2)}, u32[]{:S(2)}) collective-permute-start(bf16[4,2,48,1536]{3,2,0,1:T(8,128)(2,1)S(1)} %pad_maximum_fusion.22), channel_id=1, source_target_pairs={{0,1},{1,0},{2,3},{3,2},{4,5},{5,4},{6,7},{7,6},{8,9},{9,8},{10,11... | collective-permute-start | bytes 3538952 | tf_op jit(solution)/shard_map/ppermute | solution.py:269
  236.1 65.9 %collective-permute-start.46 = (bf16[4,2,48,1536]{3,2,1,0:T(8,128)(2,1)}, bf16[4,2,48,1536]{3,2,1,0:T(8,128)(2,1)}, u32[]{:S(2)}, u32[]{:S(2)}) collective-permute-start(bf16[4,2,48,1536]{3,2,1,0:T(8,128)(2,1)} %pad_maximum_fusion.26), channel_id=1, source_target_pairs={{0,1},{1,0},{2,3},{3,2},{4,5},{5,4},{6,7},{7,6},{8,9},{9,8},{10,11... | collective-permute-start | bytes 3538952 | tf_op jit(solution)/shard_map/ppermute | solution.py:269
  251.0 53.6 %collective-permute-start.40 = (bf16[4,2,48,1536]{3,2,0,1:T(8,128)(2,1)}, bf16[4,2,48,1536]{3,2,0,1:T(8,128)(2,1)}, u32[]{:S(2)}, u32[]{:S(2)}) collective-permute-start(bf16[4,2,48,1536]{3,2,0,1:T(8,128)(2,1)} %pad_maximum_fusion.25), channel_id=1, source_target_pairs={{0,1},{1,0},{2,3},{3,2},{4,5},{5,4},{6,7},{7,6},{8,9},{9,8},{10,11... | collective-permute-start | bytes 3538952 | tf_op jit(solution)/shard_map/ppermute | solution.py:269
  256.4 61.9 %collective-permute-start.34 = (bf16[4,2,192,768]{3,2,1,0:T(8,128)(2,1)}, bf16[4,2,192,768]{3,2,1,0:T(8,128)(2,1)}, u32[]{:S(2)}, u32[]{:S(2)}) collective-permute-start(bf16[4,2,192,768]{3,2,1,0:T(8,128)(2,1)} %pad_maximum_fusion.9), channel_id=1, source_target_pairs={{0,1},{1,0},{2,3},{3,2},{4,5},{5,4},{6,7},{7,6},{8,9},{9,8},{10,11... | collective-permute-start | bytes 7077896 | tf_op jit(solution)/shard_map/ppermute | solution.py:269
  259.2 53.9 %collective-permute-start.27 = (bf16[4,2,48,3072]{3,2,0,1:T(8,128)(2,1)}, bf16[4,2,48,3072]{3,2,0,1:T(8,128)(2,1)}, u32[]{:S(2)}, u32[]{:S(2)}) collective-permute-start(bf16[4,2,48,3072]{3,2,0,1:T(8,128)(2,1)} %pad_maximum_fusion.8), channel_id=1, source_target_pairs={{0,1},{1,0},{2,3},{3,2},{4,5},{5,4},{6,7},{7,6},{8,9},{9,8},{10,11... | collective-permute-start | bytes 7077896 | tf_op jit(solution)/shard_map/ppermute | solution.py:269
  259.9 113.2 %collective-permute-start.52 = (bf16[4,2,48,3072]{3,2,0,1:T(8,128)(2,1)}, bf16[4,2,48,3072]{3,2,0,1:T(8,128)(2,1)}, u32[]{:S(2)}, u32[]{:S(2)}) collective-permute-start(bf16[4,2,48,3072]{3,2,0,1:T(8,128)(2,1)} %pad_maximum_fusion.12), channel_id=1, source_target_pairs={{0,1},{1,0},{2,3},{3,2},{4,5},{5,4},{6,7},{7,6},{8,9},{9,8},{10,11... | collective-permute-start | bytes 7077896 | tf_op jit(solution)/shard_map/ppermute | solution.py:269
  302.0 78.1 %collective-permute-start.58 = (bf16[4,2,192,768]{3,2,1,0:T(8,128)(2,1)}, bf16[4,2,192,768]{3,2,1,0:T(8,128)(2,1)}, u32[]{:S(2)}, u32[]{:S(2)}) collective-permute-start(bf16[4,2,192,768]{3,2,1,0:T(8,128)(2,1)} %pad_maximum_fusion.13), channel_id=1, source_target_pairs={{0,1},{1,0},{2,3},{3,2},{4,5},{5,4},{6,7},{7,6},{8,9},{9,8},{10,11... | collective-permute-start | bytes 7077896 | tf_op jit(solution)/shard_map/ppermute | solution.py:269
  575.7 82.3 %collective-permute-start.59 = (bf16[2,512,768]{2,1,0:T(8,128)(2,1)}, bf16[2,512,768]{2,1,0:T(8,128)(2,1)}, u32[]{:S(2)}, u32[]{:S(2)}) collective-permute-start(bf16[2,512,768]{2,1,0:T(8,128)(2,1)} %pad_maximum_fusion.20), channel_id=1, source_target_pairs={{0,16},{16,0},{1,17},{17,1},{2,18},{18,2},{3,19},{19,3},{4,20},{20... | collective-permute-start | bytes 4718600 | tf_op jit(solution)/shard_map/ppermute | solution.py:269
  587.6 60.0 %collective-permute-start.79 = (bf16[4,2,48,1536]{3,2,1,0:T(8,128)(2,1)}, bf16[4,2,48,1536]{3,2,1,0:T(8,128)(2,1)}, u32[]{:S(2)}, u32[]{:S(2)}) collective-permute-start(bf16[4,2,48,1536]{3,2,1,0:T(8,128)(2,1)} %fusion.87), channel_id=1, source_target_pairs={{0,1},{1,0},{2,3},{3,2},{4,5},{5,4},{6,7},{7,6},{8,9},{9,8},{10,11... | collective-permute-start | bytes 3538952 | tf_op jit(solution)/shard_map/ppermute | solution.py:269
  647.6 85.9 %collective-permute-start.92 = (bf16[4,2,48,3072]{3,2,0,1:T(8,128)(2,1)}, bf16[4,2,48,3072]{3,2,0,1:T(8,128)(2,1)S(1)}, u32[]{:S(2)}, u32[]{:S(2)}) collective-permute-start(bf16[4,2,48,3072]{3,2,0,1:T(8,128)(2,1)} %bitcast.790), channel_id=1, source_target_pairs={{0,1},{1,0},{2,3},{3,2},{4,5},{5,4},{6,7},{7,6},{8,9},{9,8},{10,11... | collective-permute-start | bytes 7077896 | tf_op jit(solution)/shard_map/ppermute | solution.py:269
  737.2 47.5 %collective-permute-start.99 = (bf16[4,2,48,1536]{3,2,0,1:T(8,128)(2,1)S(1)}, bf16[4,2,48,1536]{3,2,0,1:T(8,128)(2,1)S(1)}, u32[]{:S(2)}, u32[]{:S(2)}) collective-permute-start(bf16[4,2,48,1536]{3,2,0,1:T(8,128)(2,1)S(1)} %constant_dynamic-slice_fusion.20), channel_id=1, source_target_pairs={{0,16},{16,0},{1,17},{17,1},{2,18},{18,2},{3,19},{19,3},{4,20},{20... | collective-permute-start | bytes 3538952 | tf_op jit(solution)/shard_map/ppermute | solution.py:269
  739.4 47.3 %collective-permute-start.106 = (bf16[4,192,768]{2,1,0:T(8,128)(2,1)S(1)}, bf16[4,192,768]{2,1,0:T(8,128)(2,1)S(1)}, u32[]{:S(2)}, u32[]{:S(2)}) collective-permute-start(bf16[4,192,768]{2,1,0:T(8,128)(2,1)S(1)} %dynamic-slice_bitcast_fusion.3), channel_id=1, source_target_pairs={{0,2},{1,3},{2,0},{3,1},{4,6},{5,7},{6,4},{7,5},{8,10},{9,11},{10,... | collective-permute-start | bytes 3538952 | tf_op jit(solution)/shard_map/ppermute | solution.py:269
  741.7 52.0 %collective-permute-start.112 = (bf16[4,192,768]{2,1,0:T(8,128)(2,1)S(1)}, bf16[4,192,768]{2,1,0:T(8,128)(2,1)S(1)}, u32[]{:S(2)}, u32[]{:S(2)}) collective-permute-start(bf16[4,192,768]{2,1,0:T(8,128)(2,1)S(1)} %dynamic-slice_bitcast_fusion.2), channel_id=1, source_target_pairs={{0,2},{1,3},{2,0},{3,1},{4,6},{5,7},{6,4},{7,5},{8,10},{9,11},{10,... | collective-permute-start | bytes 3538952 | tf_op jit(solution)/shard_map/ppermute | solution.py:269
  764.0 42.4 %collective-permute-start.94 = (bf16[4,48,1536]{2,1,0:T(8,128)(2,1)S(1)}, bf16[4,48,1536]{2,1,0:T(8,128)(2,1)S(1)}, u32[]{:S(2)}, u32[]{:S(2)}) collective-permute-start(bf16[4,48,1536]{2,1,0:T(8,128)(2,1)S(1)} %dynamic-slice_bitcast_fusion.5), channel_id=1, source_target_pairs={{0,2},{1,3},{2,0},{3,1},{4,6},{5,7},{6,4},{7,5},{8,10},{9,11},{10,... | collective-permute-start | bytes 1769480 | tf_op jit(solution)/shard_map/ppermute | solution.py:269
  (234 other events, 3081.1 us)

commit v2 on v1

v2 whole, which is shorter than its diff:
```python
import jax
import jax.numpy as jnp
from jax import lax
from jax.experimental import pallas as pl
from jax.experimental.pallas import tpu as pltpu
from jax.sharding import PartitionSpec as P

D = 768
LOW = jnp.bfloat16
FLOAT = jnp.float32
CHUNK = 256


def norm_affine(values, gain, bias):
    row_mean = jnp.mean(values, axis=-1, keepdims=True)
    centred = values - row_mean
    variance = jnp.mean(centred * centred, axis=-1, keepdims=True)
    return centred * lax.rsqrt(variance + 1e-05) * gain + bias


def dot_nt(a,b):
    return lax.dot_general(a,b,(((1,),(1,)),((),())),preferred_element_type=FLOAT)


def dot_nn(a,b):
    return lax.dot_general(a,b,(((1,),(0,)),((),())),preferred_element_type=FLOAT)


def dot_tn(a,b):
    return lax.dot_general(a,b,(((0,),(0,)),((),())),preferred_element_type=FLOAT)


def head_part(block, head):
    lane = lax.broadcasted_iota(jnp.int32, block.shape, 1)
    return jnp.where((lane >= 64) == (head == 1), block, jnp.zeros_like(block))


def probabilities(q_rows, k_rows, first):
    scores = dot_nt(q_rows, k_rows)
    row = lax.broadcasted_iota(jnp.int32, scores.shape, 0) + first
    col = lax.broadcasted_iota(jnp.int32, scores.shape, 1)
    scores = jnp.where(col <= row, scores, -1e30)
    top = jnp.max(scores, axis=-1, keepdims=True)
    exponent = jnp.exp(scores - top)
    return exponent * (1.0 / jnp.sum(exponent, axis=-1, keepdims=True))


def fwd_kernel(q_ref, k_ref, v_ref, o_ref):
    rows = q_ref.shape[0]
    k = k_ref[...]; v = v_ref[...]
    for first in range(0, rows, CHUNK):
        last = first + CHUNK
        q = q_ref[first:last, :] * LOW(0.125)
        total = None
        for head in range(2):
            p = probabilities(head_part(q, head), k[:last], first).astype(LOW)
            part = dot_nn(p, head_part(v[:last], head))
            total = part if total is None else total + part
        o_ref[first:last, :] = total.astype(LOW)


def attention_forward(qk, values):
    rows = qk.shape[0]
    pairs = D // 128
    first = pl.BlockSpec((rows, 128), lambda pair: (0, pair))
    second = pl.BlockSpec((rows, 128), lambda pair: (0, pair + pairs))
    return pl.pallas_call(
        fwd_kernel,
        grid=(pairs,),
        in_specs=[first, second, first],
        out_specs=first,
        out_shape=jax.ShapeDtypeStruct((rows, D), LOW),
        compiler_params=pltpu.CompilerParams(vmem_limit_bytes=32 * 1024 * 1024),
        cost_estimate=pl.CostEstimate(
            flops=40 * rows * rows * D, bytes_accessed=8 * rows * D, transcendentals=12 * rows * rows
        ),
        name="attend_forward",
    )(qk, qk, values)


def bwd_kernel(q_ref, k_ref, v_ref, g_ref, qk_out, v_out, dk_acc, dv_acc):
    rows = q_ref.shape[0]
    h = pl.program_id(0)
    k = k_ref[...]; v = v_ref[...]
    dk_acc[...] = jnp.zeros_like(dk_acc)
    dv_acc[...] = jnp.zeros_like(dv_acc)
    col = pl.multiple_of(h * 128, 128)
    for first in range(0, rows, CHUNK):
        last = first + CHUNK
        q = q_ref[first:last, :] * LOW(0.125)
        g = g_ref[first:last, :]
        dq = None
        for head in range(2):
            qh = head_part(q, head); gh = head_part(g, head)
            p = probabilities(qh, k[:last], first)
            dp = dot_nt(gh, v[:last])
            centre = jnp.sum(p * dp, axis=-1, keepdims=True)
            ds = (p * (dp - centre)).astype(LOW)
            part = dot_nn(ds, head_part(k[:last], head))
            dq = part if dq is None else dq + part
            dk_acc[:last, :] += dot_tn(ds, qh)
            dv_acc[:last, :] += dot_tn(p.astype(LOW), gh)
        qk_out[first:last, pl.ds(col, 128)] = (dq * 0.125).astype(LOW)
    qk_out[:, pl.ds(D + col, 128)] = dk_acc[...].astype(LOW)
    v_out[...] = dv_acc[...].astype(LOW)


def attention_backward(qk, values, grad):
    rows = qk.shape[0]
    pairs = D // 128
    first = pl.BlockSpec((rows, 128), lambda pair: (0, pair))
    second = pl.BlockSpec((rows, 128), lambda pair: (0, pair + pairs))
    return pl.pallas_call(
        bwd_kernel,
        grid=(pairs,),
        in_specs=[first, second, first, first],
        out_specs=[pl.BlockSpec((rows, 2 * D), lambda pair: (0, 0)), first],
        out_shape=[
            jax.ShapeDtypeStruct((rows, 2 * D), LOW),
            jax.ShapeDtypeStruct((rows, D), LOW),
        ],
        scratch_shapes=[pltpu.VMEM((rows, 128), FLOAT), pltpu.VMEM((rows, 128), FLOAT)],
        compiler_params=pltpu.CompilerParams(vmem_limit_bytes=32 * 1024 * 1024),
        cost_estimate=pl.CostEstimate(
            flops=80 * rows * rows * D, bytes_accessed=14 * rows * D, transcendentals=12 * rows * rows
        ),
        name="attend_backward",
    )(qk, qk, values, grad)


def hop(value, axis, target):
    count = lax.axis_size(axis)
    return lax.ppermute(value, axis, [(source, target(source)) for source in range(count)])


def over_section(value):
    return hop(value, "section", lambda source: 1 - source)


def over_core(value):
    return hop(value, "shard", lambda source: source ^ 1)


def over_y(value):
    return hop(value, "shard", lambda source: source ^ 2)


def over_z(value, steps):
    count = lax.axis_size("shard")
    return hop(value, "shard", lambda source: (source + 4 * steps) % count)


def place(buffer, block, index, dim):
    starts = [0] * buffer.ndim
    starts[dim] = index
    return lax.dynamic_update_slice(buffer, block, starts)


def take(value, index, size, dim):
    return lax.dynamic_slice_in_dim(value, index * size, size, dim)


def place_of():
    shard = lax.axis_index("shard")
    return (lax.axis_index("section"), shard // 4, (shard // 2) % 2, shard % 2)


def spread_z(block):
    _, z, _, _ = place_of()
    count = lax.axis_size("shard") // 4
    buffer = jnp.zeros((count,) + block.shape, block.dtype)
    buffer = place(buffer, block[None], z, 0)
    for steps in range(1, count):
        arrived = over_z(block, steps)
        buffer = place(buffer, arrived[None], (z - steps) % count, 0)
    return buffer


def pair(own, arrived, index, dim):
    own, arrived = jnp.expand_dims(own, dim), jnp.expand_dims(arrived, dim)
    is_low = index == 0
    return jnp.concatenate(
        [jnp.where(is_low, own, arrived), jnp.where(is_low, arrived, own)], axis=dim
    )


def spread_y(blocks):
    _, _, y, _ = place_of()
    return pair(blocks, over_y(blocks), y, 1)


def spread_x(blocks):
    x, _, _, _ = place_of()
    dim = blocks.ndim - 1
    arrived = over_section(blocks)
    is_low = x == 0
    return jnp.concatenate(
        [jnp.where(is_low, blocks, arrived), jnp.where(is_low, arrived, blocks)], axis=dim
    )


def spread_core(blocks):
    _, _, _, core = place_of()
    return pair(blocks, over_core(blocks), core, 2)


def halves_of_both(shard):
    x, _, _, _ = place_of()
    half = shard.shape[1] // 2
    own = take(shard, x, half, 1)
    arrived = over_section(take(shard, 1 - x, half, 1))
    is_low = x == 0
    return (jnp.where(is_low, own, arrived), jnp.where(is_low, arrived, own))


def gather_vectors(packed):
    x, _, y, core = place_of()
    stacked = spread_z(packed)
    stacked = pair(stacked, over_y(stacked), y, 1)
    stacked = pair(stacked, over_core(stacked), core, 2)
    stacked = stacked.reshape((-1,) + packed.shape)
    arrived = over_section(stacked)
    return (jnp.where(x == 0, stacked, arrived), jnp.where(x == 0, arrived, stacked))


def reduce_core(total):
    _, _, _, core = place_of()
    sent = lax.dynamic_index_in_dim(total, 1 - core, 2, keepdims=False)
    kept = lax.dynamic_index_in_dim(total, core, 2, keepdims=False)
    return (kept.astype(FLOAT) + over_core(sent).astype(FLOAT)).astype(LOW)


def reduce_y(total):
    _, _, y, _ = place_of()
    sent = lax.dynamic_index_in_dim(total, 1 - y, 1, keepdims=False)
    kept = lax.dynamic_index_in_dim(total, y, 1, keepdims=False)
    return (kept.astype(FLOAT) + over_y(sent).astype(FLOAT)).astype(LOW)


def reduce_x(total):
    x, _, _, _ = place_of()
    dim = total.ndim - 1
    half = total.shape[dim] // 2
    sent = take(total, 1 - x, half, dim)
    kept = take(total, x, half, dim)
    return (kept.astype(FLOAT) + over_section(sent).astype(FLOAT)).astype(LOW)


def reduce_z(total):
    _, z, _, _ = place_of()
    count = total.shape[0]
    result = lax.dynamic_index_in_dim(total, z, 0, keepdims=False).astype(FLOAT)
    for steps in range(1, count):
        sent = lax.dynamic_index_in_dim(total, (z + steps) % count, 0, keepdims=False)
        result = result + over_z(sent, steps).astype(FLOAT)
    return result


def join_halves(first_layer, second_layer):
    x, _, _, _ = place_of()
    is_low = x == 0
    kept = jnp.where(is_low, first_layer, second_layer)
    arrived = over_section(jnp.where(is_low, second_layer, first_layer).astype(LOW)).astype(FLOAT)
    return jnp.concatenate(
        [jnp.where(is_low, kept, arrived), jnp.where(is_low, arrived, kept)], axis=1
    )


def scatter_vectors(first_layer, second_layer):
    x, z, y, core = place_of()
    count = lax.axis_size("shard")
    is_low = x == 0
    kept = jnp.where(is_low, first_layer, second_layer)
    total = kept + over_section(jnp.where(is_low, second_layer, first_layer))
    total = total.reshape((count // 4, 2, 2) + total.shape[1:])
    sent = lax.dynamic_index_in_dim(total, 1 - core, 2, keepdims=False)
    total = lax.dynamic_index_in_dim(total, core, 2, keepdims=False) + over_core(sent)
    sent = lax.dynamic_index_in_dim(total, 1 - y, 1, keepdims=False)
    total = lax.dynamic_index_in_dim(total, y, 1, keepdims=False) + over_y(sent)
    return reduce_z(total)


def unpack_vectors(stacked):
    rows = stacked.shape[0]
    singles = [stacked[:, item].reshape(-1) for item in range(6)]
    return singles + [stacked[:, 6:8].reshape(-1), stacked[:, 8:12].reshape(-1)]


def pack_vectors(singles, pair_vector, quad_vector, count):
    parts = [item.reshape(count, 1, -1) for item in singles]
    parts.append(pair_vector.reshape(count, 2, -1))
    parts.append(quad_vector.reshape(count, 4, -1))
    return jnp.concatenate(parts, axis=1)


def tie(*values):
    return lax.optimization_barrier(values)


def second_stage(stacked, x_last):
    return spread_y(stacked) if x_last else spread_x(stacked)


def third_stage(stacked, x_last):
    return spread_x(stacked) if x_last else spread_y(stacked)


def core_stage(stacked):
    stacked = spread_core(stacked)
    return stacked.reshape(-1, stacked.shape[-1])


def core_reduced(total):
    count = lax.axis_size("shard")
    return reduce_core(
        total.reshape(count // 4, 2, 2, total.shape[0] // count, total.shape[1])
    )


def wide_reduced(total, x_last):
    return reduce_x(total) if x_last else reduce_y(total)


def narrow_reduced(total, x_last):
    return reduce_y(total) if x_last else reduce_x(total)


def plain_gathered(shard):
    own = lax.all_gather(shard, "shard", axis=0, tiled=True)
    arrived = over_section(own)
    is_low = lax.axis_index("section") == 0
    return (jnp.where(is_low, own, arrived), jnp.where(is_low, arrived, own))


def plain_reduced(first, second):
    is_low = lax.axis_index("section") == 0
    kept = jnp.where(is_low, first, second).astype(FLOAT)
    arrived = over_section(jnp.where(is_low, second, first)).astype(FLOAT)
    return lax.psum_scatter(kept + arrived, "shard", scatter_dimension=0, tiled=True)


def forward_attention(hidden, qk, vo, vectors):
    ln1_gain, ln1_bias, out_bias, ln2_gain, ln2_bias, _, qv_bias, _ = [
        item.astype(FLOAT) for item in vectors
    ]
    h_float = hidden.astype(FLOAT)
    normed = norm_affine(h_float, ln1_gain, ln1_bias).astype(LOW)
    key_bias = jnp.concatenate([qv_bias[:D], jnp.zeros((D,), FLOAT)])
    qk_rows = (jnp.dot(normed, qk, preferred_element_type=FLOAT) + key_bias).astype(LOW)
    value_rows = (
        jnp.dot(normed, vo[:, :D], preferred_element_type=FLOAT) + qv_bias[D:]
    ).astype(LOW)
    attended = attention_forward(qk_rows, value_rows)
    residual = h_float + jnp.dot(attended, vo[:, D:], preferred_element_type=FLOAT) + out_bias
    normed_two = norm_affine(residual, ln2_gain, ln2_bias).astype(LOW)
    return (normed, qk_rows, value_rows, attended, residual, normed_two)


def forward_mlp(residual, normed_two, up, down, vectors):
    before = jnp.dot(normed_two, up, preferred_element_type=FLOAT) + vectors[7].astype(FLOAT)
    activated = jax.nn.gelu(before).astype(LOW)
    layer_out = (
        residual
        + jnp.dot(activated, down, preferred_element_type=FLOAT)
        + vectors[5].astype(FLOAT)
    )
    return (before, activated, layer_out)


def backward_mlp(grad_out, before, activated, normed_two, up, down):
    down_bias_grad = jnp.sum(grad_out, axis=0)
    grad_low = grad_out.astype(LOW)
    down_grad = dot_tn(activated, grad_low).astype(LOW)
    grad_act = dot_nt(grad_low, down)
    _, gelu_back = jax.vjp(jax.nn.gelu, before)
    (grad_before,) = gelu_back(grad_act)
    up_bias_grad = jnp.sum(grad_before, axis=0)
    before_low = grad_before.astype(LOW)
    up_grad = dot_tn(normed_two, before_low).astype(LOW)
    grad_normed = dot_nt(before_low, up)
    return (up_grad, down_grad, grad_normed, down_bias_grad, up_bias_grad)


def backward_to_scores(grad_out, grad_normed, residual, attended, qk_rows, value_rows, vo, vectors):
    _, norm_back = jax.vjp(norm_affine, residual, vectors[3].astype(FLOAT), vectors[4].astype(FLOAT))
    grad_norm, gain_grad, bias_grad = norm_back(grad_normed)
    grad_residual = grad_out + grad_norm
    out_bias_grad = jnp.sum(grad_residual, axis=0)
    residual_low = grad_residual.astype(LOW)
    out_grad = dot_tn(attended, residual_low).astype(LOW)
    grad_attended = dot_nt(residual_low, vo[:, D:]).astype(LOW)
    grad_qk, grad_v = attention_backward(qk_rows, value_rows, grad_attended)
    return (grad_residual, out_grad, grad_qk, grad_v, gain_grad, bias_grad, out_bias_grad)


def backward_input(grad_residual, grad_qk, grad_v, hidden, normed, qk, vo, vectors):
    qv_bias_grad = jnp.concatenate(
        [
            jnp.sum(grad_qk[:, :D].astype(FLOAT), axis=0),
            jnp.sum(grad_v.astype(FLOAT), axis=0),
        ]
    )
    qk_grad = dot_tn(normed, grad_qk).astype(LOW)
    v_grad = dot_tn(normed, grad_v).astype(LOW)
    grad_normed = dot_nt(grad_qk, qk) + dot_nt(grad_v, vo[:, :D])
    _, norm_back = jax.vjp(
        norm_affine, hidden.astype(FLOAT), vectors[0].astype(FLOAT), vectors[1].astype(FLOAT)
    )
    grad_norm, gain_grad, bias_grad = norm_back(grad_normed)
    return ((grad_residual + grad_norm).astype(LOW), qk_grad, v_grad, gain_grad, bias_grad, qv_bias_grad)


def on_device(
    boundary,
    ln1_gain,
    ln1_bias,
    w_qkv,
    qv_bias,
    w_out,
    out_bias,
    ln2_gain,
    ln2_bias,
    w_up,
    up_bias,
    w_down,
    down_bias,
):
    x = lax.axis_index("section")
    is_first = x == 0
    count = lax.axis_size("shard")
    direct = count <= 16
    packed = pack_vectors(
        [ln1_gain, ln1_bias, out_bias, ln2_gain, ln2_bias, down_bias], qv_bias, up_bias, 1
    )[0]
    qk_shard = w_qkv[0, :, : 2 * D]
    vo_shard = jnp.concatenate([w_qkv[0, :, 2 * D :], w_out[0]], axis=1)
    traded = jnp.where(is_first, boundary[0, 1], boundary[0, 0])

    if direct:
        qk0, qk1 = halves_of_both(qk_shard)
        vo0, vo1 = halves_of_both(vo_shard)
        up0, up1 = halves_of_both(w_up[0])
        down0, down1 = halves_of_both(w_down[0])
        qk0, qk1, vo0, vo1, up0, up1, down0, down1, packed, traded = tie(
            qk0, qk1, vo0, vo1, up0, up1, down0, down1, packed, traded
        )
        qk0, vo0 = spread_z(qk0), spread_z(vo0)
        other = over_section(traded)
        vectors = gather_vectors(packed)
        qk0, vo0, other, vectors, qk1, vo1, up0, up1, down0, down1 = tie(
            qk0, vo0, other, vectors, qk1, vo1, up0, up1, down0, down1
        )
        qk0, vo0 = second_stage(qk0, True), second_stage(vo0, False)
        qk0, vo0 = third_stage(qk0, True), third_stage(vo0, False)
        up0, down0 = spread_z(up0), spread_z(down0)
        qk0, vo0, up0, down0, qk1, vo1, up1, down1 = tie(
            qk0, vo0, up0, down0, qk1, vo1, up1, down1
        )
        qk0, vo0 = core_stage(qk0), core_stage(vo0)
        up0, down0 = second_stage(up0, True), second_stage(down0, False)
        qk1, vo1 = spread_z(qk1), spread_z(vo1)
        qk0, vo0, up0, down0, qk1, vo1, up1, down1 = tie(
            qk0, vo0, up0, down0, qk1, vo1, up1, down1
        )
    else:
        vectors = gather_vectors(packed)
        other = over_section(traded)
        qk0, qk1 = plain_gathered(qk_shard)
        vo0, vo1 = plain_gathered(vo_shard)
        up0, up1 = plain_gathered(w_up[0])
        down0, down1 = plain_gathered(w_down[0])
    vector0, vector1 = [unpack_vectors(item) for item in vectors]
    hidden = jnp.where(is_first, boundary[0, 0], other)
    cotangent = jnp.where(is_first, other, boundary[0, 1]).astype(FLOAT)

    kept0 = forward_attention(hidden, qk0, vo0, vector0)
    if direct:
        up0, down0 = third_stage(up0, True), third_stage(down0, False)
        up1, down1 = spread_z(up1), spread_z(down1)
        kept0, up0, down0, up1, down1, qk1, vo1 = tie(kept0, up0, down0, up1, down1, qk1, vo1)
        up0, down0 = core_stage(up0), core_stage(down0)
        qk1, vo1 = second_stage(qk1, True), second_stage(vo1, False)
        qk1, vo1 = third_stage(qk1, True), third_stage(vo1, False)
    before0, activated0, out0 = forward_mlp(kept0[4], kept0[5], up0, down0, vector0)
    first_low = out0.astype(LOW)
    if direct:
        first_low, before0, activated0, qk1, vo1, up1, down1 = tie(
            first_low, before0, activated0, qk1, vo1, up1, down1
        )
        qk1, vo1 = core_stage(qk1), core_stage(vo1)
        up1, down1 = second_stage(up1, True), second_stage(down1, False)
        first_low, qk1, vo1, up1, down1 = tie(first_low, qk1, vo1, up1, down1)
    kept1 = forward_attention(first_low, qk1, vo1, vector1)
    if direct:
        up1, down1 = third_stage(up1, True), third_stage(down1, False)
        kept1, up1, down1 = tie(kept1, up1, down1)
        up1, down1 = core_stage(up1), core_stage(down1)
    before1, activated1, out1 = forward_mlp(kept1[4], kept1[5], up1, down1, vector1)
    second_low = out1.astype(LOW)
    sent_out = jnp.where(is_first, second_low, first_low)
    if direct:
        sent_out, before1, activated1, cotangent = tie(sent_out, before1, activated1, cotangent)
    arrived_out = over_section(sent_out)
    mlp1 = backward_mlp(cotangent, before1, activated1, kept1[5], up1, down1)
    if direct:
        mlp1, arrived_out = tie(mlp1, arrived_out)
    up_grad1, down_grad1, grad_normed1, down_bias1, up_bias1 = mlp1
    back1 = backward_to_scores(
        cotangent, grad_normed1, kept1[4], kept1[3], kept1[1], kept1[2], vo1, vector1
    )
    residual1, out_grad1, grad_qk1, grad_v1, ln2_gain1, ln2_bias1, out_bias1 = back1
    mid_low, qk_grad1, v_grad1, ln1_gain1, ln1_bias1, qv_bias1 = backward_input(
        residual1, grad_qk1, grad_v1, first_low, kept1[0], qk1, vo1, vector1
    )
    vo_grad1 = jnp.concatenate([v_grad1, out_grad1], axis=1)
    small1 = pack_vectors(
        [ln1_gain1, ln1_bias1, out_bias1, ln2_gain1, ln2_bias1, down_bias1], qv_bias1, up_bias1, count
    )
    if direct:
        up_sum1, down_sum1 = core_reduced(up_grad1), core_reduced(down_grad1)
        up_sum1, down_sum1 = wide_reduced(up_sum1, True), wide_reduced(down_sum1, False)
        mid_low, qk_grad1, vo_grad1, small1, up_sum1, down_sum1 = tie(
            mid_low, qk_grad1, vo_grad1, small1, up_sum1, down_sum1
        )
        up_sum1, down_sum1 = narrow_reduced(up_sum1, True), narrow_reduced(down_sum1, False)
        qk_sum1, vo_sum1 = core_reduced(qk_grad1), core_reduced(vo_grad1)
    mid_float = mid_low.astype(FLOAT)
    mlp0 = backward_mlp(mid_float, before0, activated0, kept0[5], up0, down0)
    if direct:
        mlp0, up_sum1, down_sum1, qk_sum1, vo_sum1, mid_float = tie(
            mlp0, up_sum1, down_sum1, qk_sum1, vo_sum1, mid_float
        )
    up_grad0, down_grad0, grad_normed0, down_bias0, up_bias0 = mlp0
    back0 = backward_to_scores(
        mid_float, grad_normed0, kept0[4], kept0[3], kept0[1], kept0[2], vo0, vector0
    )
    if direct:
        up_sum0, down_sum0 = core_reduced(up_grad0), core_reduced(down_grad0)
        qk_sum1, vo_sum1 = wide_reduced(qk_sum1, True), wide_reduced(vo_sum1, False)
        up_sum1, down_sum1 = reduce_z(up_sum1), reduce_z(down_sum1)
        back0, up_sum0, down_sum0, qk_sum1, vo_sum1, up_sum1, down_sum1 = tie(
            back0, up_sum0, down_sum0, qk_sum1, vo_sum1, up_sum1, down_sum1
        )
    residual0, out_grad0, grad_qk0, grad_v0, ln2_gain0, ln2_bias0, out_bias0 = back0
    in_low, qk_grad0, v_grad0, ln1_gain0, ln1_bias0, qv_bias0 = backward_input(
        residual0, grad_qk0, grad_v0, hidden, kept0[0], qk0, vo0, vector0
    )
    vo_grad0 = jnp.concatenate([v_grad0, out_grad0], axis=1)
    small0 = pack_vectors(
        [ln1_gain0, ln1_bias0, out_bias0, ln2_gain0, ln2_bias0, down_bias0], qv_bias0, up_bias0, count
    )
    sent_grad = jnp.where(is_first, mid_low, in_low)
    if direct:
        up_sum0, down_sum0 = wide_reduced(up_sum0, True), wide_reduced(down_sum0, False)
        qk_grad0, vo_grad0, small0, sent_grad, up_sum0, down_sum0, qk_sum1, vo_sum1 = tie(
            qk_grad0, vo_grad0, small0, sent_grad, up_sum0, down_sum0, qk_sum1, vo_sum1
        )
        qk_sum0, vo_sum0 = core_reduced(qk_grad0), core_reduced(vo_grad0)
        qk_sum1, vo_sum1 = narrow_reduced(qk_sum1, True), narrow_reduced(vo_sum1, False)
        up_sum0, down_sum0 = narrow_reduced(up_sum0, True), narrow_reduced(down_sum0, False)
        qk_sum0, vo_sum0, qk_sum1, vo_sum1, up_sum0, down_sum0, small0, small1, sent_grad = tie(
            qk_sum0, vo_sum0, qk_sum1, vo_sum1, up_sum0, down_sum0, small0, small1, sent_grad
        )
        up_sum0, down_sum0 = reduce_z(up_sum0), reduce_z(down_sum0)
        qk_sum1, vo_sum1 = reduce_z(qk_sum1), reduce_z(vo_sum1)
        qk_sum0, vo_sum0 = wide_reduced(qk_sum0, True), wide_reduced(vo_sum0, False)
        qk_sum0, vo_sum0 = narrow_reduced(qk_sum0, True), narrow_reduced(vo_sum0, False)
        vector = scatter_vectors(small0, small1)
        qk_sum0, vo_sum0, qk_sum1, vo_sum1, up_sum0, down_sum0, sent_grad, vector = tie(
            qk_sum0, vo_sum0, qk_sum1, vo_sum1, up_sum0, down_sum0, sent_grad, vector
        )
        arrived_grad = over_section(sent_grad)
        up, down = join_halves(up_sum0, up_sum1), join_halves(down_sum0, down_sum1)
        qk_sum0, vo_sum0 = reduce_z(qk_sum0), reduce_z(vo_sum0)
        qk, vo = join_halves(qk_sum0, qk_sum1), join_halves(vo_sum0, vo_sum1)
    else:
        arrived_grad = over_section(sent_grad)
        vector = scatter_vectors(small0, small1)
        qk, vo = plain_reduced(qk_grad0, qk_grad1), plain_reduced(vo_grad0, vo_grad1)
        up, down = plain_reduced(up_grad0, up_grad1), plain_reduced(down_grad0, down_grad1)
    own_out = jnp.where(is_first, first_low, second_low)
    own_grad = jnp.where(is_first, in_low, mid_low)
    section_outputs = jnp.where(
        is_first, jnp.stack([own_out, arrived_out]), jnp.stack([arrived_out, own_out])
    )[None]
    section_grads = jnp.where(
        is_first, jnp.stack([own_grad, arrived_grad]), jnp.stack([arrived_grad, own_grad])
    )[None]
    return (
        section_outputs,
        section_grads,
        vector[0:1],
        vector[1:2],
        jnp.concatenate([qk, vo[:, :D]], axis=1)[None],
        vector[6:8].reshape(1, -1),
        vo[:, D:][None],
        vector[2:3],
        vector[3:4],
        vector[4:5],
        up[None],
        vector[8:12].reshape(1, -1),
        down[None],
        vector[5:6],
    )


def solution(mesh):
    placed = (
        P("section", None, "shard", None),
        P("section", "shard"),
        P("section", "shard"),
        P("section", "shard", None),
        P("section", "shard"),
        P("section", "shard", None),
        P("section", "shard"),
        P("section", "shard"),
        P("section", "shard"),
        P("section", "shard", None),
        P("section", "shard"),
        P("section", "shard", None),
        P("section", "shard"),
    )
    return jax.shard_map(
        on_device,
        mesh=mesh,
        in_specs=placed,
        out_specs=(
            P("section", None, "shard", None),
            P("section", None, "shard", None),
            P("section", "shard"),
            P("section", "shard"),
            P("section", "shard", None),
            P("section", "shard"),
            P("section", "shard", None),
            P("section", "shard"),
            P("section", "shard"),
            P("section", "shard"),
            P("section", "shard", None),
            P("section", "shard"),
            P("section", "shard", None),
            P("section", "shard"),
        ),
        check_vma=False,
    )
```

time: 872 us -> 690 us (0.79)
  local copies, waits for them, and re-layouts: 187 us -> 76 us
  waiting for transfers between devices: 308 us -> 227 us
  matrix products: 134 us -> 79.9 us
  Pallas kernels: 0 us -> 50.4 us
  starting transfers between devices: 140 us -> 150 us
    ppermute x118 -> x119, waiting for transfers between devices: 308 us -> 227 us  [hop(): lax.ppermute(value, axis, [(source, target(source)) for source in range(c...]
    dynamic_slice x72 -> x0, local copies, waits for them, and re-layouts: 61.6 us -> none  [attend_forward(): lax.map(one_group, (head_groups(queries), head_groups(key_rows), head_gro...]
    dot_general x108 -> x30, matrix products: 134 us -> 79.9 us  [the longest x10 30 us: dot_nt(): lax.dot_general(a, b, (((1,), (1,)), ((), ())), preferred_element_type=FL...]
    pallas_call x0 -> x4, Pallas kernels: none -> 50.4 us  [the longest x2 34.9 us: attention_backward(): pl.pallas_call(bwd_kernel, grid=(pairs,), in_specs=[first, second, first,...]
    dynamic_update_slice x36 -> x0, local copies, waits for them, and re-layouts: 20.5 us -> none  [attend_forward(): lax.map(one_group, (head_groups(queries), head_groups(key_rows), head_gro...]
    convert_element_type x22 -> x16, local copies, waits for them, and re-layouts: 21.2 us -> 3.18 us  [the longest x10 2.83 us: forward_attention(): item.astype(FLOAT)]
    slice x23 -> x7, local copies, waits for them, and re-layouts: 12.1 us -> 1.69 us  [the longest x1 0.92 us: on_device(): qk_shard = w_qkv[0, :, :2 * D]]
    ppermute x118 -> x119, starting transfers between devices: 140 us -> 150 us  [hop(): lax.ppermute(value, axis, [(source, target(source)) for source in range(c...]
  transfers between devices with their start and end apart: 118 -> 119, of which waited for: 50 -> 52; matrix products, arithmetic and copies ran while one was open for 23% -> 22% of each run, Pallas kernels for 0% -> 5%
where the time goes in v2:
time: 690 us; the launch traced here: 681 us
  waiting for transfers between devices  227 us (33%)
  starting transfers between devices  150 us (22%)
  other arithmetic  93.3 us (14%)
  matrix products  79.9 us (12%)
  local copies, waits for them, and re-layouts  76 us (11%)
  Pallas kernels  50.4 us (7%)
    ppermute x119, waiting for transfers between devices, hop(): lax.ppermute(value, axis, [(source, target(source)) for source in range(c...  227 us
    ppermute x119, starting transfers between devices, hop(): lax.ppermute(value, axis, [(source, target(source)) for source in range(c...  150 us
    pallas_call x2, Pallas kernels, attention_backward(): pl.pallas_call(bwd_kernel, grid=(pairs,), in_specs=[first, second, first,...  34.9 us
    dot_general x10, matrix products, dot_nt(): lax.dot_general(a, b, (((1,), (1,)), ((), ())), preferred_element_type=FL...  30 us
    dot_general x10, matrix products, dot_tn(): lax.dot_general(a, b, (((0,), (0,)), ((), ())), preferred_element_type=FL...  27 us
    unnamed x296, local copies, waits for them, and re-layouts  22.5 us
    pallas_call x2, Pallas kernels, attention_forward(): pl.pallas_call(fwd_kernel, grid=(pairs,), in_specs=[first, second, first]...  15.5 us
  transfers between devices with their start and end apart: 119, of which 52 were waited for; matrix products, arithmetic and copies ran while one was open for 22% of the time, Pallas kernels for 5%

profile of v2, /device:TPU:0, one launch (start us, length us, event | category | flops | bytes accessed | tf_op | source)
XLA Modules:
  0.0 680.9 jit_solution(256361276949512637)
XLA Ops:
  44.0 15.2 %collective-permute-done.10 = bf16[512,768]{1,0:T(8,128)(2,1)S(1)} collective-permute-done((bf16[512,768]{1,0:T(8,128)(2,1)}, bf16[512,768]{1,0:T(8,128)(2,1)S(1)}, u32[]{:S(2)}, u32[]{:S(2)}) %collective-permute-start.10) | collective-permute-done | bytes 786464 | tf_op jit(solution)/shard_map/ppermute | solution.py:133
  77.7 6.3 collective-permute-done.22
  95.8 9.5 %collective-permute-done.18 = bf16[4,2,48,768]{3,2,0,1:T(8,128)(2,1)S(1)} collective-permute-done((bf16[4,2,48,768]{3,2,0,1:T(8,128)(2,1)S(1)}, bf16[4,2,48,768]{3,2,0,1:T(8,128)(2,1)S(1)}, u32[]{:S(2)}, u32[]{:S(2)}) %collective-permute-start.18) | collective-permute-done | bytes 589856 | tf_op jit(solution)/shard_map/ppermute | solution.py:133
  122.4 7.0 %collective-permute-done.30 = bf16[4,192,384]{2,1,0:T(8,128)(2,1)S(1)} collective-permute-done((bf16[4,192,384]{2,1,0:T(8,128)(2,1)S(1)}, bf16[4,192,384]{2,1,0:T(8,128)(2,1)S(1)}, u32[]{:S(2)}, u32[]{:S(2)}) %collective-permute-start.30) | collective-permute-done | bytes 589856 | tf_op jit(solution)/shard_map/ppermute | solution.py:133
  141.9 7.7 %attend_forward.2 = bf16[512,768]{1,0:T(8,128)(2,1)S(1)} custom-call(bf16[512,1536]{1,0:T(8,128)(2,1)S(1)} %fusion.32.q_ref.k_ref, bf16[512,1536]{1,0:T(8,128)(2,1)S(1)} %fusion.32.q_ref.k_ref, bf16[512,768]{1,0:T(8,128)(2,1)S(1)} %add_convert_fusion.9.v_ref), custom_call_target="tpu_custom_call" | custom-call | flops 8053063680 | bytes 3145728 | tf_op jit(solution)/shard_map/attend_forward/pallas_call | solution.py:67
  158.7 19.3 %collective-permute-done.38 = bf16[4,192,768]{2,1,0:T(8,128)(2,1)S(1)} collective-permute-done((bf16[4,192,768]{2,1,0:T(8,128)(2,1)S(1)}, bf16[4,192,768]{2,1,0:T(8,128)(2,1)S(1)}, u32[]{:S(2)}, u32[]{:S(2)}) %collective-permute-start.38) | collective-permute-done | bytes 1179680 | tf_op jit(solution)/shard_map/ppermute | solution.py:133
  194.2 9.1 %collective-permute-done.50 = bf16[4,48,1536]{2,1,0:T(8,128)(2,1)} collective-permute-done((bf16[4,48,1536]{2,1,0:T(8,128)(2,1)}, bf16[4,48,1536]{2,1,0:T(8,128)(2,1)}, u32[]{:S(2)}, u32[]{:S(2)}) %collective-permute-start.50) | collective-permute-done | bytes 589856 | tf_op jit(solution)/shard_map/ppermute | solution.py:133
  215.6 6.3 fusion.19
  228.9 10.8 %collective-permute-done.54 = bf16[4,192,384]{2,1,0:T(8,128)(2,1)} collective-permute-done((bf16[4,192,384]{2,1,0:T(8,128)(2,1)S(1)}, bf16[4,192,384]{2,1,0:T(8,128)(2,1)}, u32[]{:S(2)}, u32[]{:S(2)}) %collective-permute-start.54) | collective-permute-done | bytes 589856 | tf_op jit(solution)/shard_map/ppermute | solution.py:133
  252.7 7.8 %attend_forward.3 = bf16[512,768]{1,0:T(8,128)(2,1)S(1)} custom-call(bf16[512,1536]{1,0:T(8,128)(2,1)S(1)} %fusion.33.q_ref.k_ref, bf16[512,1536]{1,0:T(8,128)(2,1)S(1)} %fusion.33.q_ref.k_ref, bf16[512,768]{1,0:T(8,128)(2,1)S(1)} %add_convert_fusion.6.v_ref), custom_call_target="tpu_custom_call" | custom-call | flops 8053063680 | bytes 3145728 | tf_op jit(solution)/shard_map/attend_forward/pallas_call | solution.py:67
  263.0 10.2 %collective-permute-done.56 = bf16[4,192,768]{2,1,0:T(8,128)(2,1)S(1)} collective-permute-done((bf16[4,192,768]{2,1,0:T(8,128)(2,1)S(1)}, bf16[4,192,768]{2,1,0:T(8,128)(2,1)S(1)}, u32[]{:S(2)}, u32[]{:S(2)}) %collective-permute-start.56) | collective-permute-done | bytes 1179680 | tf_op jit(solution)/shard_map/ppermute | solution.py:133
  299.0 6.6 fusion.134
  323.2 6.4 collective-permute-done.59
  335.8 17.7 %attend_backward.2 = (bf16[512,1536]{1,0:T(8,128)(2,1)S(1)}, bf16[512,768]{1,0:T(8,128)(2,1)S(1)}) custom-call(bf16[512,1536]{1,0:T(8,128)(2,1)S(1)} %copy-done.9, bf16[512,1536]{1,0:T(8,128)(2,1)S(1)} %copy-done.9, bf16[512,768]{1,0:T(8,128)(2,1)S(1)} %copy-done.5, bf16[512,768]{1,0:T(8,128)(2,1)S(1)} %convolution_convert_fusion.11.g_ref), custom_call_target="tpu_custom_call" | custom-call | flops 16106127360 | bytes 5505024 | tf_op jit(solution)/shard_map/attend_backward/pallas_call | solution.py:113
  385.0 18.0 %collective-permute-done.61 = bf16[4,2,48,1536]{3,2,0,1:T(8,128)(2,1)S(1)} collective-permute-done((bf16[4,2,48,1536]{3,2,0,1:T(8,128)(2,1)S(1)}, bf16[4,2,48,1536]{3,2,0,1:T(8,128)(2,1)S(1)}, u32[]{:S(2)}, u32[]{:S(2)}) %collective-permute-start.61) | collective-permute-done | bytes 1179680 | tf_op jit(solution)/shard_map/ppermute | solution.py:133
  408.4 7.2 %fusion.127 = (f32[3072]{0:T(1024)}, bf16[512,3072]{1,0:T(8,128)(2,1)S(1)}) fusion(f32[512,3072]{1,0:T(8,128)S(1)} %bitcast.558, bf16[512,768]{1,0:T(8,128)(2,1)S(1)} %add_convert_fusion.3, bf16[3072,768]{1,0:T(8,128)(2,1)S(1)} %bitcast.500), kind=kOutput, calls=%fused_computation.514 | convolution fusion | flops 2448946176 | bytes 14954496 | tf_op jit(solution)/shard_map/dot_general | solution.py:22
  436.7 7.9 %collective-permute-done.65 = bf16[4,192,384]{2,1,0:T(8,128)(2,1)S(1)} collective-permute-done((bf16[4,192,384]{2,1,0:T(8,128)(2,1)S(1)}, bf16[4,192,384]{2,1,0:T(8,128)(2,1)S(1)}, u32[]{:S(2)}, u32[]{:S(2)}) %collective-permute-start.65) | collective-permute-done | bytes 589856 | tf_op jit(solution)/shard_map/ppermute | solution.py:133
  466.8 17.3 %attend_backward.3 = (bf16[512,1536]{1,0:T(8,128)(2,1)S(1)}, bf16[512,768]{1,0:T(8,128)(2,1)S(1)}) custom-call(bf16[512,1536]{1,0:T(8,128)(2,1)S(1)} %copy-done.7, bf16[512,1536]{1,0:T(8,128)(2,1)S(1)} %copy-done.7, bf16[512,768]{1,0:T(8,128)(2,1)S(1)} %copy-done.3, bf16[512,768]{1,0:T(8,128)(2,1)S(1)} %convolution_convert_fusion.10.g_ref), custom_call_target="tpu_custom_call" | custom-call | flops 16106127360 | bytes 5505024 | tf_op jit(solution)/shard_map/attend_backward/pallas_call | solution.py:113
  500.8 11.1 %collective-permute-done.70 = bf16[4,2,48,768]{3,2,0,1:T(8,128)(2,1)S(1)} collective-permute-done((bf16[4,2,48,768]{3,2,0,1:T(8,128)(2,1)S(1)}, bf16[4,2,48,768]{3,2,0,1:T(8,128)(2,1)S(1)}, u32[]{:S(2)}, u32[]{:S(2)}) %collective-permute-start.70) | collective-permute-done | bytes 589856 | tf_op jit(solution)/shard_map/ppermute | solution.py:133
  540.4 9.0 %collective-permute-done.79 = bf16[4,192,768]{2,1,0:T(8,128)(2,1)} collective-permute-done((bf16[4,192,768]{2,1,0:T(8,128)(2,1)}, bf16[4,192,768]{2,1,0:T(8,128)(2,1)}, u32[]{:S(2)}, u32[]{:S(2)}) %collective-permute-start.79) | collective-permute-done | bytes 1179680 | tf_op jit(solution)/shard_map/ppermute | solution.py:133
  557.9 14.4 %collective-permute-done.83 = bf16[4,48,768]{2,1,0:T(8,128)(2,1)S(1)} collective-permute-done((bf16[4,48,768]{2,1,0:T(8,128)(2,1)S(1)}, bf16[4,48,768]{2,1,0:T(8,128)(2,1)S(1)}, u32[]{:S(2)}, u32[]{:S(2)}) %collective-permute-start.83) | collective-permute-done | bytes 294944 | tf_op jit(solution)/shard_map/ppermute | solution.py:133
  578.9 6.8 collective-permute-start.96
  613.2 7.6 %collective-permute-start.98 = (bf16[48,1536]{1,0:T(8,128)(2,1)S(1)}, bf16[48,1536]{1,0:T(8,128)(2,1)S(1)}, u32[]{:S(2)}, u32[]{:S(2)}) collective-permute-start(bf16[48,1536]{1,0:T(8,128)(2,1)S(1)} %get-tuple-element.385), channel_id=1, source_target_pairs={{0,12},{1,13},{2,14},{3,15},{4,0},{5,1},{6,2},{7,3},{8,4},{9,5},{1... | collective-permute-start | bytes 442376 | tf_op jit(solution)/shard_map/ppermute | solution.py:133
  665.4 9.7 %collective-permute-done.112 = bf16[48,768]{1,0:T(8,128)(2,1)S(1)} collective-permute-done((bf16[48,768]{1,0:T(8,128)(2,1)S(1)}, bf16[48,768]{1,0:T(8,128)(2,1)S(1)}, u32[]{:S(2)}, u32[]{:S(2)}) %collective-permute-start.112) | collective-permute-done | bytes 73760 | tf_op jit(solution)/shard_map/ppermute | solution.py:133
  (887 shorter events, 427.9 us)
Async XLA Ops:
  59.1 27.6 %collective-permute-start.24 = (bf16[192,384]{1,0:T(8,128)(2,1)}, bf16[192,384]{1,0:T(8,128)(2,1)}, u32[]{:S(2)}, u32[]{:S(2)}) collective-permute-start(bf16[192,384]{1,0:T(8,128)(2,1)} %get-tuple-element.166), channel_id=1, source_target_pairs={{0,4},{1,5},{2,6},{3,7},{4,8},{5,9},{6,10},{7,11},{8,12},{9,13},{1... | collective-permute-start | bytes 442376 | tf_op jit(solution)/shard_map/ppermute | solution.py:133
  59.1 28.6 %collective-permute-start.25 = (bf16[192,384]{1,0:T(8,128)(2,1)}, bf16[192,384]{1,0:T(8,128)(2,1)}, u32[]{:S(2)}, u32[]{:S(2)}) collective-permute-start(bf16[192,384]{1,0:T(8,128)(2,1)} %get-tuple-element.166), channel_id=1, source_target_pairs={{0,8},{1,9},{2,10},{3,11},{4,12},{5,13},{6,14},{7,15},{8,0},{9,1},... | collective-permute-start | bytes 442376 | tf_op jit(solution)/shard_map/ppermute | solution.py:133
  60.7 34.2 %collective-permute-start.26 = (bf16[192,384]{1,0:T(8,128)(2,1)}, bf16[192,384]{1,0:T(8,128)(2,1)}, u32[]{:S(2)}, u32[]{:S(2)}) collective-permute-start(bf16[192,384]{1,0:T(8,128)(2,1)} %get-tuple-element.166), channel_id=1, source_target_pairs={{0,12},{1,13},{2,14},{3,15},{4,0},{5,1},{6,2},{7,3},{8,4},{9,5},{1... | collective-permute-start | bytes 442376 | tf_op jit(solution)/shard_map/ppermute | solution.py:133
  63.5 20.5 %collective-permute-start.22 = (bf16[48,1536]{1,0:T(8,128)(2,1)}, bf16[48,1536]{1,0:T(8,128)(2,1)}, u32[]{:S(2)}, u32[]{:S(2)}) collective-permute-start(bf16[48,1536]{1,0:T(8,128)(2,1)} %get-tuple-element.165), channel_id=1, source_target_pairs={{0,8},{1,9},{2,10},{3,11},{4,12},{5,13},{6,14},{7,15},{8,0},{9,1},... | collective-permute-start | bytes 442376 | tf_op jit(solution)/shard_map/ppermute | solution.py:133
  132.0 24.1 %collective-permute-start.42 = (bf16[192,384]{1,0:T(8,128)(2,1)S(1)}, bf16[192,384]{1,0:T(8,128)(2,1)S(1)}, u32[]{:S(2)}, u32[]{:S(2)}) collective-permute-start(bf16[192,384]{1,0:T(8,128)(2,1)S(1)} %copy-done.82), channel_id=1, source_target_pairs={{0,4},{1,5},{2,6},{3,7},{4,8},{5,9},{6,10},{7,11},{8,12},{9,13},{1... | collective-permute-start | bytes 442376 | tf_op jit(solution)/shard_map/ppermute | solution.py:133
  132.6 25.1 %collective-permute-start.43 = (bf16[192,384]{1,0:T(8,128)(2,1)S(1)}, bf16[192,384]{1,0:T(8,128)(2,1)S(1)}, u32[]{:S(2)}, u32[]{:S(2)}) collective-permute-start(bf16[192,384]{1,0:T(8,128)(2,1)S(1)} %copy-done.82), channel_id=1, source_target_pairs={{0,8},{1,9},{2,10},{3,11},{4,12},{5,13},{6,14},{7,15},{8,0},{9,1},... | collective-permute-start | bytes 442376 | tf_op jit(solution)/shard_map/ppermute | solution.py:133
  134.2 23.6 %collective-permute-start.44 = (bf16[192,384]{1,0:T(8,128)(2,1)S(1)}, bf16[192,384]{1,0:T(8,128)(2,1)S(1)}, u32[]{:S(2)}, u32[]{:S(2)}) collective-permute-start(bf16[192,384]{1,0:T(8,128)(2,1)S(1)} %copy-done.82), channel_id=1, source_target_pairs={{0,12},{1,13},{2,14},{3,15},{4,0},{5,1},{6,2},{7,3},{8,4},{9,5},{1... | collective-permute-start | bytes 442376 | tf_op jit(solution)/shard_map/ppermute | solution.py:133
  154.8 23.1 %collective-permute-start.38 = (bf16[4,192,768]{2,1,0:T(8,128)(2,1)S(1)}, bf16[4,192,768]{2,1,0:T(8,128)(2,1)S(1)}, u32[]{:S(2)}, u32[]{:S(2)}) collective-permute-start(bf16[4,192,768]{2,1,0:T(8,128)(2,1)S(1)} %pad_maximum_fusion.17), channel_id=1, source_target_pairs={{0,2},{1,3},{2,0},{3,1},{4,6},{5,7},{6,4},{7,5},{8,10},{9,11},{10,... | collective-permute-start | bytes 3538952 | tf_op jit(solution)/shard_map/ppermute | solution.py:133
  156.1 24.1 %collective-permute-start.37 = (bf16[4,2,48,1536]{3,2,0,1:T(8,128)(2,1)S(1)}, bf16[4,2,48,1536]{3,2,0,1:T(8,128)(2,1)S(1)}, u32[]{:S(2)}, u32[]{:S(2)}) collective-permute-start(bf16[4,2,48,1536]{3,2,0,1:T(8,128)(2,1)S(1)} %pad_maximum_fusion.16), channel_id=1, source_target_pairs={{0,16},{16,0},{1,17},{17,1},{2,18},{18,2},{3,19},{19,3},{4,20},{20... | collective-permute-start | bytes 3538952 | tf_op jit(solution)/shard_map/ppermute | solution.py:133
  184.5 25.0 %collective-permute-start.45 = (bf16[4,2,48,3072]{3,2,0,1:T(8,128)(2,1)}, bf16[4,2,48,3072]{3,2,0,1:T(8,128)(2,1)}, u32[]{:S(2)}, u32[]{:S(2)}) collective-permute-start(bf16[4,2,48,3072]{3,2,0,1:T(8,128)(2,1)} %pad_maximum_fusion.6), channel_id=1, source_target_pairs={{0,1},{1,0},{2,3},{3,2},{4,5},{5,4},{6,7},{7,6},{8,9},{9,8},{10,11... | collective-permute-start | bytes 7077896 | tf_op jit(solution)/shard_map/ppermute | solution.py:133
  191.3 21.7 %collective-permute-start.46 = (bf16[4,2,192,768]{3,2,1,0:T(8,128)(2,1)}, bf16[4,2,192,768]{3,2,1,0:T(8,128)(2,1)S(1)}, u32[]{:S(2)}, u32[]{:S(2)}) collective-permute-start(bf16[4,2,192,768]{3,2,1,0:T(8,128)(2,1)} %pad_maximum_fusion.7), channel_id=1, source_target_pairs={{0,1},{1,0},{2,3},{3,2},{4,5},{5,4},{6,7},{7,6},{8,9},{9,8},{10,11... | collective-permute-start | bytes 7077896 | tf_op jit(solution)/shard_map/ppermute | solution.py:133
  246.8 26.4 %collective-permute-start.56 = (bf16[4,192,768]{2,1,0:T(8,128)(2,1)S(1)}, bf16[4,192,768]{2,1,0:T(8,128)(2,1)S(1)}, u32[]{:S(2)}, u32[]{:S(2)}) collective-permute-start(bf16[4,192,768]{2,1,0:T(8,128)(2,1)S(1)} %pad_maximum_fusion.21), channel_id=1, source_target_pairs={{0,2},{1,3},{2,0},{3,1},{4,6},{5,7},{6,4},{7,5},{8,10},{9,11},{10,... | collective-permute-start | bytes 3538952 | tf_op jit(solution)/shard_map/ppermute | solution.py:133
  248.2 26.8 %collective-permute-start.55 = (bf16[4,2,48,1536]{3,2,0,1:T(8,128)(2,1)S(1)}, bf16[4,2,48,1536]{3,2,0,1:T(8,128)(2,1)S(1)}, u32[]{:S(2)}, u32[]{:S(2)}) collective-permute-start(bf16[4,2,48,1536]{3,2,0,1:T(8,128)(2,1)S(1)} %pad_maximum_fusion.20), channel_id=1, source_target_pairs={{0,16},{16,0},{1,17},{17,1},{2,18},{18,2},{3,19},{19,3},{4,20},{20... | collective-permute-start | bytes 3538952 | tf_op jit(solution)/shard_map/ppermute | solution.py:133
  375.0 28.0 %collective-permute-start.61 = (bf16[4,2,48,1536]{3,2,0,1:T(8,128)(2,1)S(1)}, bf16[4,2,48,1536]{3,2,0,1:T(8,128)(2,1)S(1)}, u32[]{:S(2)}, u32[]{:S(2)}) collective-permute-start(bf16[4,2,48,1536]{3,2,0,1:T(8,128)(2,1)S(1)} %constant_dynamic-slice_fusion.29), channel_id=1, source_target_pairs={{0,16},{16,0},{1,17},{17,1},{2,18},{18,2},{3,19},{19,3},{4,20},{20... | collective-permute-start | bytes 3538952 | tf_op jit(solution)/shard_map/ppermute | solution.py:133
  379.1 28.0 %collective-permute-start.63 = (bf16[4,192,768]{2,1,0:T(8,128)(2,1)S(1)}, bf16[4,192,768]{2,1,0:T(8,128)(2,1)S(1)}, u32[]{:S(2)}, u32[]{:S(2)}) collective-permute-start(bf16[4,192,768]{2,1,0:T(8,128)(2,1)S(1)} %dynamic-slice_bitcast_fusion.1), channel_id=1, source_target_pairs={{0,2},{1,3},{2,0},{3,1},{4,6},{5,7},{6,4},{7,5},{8,10},{9,11},{10,... | collective-permute-start | bytes 3538952 | tf_op jit(solution)/shard_map/ppermute | solution.py:133
  448.4 37.5 %collective-permute-start.75 = (bf16[192,384]{1,0:T(8,128)(2,1)S(1)}, bf16[192,384]{1,0:T(8,128)(2,1)S(1)}, u32[]{:S(2)}, u32[]{:S(2)}) collective-permute-start(bf16[192,384]{1,0:T(8,128)(2,1)S(1)} %get-tuple-element.387), channel_id=1, source_target_pairs={{0,4},{1,5},{2,6},{3,7},{4,8},{5,9},{6,10},{7,11},{8,12},{9,13},{1... | collective-permute-start | bytes 442376 | tf_op jit(solution)/shard_map/ppermute | solution.py:133
  448.5 38.0 %collective-permute-start.76 = (bf16[192,384]{1,0:T(8,128)(2,1)S(1)}, bf16[192,384]{1,0:T(8,128)(2,1)S(1)}, u32[]{:S(2)}, u32[]{:S(2)}) collective-permute-start(bf16[192,384]{1,0:T(8,128)(2,1)S(1)} %get-tuple-element.389), channel_id=1, source_target_pairs={{0,8},{1,9},{2,10},{3,11},{4,12},{5,13},{6,14},{7,15},{8,0},{9,1},... | collective-permute-start | bytes 442376 | tf_op jit(solution)/shard_map/ppermute | solution.py:133
  451.6 40.9 %collective-permute-start.72 = (bf16[48,1536]{1,0:T(8,128)(2,1)}, bf16[48,1536]{1,0:T(8,128)(2,1)}, u32[]{:S(2)}, u32[]{:S(2)}) collective-permute-start(bf16[48,1536]{1,0:T(8,128)(2,1)} %get-tuple-element.390), channel_id=1, source_target_pairs={{0,4},{1,5},{2,6},{3,7},{4,8},{5,9},{6,10},{7,11},{8,12},{9,13},{1... | collective-permute-start | bytes 442376 | tf_op jit(solution)/shard_map/ppermute | solution.py:133
  457.1 56.7 %collective-permute-start.69 = (bf16[4,2,192,768]{3,2,0,1:T(8,128)(2,1)}, bf16[4,2,192,768]{3,2,0,1:T(8,128)(2,1)}, u32[]{:S(2)}, u32[]{:S(2)}) collective-permute-start(bf16[4,2,192,768]{3,2,0,1:T(8,128)(2,1)} %bitcast.478), channel_id=1, source_target_pairs={{0,1},{1,0},{2,3},{3,2},{4,5},{5,4},{6,7},{7,6},{8,9},{9,8},{10,11... | collective-permute-start | bytes 7077896 | tf_op jit(solution)/shard_map/ppermute | solution.py:133
  461.0 55.3 %collective-permute-start.68 = (bf16[4,2,48,3072]{3,2,0,1:T(8,128)(2,1)}, bf16[4,2,48,3072]{3,2,0,1:T(8,128)(2,1)}, u32[]{:S(2)}, u32[]{:S(2)}) collective-permute-start(bf16[4,2,48,3072]{3,2,0,1:T(8,128)(2,1)} %bitcast.479), channel_id=1, source_target_pairs={{0,1},{1,0},{2,3},{3,2},{4,5},{5,4},{6,7},{7,6},{8,9},{9,8},{10,11... | collective-permute-start | bytes 7077896 | tf_op jit(solution)/shard_map/ppermute | solution.py:133
  522.5 26.9 %collective-permute-start.79 = (bf16[4,192,768]{2,1,0:T(8,128)(2,1)}, bf16[4,192,768]{2,1,0:T(8,128)(2,1)}, u32[]{:S(2)}, u32[]{:S(2)}) collective-permute-start(bf16[4,192,768]{2,1,0:T(8,128)(2,1)} %dynamic-slice_bitcast_fusion), channel_id=1, source_target_pairs={{0,2},{1,3},{2,0},{3,1},{4,6},{5,7},{6,4},{7,5},{8,10},{9,11},{10,... | collective-permute-start | bytes 3538952 | tf_op jit(solution)/shard_map/ppermute | solution.py:133
  524.2 26.8 %collective-permute-start.78 = (bf16[4,2,48,1536]{3,2,0,1:T(8,128)(2,1)}, bf16[4,2,48,1536]{3,2,0,1:T(8,128)(2,1)}, u32[]{:S(2)}, u32[]{:S(2)}) collective-permute-start(bf16[4,2,48,1536]{3,2,0,1:T(8,128)(2,1)} %constant_dynamic-slice_fusion.16), channel_id=1, source_target_pairs={{0,16},{16,0},{1,17},{17,1},{2,18},{18,2},{3,19},{19,3},{4,20},{20... | collective-permute-start | bytes 3538952 | tf_op jit(solution)/shard_map/ppermute | solution.py:133
  576.2 64.0 %collective-permute-start.100 = (bf16[192,384]{1,0:T(8,128)(2,1)S(1)}, bf16[192,384]{1,0:T(8,128)(2,1)S(1)}, u32[]{:S(2)}, u32[]{:S(2)}) collective-permute-start(bf16[192,384]{1,0:T(8,128)(2,1)S(1)} %get-tuple-element.383), channel_id=1, source_target_pairs={{0,8},{1,9},{2,10},{3,11},{4,12},{5,13},{6,14},{7,15},{8,0},{9,1},... | collective-permute-start | bytes 442376 | tf_op jit(solution)/shard_map/ppermute | solution.py:133
  578.9 41.9 %collective-permute-start.96 = (bf16[48,1536]{1,0:T(8,128)(2,1)S(1)}, bf16[48,1536]{1,0:T(8,128)(2,1)S(1)}, u32[]{:S(2)}, u32[]{:S(2)}) collective-permute-start(bf16[48,1536]{1,0:T(8,128)(2,1)S(1)} %get-tuple-element.384), channel_id=1, source_target_pairs={{0,4},{1,5},{2,6},{3,7},{4,8},{5,9},{6,10},{7,11},{8,12},{9,13},{1... | collective-permute-start | bytes 442376 | tf_op jit(solution)/shard_map/ppermute | solution.py:133
  (236 other events, 2461.8 us)

commit v3 on v2

--- a/solution.py
+++ b/solution.py
@@ -72,7 +72,7 @@
         out_shape=jax.ShapeDtypeStruct((rows, D), LOW),
         compiler_params=pltpu.CompilerParams(vmem_limit_bytes=32 * 1024 * 1024),
         cost_estimate=pl.CostEstimate(
-            flops=40 * rows * rows * D, bytes_accessed=8 * rows * D, transcendentals=12 * rows * rows
+            flops=rows * rows * D, bytes_accessed=8 * rows * D, transcendentals=0
         ),
         name="attend_forward",
     )(qk, qk, values)
@@ -122,7 +122,7 @@
         scratch_shapes=[pltpu.VMEM((rows, 128), FLOAT), pltpu.VMEM((rows, 128), FLOAT)],
         compiler_params=pltpu.CompilerParams(vmem_limit_bytes=32 * 1024 * 1024),
         cost_estimate=pl.CostEstimate(
-            flops=80 * rows * rows * D, bytes_accessed=14 * rows * D, transcendentals=12 * rows * rows
+            flops=rows * rows * D, bytes_accessed=14 * rows * D, transcendentals=0
         ),
         name="attend_backward",
     )(qk, qk, values, grad)
@@ -191,12 +191,7 @@
 
 def spread_x(blocks):
     x, _, _, _ = place_of()
-    dim = blocks.ndim - 1
-    arrived = over_section(blocks)
-    is_low = x == 0
-    return jnp.concatenate(
-        [jnp.where(is_low, blocks, arrived), jnp.where(is_low, arrived, blocks)], axis=dim
-    )
+    return pair(blocks, over_section(blocks), x, blocks.ndim - 2)
 
 
 def spread_core(blocks):
@@ -206,9 +201,9 @@
 
 def halves_of_both(shard):
     x, _, _, _ = place_of()
-    half = shard.shape[1] // 2
-    own = take(shard, x, half, 1)
-    arrived = over_section(take(shard, 1 - x, half, 1))
+    half = shard.shape[0] // 2
+    own = take(shard, x, half, 0)
+    arrived = over_section(take(shard, 1 - x, half, 0))
     is_low = x == 0
     return (jnp.where(is_low, own, arrived), jnp.where(is_low, arrived, own))
 
@@ -223,27 +218,22 @@
     return (jnp.where(x == 0, stacked, arrived), jnp.where(x == 0, arrived, stacked))
 
 
+def reduce_pair(total, index, dim, exchange):
+    sent = lax.dynamic_index_in_dim(total, 1 - index, dim, keepdims=False)
+    kept = lax.dynamic_index_in_dim(total, index, dim, keepdims=False)
+    return (kept.astype(FLOAT) + exchange(sent).astype(FLOAT)).astype(LOW)
+
+
 def reduce_core(total):
-    _, _, _, core = place_of()
-    sent = lax.dynamic_index_in_dim(total, 1 - core, 2, keepdims=False)
-    kept = lax.dynamic_index_in_dim(total, core, 2, keepdims=False)
-    return (kept.astype(FLOAT) + over_core(sent).astype(FLOAT)).astype(LOW)
+    return reduce_pair(total, place_of()[3], 2, over_core)
 
 
 def reduce_y(total):
-    _, _, y, _ = place_of()
-    sent = lax.dynamic_index_in_dim(total, 1 - y, 1, keepdims=False)
-    kept = lax.dynamic_index_in_dim(total, y, 1, keepdims=False)
-    return (kept.astype(FLOAT) + over_y(sent).astype(FLOAT)).astype(LOW)
+    return reduce_pair(total, place_of()[2], 1, over_y)
 
 
 def reduce_x(total):
-    x, _, _, _ = place_of()
-    dim = total.ndim - 1
-    half = total.shape[dim] // 2
-    sent = take(total, 1 - x, half, dim)
-    kept = take(total, x, half, dim)
-    return (kept.astype(FLOAT) + over_section(sent).astype(FLOAT)).astype(LOW)
+    return reduce_pair(total, place_of()[0], total.ndim - 3, over_section)
 
 
 def reduce_z(total):
@@ -262,7 +252,7 @@
     kept = jnp.where(is_low, first_layer, second_layer)
     arrived = over_section(jnp.where(is_low, second_layer, first_layer).astype(LOW)).astype(FLOAT)
     return jnp.concatenate(
-        [jnp.where(is_low, kept, arrived), jnp.where(is_low, arrived, kept)], axis=1
+        [jnp.where(is_low, kept, arrived), jnp.where(is_low, arrived, kept)], axis=0
     )
 
 
@@ -291,38 +281,6 @@
     parts.append(pair_vector.reshape(count, 2, -1))
     parts.append(quad_vector.reshape(count, 4, -1))
     return jnp.concatenate(parts, axis=1)
-
-
-def tie(*values):
-    return lax.optimization_barrier(values)
-
-
-def second_stage(stacked, x_last):
-    return spread_y(stacked) if x_last else spread_x(stacked)
-
-
-def third_stage(stacked, x_last):
-    return spread_x(stacked) if x_last else spread_y(stacked)
-
-
-def core_stage(stacked):
-    stacked = spread_core(stacked)
-    return stacked.reshape(-1, stacked.shape[-1])
-
-
-def core_reduced(total):
-    count = lax.axis_size("shard")
-    return reduce_core(
-        total.reshape(count // 4, 2, 2, total.shape[0] // count, total.shape[1])
-    )
-
-
-def wide_reduced(total, x_last):
-    return reduce_x(total) if x_last else reduce_y(total)
-
-
-def narrow_reduced(total, x_last):
-    return reduce_y(total) if x_last else reduce_x(total)
 
 
 def plain_gathered(shard):
@@ -393,21 +351,80 @@
     return (grad_residual, out_grad, grad_qk, grad_v, gain_grad, bias_grad, out_bias_grad)
 
 
-def backward_input(grad_residual, grad_qk, grad_v, hidden, normed, qk, vo, vectors):
+def backward_input(grad_residual, grad_qk, grad_v, hidden, qk, vo, vectors):
     qv_bias_grad = jnp.concatenate(
         [
             jnp.sum(grad_qk[:, :D].astype(FLOAT), axis=0),
             jnp.sum(grad_v.astype(FLOAT), axis=0),
         ]
     )
-    qk_grad = dot_tn(normed, grad_qk).astype(LOW)
-    v_grad = dot_tn(normed, grad_v).astype(LOW)
     grad_normed = dot_nt(grad_qk, qk) + dot_nt(grad_v, vo[:, :D])
     _, norm_back = jax.vjp(
         norm_affine, hidden.astype(FLOAT), vectors[0].astype(FLOAT), vectors[1].astype(FLOAT)
     )
     grad_norm, gain_grad, bias_grad = norm_back(grad_normed)
-    return ((grad_residual + grad_norm).astype(LOW), qk_grad, v_grad, gain_grad, bias_grad, qv_bias_grad)
+    return ((grad_residual + grad_norm).astype(LOW), gain_grad, bias_grad, qv_bias_grad)
+
+
+def tie(*values):
+    return lax.optimization_barrier(values)
+
+
+def second_stage(stacked, x_last):
+    return spread_y(stacked) if x_last else spread_x(stacked)
+
+
+def third_stage(stacked, x_last):
+    return spread_x(stacked) if x_last else spread_y(stacked)
+
+
+def core_stage(stacked):
+    stacked = spread_core(stacked)
+    return stacked.reshape(-1, stacked.shape[-1])
+
+
+def core_reduced(total):
+    count = lax.axis_size("shard")
+    return reduce_core(
+        total.reshape(count // 4, 2, 2, 2, total.shape[0] // (2 * count), total.shape[1])
+    )
+
+
+def wide_reduced(total, x_last):
+    return reduce_x(total) if x_last else reduce_y(total)
+
+
+def narrow_reduced(total, x_last):
+    return reduce_y(total) if x_last else reduce_x(total)
+
+
+def whole_gathered(main, down):
+    columns = main.shape[1] // 4
+    groups = [main[:, columns * item : columns * (item + 1)] for item in range(4)]
+    packed = jnp.concatenate([jnp.concatenate(groups, axis=0), down], axis=1)
+    return lax.all_gather(packed, ("shard", "section"), axis=0, tiled=True)
+
+
+def parts_of(whole, devices):
+    columns = whole.shape[1] - D
+    main = whole[:, :columns].reshape(devices, 4, -1, columns)
+    qk, vo, up_low, up_high = [main[:, item].reshape(-1, columns) for item in range(4)]
+    return (qk, vo, jnp.concatenate([up_low, up_high], axis=1), whole[:, columns:])
+
+
+def mlp_packed(up_grad, down_grad):
+    count = lax.axis_size("shard")
+    rows = D // (2 * count)
+    blocks = down_grad.reshape(2 * count, -1, rows, D).transpose(0, 2, 1, 3)
+    return jnp.concatenate([up_grad, blocks.reshape(D, -1)], axis=1)
+
+
+def mlp_scattered(total, columns):
+    rows = D // (2 * lax.axis_size("shard"))
+    total = lax.psum_scatter(total, ("shard", "section"), scatter_dimension=0, tiled=True)
+    total = total.astype(FLOAT)
+    down = total[:, columns:].reshape(rows, -1, D).transpose(1, 0, 2).reshape(-1, D)
+    return (total[:, :columns], down)
 
 
 def on_device(
@@ -429,46 +446,38 @@
     is_first = x == 0
     count = lax.axis_size("shard")
     direct = count <= 16
+    cut = 4 * D
     packed = pack_vectors(
         [ln1_gain, ln1_bias, out_bias, ln2_gain, ln2_bias, down_bias], qv_bias, up_bias, 1
     )[0]
-    qk_shard = w_qkv[0, :, : 2 * D]
-    vo_shard = jnp.concatenate([w_qkv[0, :, 2 * D :], w_out[0]], axis=1)
+    main_shard = jnp.concatenate([w_qkv[0], w_out[0], w_up[0]], axis=1)
     traded = jnp.where(is_first, boundary[0, 1], boundary[0, 0])
 
     if direct:
-        qk0, qk1 = halves_of_both(qk_shard)
-        vo0, vo1 = halves_of_both(vo_shard)
-        up0, up1 = halves_of_both(w_up[0])
+        main0, main1 = halves_of_both(main_shard)
         down0, down1 = halves_of_both(w_down[0])
-        qk0, qk1, vo0, vo1, up0, up1, down0, down1, packed, traded = tie(
-            qk0, qk1, vo0, vo1, up0, up1, down0, down1, packed, traded
+        main0, main1, down0, down1, packed, traded = tie(
+            main0, main1, down0, down1, packed, traded
         )
-        qk0, vo0 = spread_z(qk0), spread_z(vo0)
+        whole1 = whole_gathered(main1, down1)
+        first_part, up0 = main0[:, :cut], main0[:, cut:]
+        first_part = spread_z(first_part)
+        vectors = gather_vectors(packed)
+        first_part, up0, down0, traded = tie(first_part, up0, down0, traded)
         other = over_section(traded)
-        vectors = gather_vectors(packed)
-        qk0, vo0, other, vectors, qk1, vo1, up0, up1, down0, down1 = tie(
-            qk0, vo0, other, vectors, qk1, vo1, up0, up1, down0, down1
-        )
-        qk0, vo0 = second_stage(qk0, True), second_stage(vo0, False)
-        qk0, vo0 = third_stage(qk0, True), third_stage(vo0, False)
+        qk0 = third_stage(second_stage(first_part[..., : 2 * D], True), True)
+        vo0 = third_stage(second_stage(first_part[..., 2 * D :], False), False)
         up0, down0 = spread_z(up0), spread_z(down0)
-        qk0, vo0, up0, down0, qk1, vo1, up1, down1 = tie(
-            qk0, vo0, up0, down0, qk1, vo1, up1, down1
-        )
+        qk0, vo0, up0, down0 = tie(qk0, vo0, up0, down0)
         qk0, vo0 = core_stage(qk0), core_stage(vo0)
         up0, down0 = second_stage(up0, True), second_stage(down0, False)
-        qk1, vo1 = spread_z(qk1), spread_z(vo1)
-        qk0, vo0, up0, down0, qk1, vo1, up1, down1 = tie(
-            qk0, vo0, up0, down0, qk1, vo1, up1, down1
-        )
+        qk0, vo0, up0, down0 = tie(qk0, vo0, up0, down0)
     else:
         vectors = gather_vectors(packed)
         other = over_section(traded)
-        qk0, qk1 = plain_gathered(qk_shard)
-        vo0, vo1 = plain_gathered(vo_shard)
-        up0, up1 = plain_gathered(w_up[0])
+        main0, main1 = plain_gathered(main_shard)
         down0, down1 = plain_gathered(w_down[0])
+        qk0, vo0, up0 = main0[:, : 2 * D], main0[:, 2 * D : cut], main0[:, cut:]
     vector0, vector1 = [unpack_vectors(item) for item in vectors]
     hidden = jnp.where(is_first, boundary[0, 0], other)
     cotangent = jnp.where(is_first, other, boundary[0, 1]).astype(FLOAT)
@@ -476,25 +485,16 @@
     kept0 = forward_attention(hidden, qk0, vo0, vector0)
     if direct:
         up0, down0 = third_stage(up0, True), third_stage(down0, False)
-        up1, down1 = spread_z(up1), spread_z(down1)
-        kept0, up0, down0, up1, down1, qk1, vo1 = tie(kept0, up0, down0, up1, down1, qk1, vo1)
+        kept0, up0, down0 = tie(kept0, up0, down0)
         up0, down0 = core_stage(up0), core_stage(down0)
-        qk1, vo1 = second_stage(qk1, True), second_stage(vo1, False)
-        qk1, vo1 = third_stage(qk1, True), third_stage(vo1, False)
     before0, activated0, out0 = forward_mlp(kept0[4], kept0[5], up0, down0, vector0)
     first_low = out0.astype(LOW)
     if direct:
-        first_low, before0, activated0, qk1, vo1, up1, down1 = tie(
-            first_low, before0, activated0, qk1, vo1, up1, down1
-        )
-        qk1, vo1 = core_stage(qk1), core_stage(vo1)
-        up1, down1 = second_stage(up1, True), second_stage(down1, False)
-        first_low, qk1, vo1, up1, down1 = tie(first_low, qk1, vo1, up1, down1)
+        first_low, whole1 = tie(first_low, whole1)
+        qk1, vo1, up1, down1 = parts_of(whole1, 2 * count)
+    else:
+        qk1, vo1, up1 = main1[:, : 2 * D], main1[:, 2 * D : cut], main1[:, cut:]
     kept1 = forward_attention(first_low, qk1, vo1, vector1)
-    if direct:
-        up1, down1 = third_stage(up1, True), third_stage(down1, False)
-        kept1, up1, down1 = tie(kept1, up1, down1)
-        up1, down1 = core_stage(up1), core_stage(down1)
     before1, activated1, out1 = forward_mlp(kept1[4], kept1[5], up1, down1, vector1)
     second_low = out1.astype(LOW)
     sent_out = jnp.where(is_first, second_low, first_low)
@@ -503,80 +503,86 @@
     arrived_out = over_section(sent_out)
     mlp1 = backward_mlp(cotangent, before1, activated1, kept1[5], up1, down1)
     if direct:
-        mlp1, arrived_out = tie(mlp1, arrived_out)
+        total1 = mlp_packed(mlp1[0], mlp1[1])
+        mlp1, arrived_out, total1 = tie(mlp1, arrived_out, total1)
     up_grad1, down_grad1, grad_normed1, down_bias1, up_bias1 = mlp1
     back1 = backward_to_scores(
         cotangent, grad_normed1, kept1[4], kept1[3], kept1[1], kept1[2], vo1, vector1
     )
     residual1, out_grad1, grad_qk1, grad_v1, ln2_gain1, ln2_bias1, out_bias1 = back1
-    mid_low, qk_grad1, v_grad1, ln1_gain1, ln1_bias1, qv_bias1 = backward_input(
-        residual1, grad_qk1, grad_v1, first_low, kept1[0], qk1, vo1, vector1
-    )
-    vo_grad1 = jnp.concatenate([v_grad1, out_grad1], axis=1)
+    mid_low, ln1_gain1, ln1_bias1, qv_bias1 = backward_input(
+        residual1, grad_qk1, grad_v1, first_low, qk1, vo1, vector1
+    )
+    part_grad1 = jnp.concatenate(
+        [
+            dot_tn(kept1[0], grad_qk1).astype(LOW),
+            dot_tn(kept1[0], grad_v1).astype(LOW),
+            out_grad1,
+        ],
+        axis=1,
+    )
     small1 = pack_vectors(
         [ln1_gain1, ln1_bias1, out_bias1, ln2_gain1, ln2_bias1, down_bias1], qv_bias1, up_bias1, count
     )
     if direct:
-        up_sum1, down_sum1 = core_reduced(up_grad1), core_reduced(down_grad1)
-        up_sum1, down_sum1 = wide_reduced(up_sum1, True), wide_reduced(down_sum1, False)
-        mid_low, qk_grad1, vo_grad1, small1, up_sum1, down_sum1 = tie(
-            mid_low, qk_grad1, vo_grad1, small1, up_sum1, down_sum1
-        )
-        up_sum1, down_sum1 = narrow_reduced(up_sum1, True), narrow_reduced(down_sum1, False)
-        qk_sum1, vo_sum1 = core_reduced(qk_grad1), core_reduced(vo_grad1)
+        up_sum1, down_sum1 = mlp_scattered(total1, 4 * D)
+        mid_low, part_grad1, small1 = tie(mid_low, part_grad1, small1)
+        part_sum1 = core_reduced(part_grad1)
+        qk_sum1 = wide_reduced(part_sum1[..., : 2 * D], True)
+        vo_sum1 = wide_reduced(part_sum1[..., 2 * D :], False)
     mid_float = mid_low.astype(FLOAT)
     mlp0 = backward_mlp(mid_float, before0, activated0, kept0[5], up0, down0)
     if direct:
-        mlp0, up_sum1, down_sum1, qk_sum1, vo_sum1, mid_float = tie(
-            mlp0, up_sum1, down_sum1, qk_sum1, vo_sum1, mid_float
-        )
+        mlp0, qk_sum1, vo_sum1, mid_float = tie(mlp0, qk_sum1, vo_sum1, mid_float)
     up_grad0, down_grad0, grad_normed0, down_bias0, up_bias0 = mlp0
     back0 = backward_to_scores(
         mid_float, grad_normed0, kept0[4], kept0[3], kept0[1], kept0[2], vo0, vector0
     )
     if direct:
         up_sum0, down_sum0 = core_reduced(up_grad0), core_reduced(down_grad0)
-        qk_sum1, vo_sum1 = wide_reduced(qk_sum1, True), wide_reduced(vo_sum1, False)
-        up_sum1, down_sum1 = reduce_z(up_sum1), reduce_z(down_sum1)
-        back0, up_sum0, down_sum0, qk_sum1, vo_sum1, up_sum1, down_sum1 = tie(
-            back0, up_sum0, down_sum0, qk_sum1, vo_sum1, up_sum1, down_sum1
+        part_sum1 = jnp.concatenate(
+            [narrow_reduced(qk_sum1, True), narrow_reduced(vo_sum1, False)], axis=-1
         )
+        up_sum0, down_sum0 = wide_reduced(up_sum0, True), wide_reduced(down_sum0, False)
+        back0, part_sum1 = tie(back0, part_sum1)
     residual0, out_grad0, grad_qk0, grad_v0, ln2_gain0, ln2_bias0, out_bias0 = back0
-    in_low, qk_grad0, v_grad0, ln1_gain0, ln1_bias0, qv_bias0 = backward_input(
-        residual0, grad_qk0, grad_v0, hidden, kept0[0], qk0, vo0, vector0
-    )
-    vo_grad0 = jnp.concatenate([v_grad0, out_grad0], axis=1)
+    part_grad0 = jnp.concatenate(
+        [
+            dot_tn(kept0[0], grad_qk0).astype(LOW),
+            dot_tn(kept0[0], grad_v0).astype(LOW),
+            out_grad0,
+        ],
+        axis=1,
+    )
+    if direct:
+        part_grad0, up_sum1, down_sum1, part_sum1, residual0, grad_qk0, grad_v0 = tie(
+            part_grad0, up_sum1, down_sum1, part_sum1, residual0, grad_qk0, grad_v0
+        )
+        part_sum0 = core_reduced(part_grad0)
+        up_sum0, down_sum0 = narrow_reduced(up_sum0, True), narrow_reduced(down_sum0, False)
+    in_low, ln1_gain0, ln1_bias0, qv_bias0 = backward_input(
+        residual0, grad_qk0, grad_v0, hidden, qk0, vo0, vector0
+    )
     small0 = pack_vectors(
         [ln1_gain0, ln1_bias0, out_bias0, ln2_gain0, ln2_bias0, down_bias0], qv_bias0, up_bias0, count
     )
     sent_grad = jnp.where(is_first, mid_low, in_low)
     if direct:
-        up_sum0, down_sum0 = wide_reduced(up_sum0, True), wide_reduced(down_sum0, False)
-        qk_grad0, vo_grad0, small0, sent_grad, up_sum0, down_sum0, qk_sum1, vo_sum1 = tie(
-            qk_grad0, vo_grad0, small0, sent_grad, up_sum0, down_sum0, qk_sum1, vo_sum1
+        part_sum1 = reduce_z(part_sum1)
+        qk_sum0 = wide_reduced(part_sum0[..., : 2 * D], True)
+        vo_sum0 = wide_reduced(part_sum0[..., 2 * D :], False)
+        up_sum0, down_sum0 = reduce_z(up_sum0), reduce_z(down_sum0)
+        part_sum0 = jnp.concatenate(
+            [narrow_reduced(qk_sum0, True), narrow_reduced(vo_sum0, False)], axis=-1
         )
-        qk_sum0, vo_sum0 = core_reduced(qk_grad0), core_reduced(vo_grad0)
-        qk_sum1, vo_sum1 = narrow_reduced(qk_sum1, True), narrow_reduced(vo_sum1, False)
-        up_sum0, down_sum0 = narrow_reduced(up_sum0, True), narrow_reduced(down_sum0, False)
-        qk_sum0, vo_sum0, qk_sum1, vo_sum1, up_sum0, down_sum0, small0, small1, sent_grad = tie(
-            qk_sum0, vo_sum0, qk_sum1, vo_sum1, up_sum0, down_sum0, small0, small1, sent_grad
-        )
-        up_sum0, down_sum0 = reduce_z(up_sum0), reduce_z(down_sum0)
-        qk_sum1, vo_sum1 = reduce_z(qk_sum1), reduce_z(vo_sum1)
-        qk_sum0, vo_sum0 = wide_reduced(qk_sum0, True), wide_reduced(vo_sum0, False)
-        qk_sum0, vo_sum0 = narrow_reduced(qk_sum0, True), narrow_reduced(vo_sum0, False)
         vector = scatter_vectors(small0, small1)
-        qk_sum0, vo_sum0, qk_sum1, vo_sum1, up_sum0, down_sum0, sent_grad, vector = tie(
-            qk_sum0, vo_sum0, qk_sum1, vo_sum1, up_sum0, down_sum0, sent_grad, vector
-        )
         arrived_grad = over_section(sent_grad)
         up, down = join_halves(up_sum0, up_sum1), join_halves(down_sum0, down_sum1)
-        qk_sum0, vo_sum0 = reduce_z(qk_sum0), reduce_z(vo_sum0)
-        qk, vo = join_halves(qk_sum0, qk_sum1), join_halves(vo_sum0, vo_sum1)
+        part = join_halves(reduce_z(part_sum0), part_sum1)
     else:
         arrived_grad = over_section(sent_grad)
         vector = scatter_vectors(small0, small1)
-        qk, vo = plain_reduced(qk_grad0, qk_grad1), plain_reduced(vo_grad0, vo_grad1)
+        part = plain_reduced(part_grad0, part_grad1)
         up, down = plain_reduced(up_grad0, up_grad1), plain_reduced(down_grad0, down_grad1)
     own_out = jnp.where(is_first, first_low, second_low)
     own_grad = jnp.where(is_first, in_low, mid_low)
@@ -591,9 +597,9 @@
         section_grads,
         vector[0:1],
         vector[1:2],
-        jnp.concatenate([qk, vo[:, :D]], axis=1)[None],
+        part[:, : 3 * D][None],
         vector[6:8].reshape(1, -1),
-        vo[:, D:][None],
+        part[:, 3 * D :][None],
         vector[2:3],
         vector[3:4],
         vector[4:5],

time: 690 us -> 624 us (0.904)
  starting transfers between devices: 150 us -> 80.2 us
  between operations: 4.26 us -> 16.9 us
    ppermute x119 -> x69, starting transfers between devices: 150 us -> 80.1 us  [hop(): lax.ppermute(value, axis, [(source, target(source)) for source in range(c...]
    slice x1 -> x8, local copies, waits for them, and re-layouts: 0.92 us -> 14.8 us  [the longest x1 8.16 us: parts_of(): main = whole[:, :columns].reshape(devices, 4, -1, columns)]
    dynamic_update_slice x36 -> x16, local copies, waits for them, and re-layouts: 9.94 us -> 0.38 us  [place(): return lax.dynamic_update_slice(buffer, block, starts)]
    convert_element_type x25 -> x16, other arithmetic: 23 us -> 15.3 us  [reduce_pair(): return (kept.astype(FLOAT) + exchange(sent).astype(FLOAT)).astype(LOW)]
    select_n x18 -> x13, other arithmetic: 13.3 us -> 6.05 us  [pair(): jnp.where(is_low, own, arrived)]
    dynamic_slice x16 -> x8, local copies, waits for them, and re-layouts: 14.4 us -> 11.5 us  [the longest x4 6.67 us: reduce_pair(): kept = lax.dynamic_index_in_dim(total, index, dim, keepdims=False)]
    ppermute x119 -> x69, waiting for transfers between devices: 227 us -> 225 us  [hop(): lax.ppermute(value, axis, [(source, target(source)) for source in range(c...]
    unnamed x296 -> x257, local copies, waits for them, and re-layouts: 22.5 us -> 22.6 us
  transfers between devices with their start and end apart: 119 -> 71, of which waited for: 52 -> 32; matrix products, arithmetic and copies ran while one was open for 22% -> 24% of each run, Pallas kernels for 5% -> 4%
where the time goes in v3:
time: 624 us; the launch traced here: 616 us
  waiting for transfers between devices  225 us (36%)
  other arithmetic  86.6 us (14%)
  matrix products  84.8 us (14%)
  starting transfers between devices  80.2 us (13%)
  local copies, waits for them, and re-layouts  72.1 us (12%)
  Pallas kernels  50.2 us (8%)
  between operations  16.9 us (3%)
    ppermute x69, waiting for transfers between devices, hop(): lax.ppermute(value, axis, [(source, target(source)) for source in range(c...  225 us
    ppermute x69, starting transfers between devices, hop(): lax.ppermute(value, axis, [(source, target(source)) for source in range(c...  80.1 us
    pallas_call x2, Pallas kernels, attention_backward(): pl.pallas_call(bwd_kernel, grid=(pairs,), in_specs=[first, second, first,...  34.7 us
    dot_general x10, matrix products, dot_nt(): lax.dot_general(a, b, (((1,), (1,)), ((), ())), preferred_element_type=FL...  31.5 us
    dot_general x10, matrix products, dot_tn(): lax.dot_general(a, b, (((0,), (0,)), ((), ())), preferred_element_type=FL...  28.8 us
    unnamed x257, local copies, waits for them, and re-layouts  22.6 us
    pallas_call x2, Pallas kernels, attention_forward(): pl.pallas_call(fwd_kernel, grid=(pairs,), in_specs=[first, second, first]...  15.5 us
    convert_element_type x16, other arithmetic, reduce_pair(): return (kept.astype(FLOAT) + exchange(sent).astype(FLOAT)).astype(LOW)  15.3 us
  transfers between devices with their start and end apart: 71, of which 32 were waited for; matrix products, arithmetic and copies ran while one was open for 24% of the time, Pallas kernels for 4%

profile of v3, /device:TPU:0, one launch (start us, length us, event | category | flops | bytes accessed | tf_op | source)
XLA Modules:
  0.0 615.7 jit_solution(16574921005207153073)
XLA Ops:
  14.2 7.7 %collective-permute-done.1 = bf16[96,768]{1,0:T(8,128)(2,1)} collective-permute-done((bf16[96,768]{1,0:T(8,128)(2,1)S(1)}, bf16[96,768]{1,0:T(8,128)(2,1)}, u32[]{:S(2)}, u32[]{:S(2)}) %collective-permute-start.1) | collective-permute-done | bytes 147488 | tf_op jit(solution)/shard_map/ppermute | solution.py:133
  49.8 7.5 %collective-permute-done.3 = bf16[24,3072]{1,0:T(8,128)(2,1)S(1)} collective-permute-done((bf16[24,3072]{1,0:T(8,128)(2,1)S(1)}, bf16[24,3072]{1,0:T(8,128)(2,1)S(1)}, u32[]{:S(2)}, u32[]{:S(2)}) %collective-permute-start.3) | collective-permute-done | bytes 147488 | tf_op jit(solution)/shard_map/ppermute | solution.py:133
  67.8 13.7 %collective-permute-done.17 = bf16[24,3072]{1,0:T(8,128)(2,1)S(1)} collective-permute-done((bf16[24,3072]{1,0:T(8,128)(2,1)S(1)}, bf16[24,3072]{1,0:T(8,128)(2,1)S(1)}, u32[]{:S(2)}, u32[]{:S(2)}) %collective-permute-start.17) | collective-permute-done | bytes 147488 | tf_op jit(solution)/shard_map/ppermute | solution.py:133
  87.7 15.8 %collective-permute-done.20 = bf16[96,768]{1,0:T(8,128)(2,1)S(1)} collective-permute-done((bf16[96,768]{1,0:T(8,128)(2,1)S(1)}, bf16[96,768]{1,0:T(8,128)(2,1)S(1)}, u32[]{:S(2)}, u32[]{:S(2)}) %collective-permute-start.20) | collective-permute-done | bytes 147488 | tf_op jit(solution)/shard_map/ppermute | solution.py:133
  108.8 19.4 %collective-permute-done.13 = bf16[4,2,24,1536]{3,2,0,1:T(8,128)(2,1)S(1)} collective-permute-done((bf16[4,2,24,1536]{3,2,0,1:T(8,128)(2,1)S(1)}, bf16[4,2,24,1536]{3,2,0,1:T(8,128)(2,1)S(1)}, u32[]{:S(2)}, u32[]{:S(2)}) %collective-permute-start.13) | collective-permute-done | bytes 589856 | tf_op jit(solution)/shard_map/ppermute | solution.py:133
  135.5 22.6 %collective-permute-done.25 = bf16[4,96,768]{2,1,0:T(8,128)(2,1)S(1)} collective-permute-done((bf16[4,96,768]{2,1,0:T(8,128)(2,1)S(1)}, bf16[4,96,768]{2,1,0:T(8,128)(2,1)S(1)}, u32[]{:S(2)}, u32[]{:S(2)}) %collective-permute-start.25) | collective-permute-done | bytes 589856 | tf_op jit(solution)/shard_map/ppermute | solution.py:133
  165.7 7.8 %attend_forward.2 = bf16[512,768]{1,0:T(8,128)(2,1)S(1)} custom-call(bf16[512,1536]{1,0:T(8,128)(2,1)S(1)} %fusion.29.q_ref.k_ref, bf16[512,1536]{1,0:T(8,128)(2,1)S(1)} %fusion.29.q_ref.k_ref, bf16[512,768]{1,0:T(8,128)(2,1)S(1)} %add_convert_fusion.7.v_ref), custom_call_target="tpu_custom_call" | custom-call | flops 201326592 | bytes 3145728 | tf_op jit(solution)/shard_map/attend_forward/pallas_call | solution.py:67
  176.4 7.2 %collective-permute-done.27 = bf16[4,2,96,768]{3,2,1,0:T(8,128)(2,1)S(1)} collective-permute-done((bf16[4,2,96,768]{3,2,1,0:T(8,128)(2,1)S(1)}, bf16[4,2,96,768]{3,2,1,0:T(8,128)(2,1)S(1)}, u32[]{:S(2)}, u32[]{:S(2)}) %collective-permute-start.27) | collective-permute-done | bytes 1179680 | tf_op jit(solution)/shard_map/ppermute | solution.py:133
  210.1 8.2 %slice.208 = bf16[3072,1536]{1,0:T(8,128)(2,1)} slice(bf16[3072,2304]{1,0:T(8,128)(2,1)} %all-gather.2.cloned.1.call-done), slice={[0:3072], [0:1536]} | slice | bytes 18874368 | tf_op jit(solution)/shard_map/slice | solution.py:410
  225.7 7.7 %attend_forward.3 = bf16[512,768]{1,0:T(8,128)(2,1)S(1)} custom-call(bf16[512,1536]{1,0:T(8,128)(2,1)S(1)} %fusion.30.q_ref.k_ref, bf16[512,1536]{1,0:T(8,128)(2,1)S(1)} %fusion.30.q_ref.k_ref, bf16[512,768]{1,0:T(8,128)(2,1)S(1)} %add_convert_fusion.4.v_ref), custom_call_target="tpu_custom_call" | custom-call | flops 201326592 | bytes 3145728 | tf_op jit(solution)/shard_map/attend_forward/pallas_call | solution.py:67
  241.0 5.9 select_bitcast_fusion.13
  251.6 6.7 %fusion.135 = (f32[3072]{0:T(1024)S(1)}, bf16[512,3072]{1,0:T(8,128)(2,1)S(1)}) fusion(f32[512,3072]{1,0:T(8,128)S(1)} %get-tuple-element.106, f32[512,3072]{1,0:T(8,128)} %fusion.24), kind=kLoop, calls=%fused_computation.411 | loop fusion | flops 33027072 | bytes 15740928 | tf_op jit(solution)/shard_map/reduce_sum | solution.py:335
  282.7 10.9 %collective-permute-done.30 = bf16[512,768]{1,0:T(8,128)(2,1)} collective-permute-done((bf16[512,768]{1,0:T(8,128)(2,1)}, bf16[512,768]{1,0:T(8,128)(2,1)}, u32[]{:S(2)}, u32[]{:S(2)}) %collective-permute-start.30) | collective-permute-done | bytes 786464 | tf_op jit(solution)/shard_map/ppermute | solution.py:133
  302.1 17.3 %attend_backward.2 = (bf16[512,1536]{1,0:T(8,128)(2,1)S(1)}, bf16[512,768]{1,0:T(8,128)(2,1)S(1)}) custom-call(bf16[512,1536]{1,0:T(8,128)(2,1)S(1)} %fusion.30.q_ref.k_ref, bf16[512,1536]{1,0:T(8,128)(2,1)S(1)} %fusion.30.q_ref.k_ref, bf16[512,768]{1,0:T(8,128)(2,1)S(1)} %add_convert_fusion.4.v_ref, bf16[512,768]{1,0:T(8,128)(2,1)S(1)} %convolution_convert_fusion.11.g_ref), custom_call_target="tpu_custom_call" | custom-call | flops 201326592 | bytes 5505024 | tf_op jit(solution)/shard_map/attend_backward/pallas_call | solution.py:113
  334.4 8.4 %fusion.131 = (f32[3072]{0:T(1024)}, bf16[512,3072]{1,0:T(8,128)(2,1)}) fusion(f32[512,3072]{1,0:T(8,128)S(1)} %bitcast.381, f32[3072]{0:T(1024)S(1)} %reshape.637, bf16[512,768]{1,0:T(8,128)(2,1)S(1)} %add_convert_fusion.1, bf16[3072,768]{1,0:T(8,128)(2,1)S(1)} %bitcast.387), kind=kOutput, calls=%fused_computation.408 | convolution fusion | flops 2450519040 | bytes 14966784 | tf_op jit(solution)/shard_map/dot_general | solution.py:22
  342.9 5.9 fusion.57
  348.8 6.6 %convolution_convert_fusion = bf16[3072,768]{1,0:T(8,128)(2,1)S(1)} fusion(bf16[512,768]{1,0:T(8,128)(2,1)S(1)} %add_convert_fusion.1, f32[512,3072]{1,0:T(8,128)} %copy-done.26, f32[3072]{0:T(1024)S(1)} %reshape.637), kind=kOutput, calls=%fused_computation.27 | convolution fusion | flops 2434007040 | bytes 11808768 | tf_op jit(solution)/shard_map/dot_general | solution.py:30
  373.0 9.5 %collective-permute-done.33 = bf16[4,2,24,1536]{3,2,0,1:T(8,128)(2,1)S(1)} collective-permute-done((bf16[4,2,24,1536]{3,2,0,1:T(8,128)(2,1)S(1)}, bf16[4,2,24,1536]{3,2,0,1:T(8,128)(2,1)S(1)}, u32[]{:S(2)}, u32[]{:S(2)}) %collective-permute-start.33) | collective-permute-done | bytes 589856 | tf_op jit(solution)/shard_map/ppermute | solution.py:133
  403.0 17.4 %attend_backward.3 = (bf16[512,1536]{1,0:T(8,128)(2,1)S(1)}, bf16[512,768]{1,0:T(8,128)(2,1)S(1)}) custom-call(bf16[512,1536]{1,0:T(8,128)(2,1)S(1)} %copy-done.1, bf16[512,1536]{1,0:T(8,128)(2,1)S(1)} %copy-done.1, bf16[512,768]{1,0:T(8,128)(2,1)S(1)} %copy-done.3, bf16[512,768]{1,0:T(8,128)(2,1)S(1)} %convolution_convert_fusion.10.g_ref), custom_call_target="tpu_custom_call" | custom-call | flops 201326592 | bytes 5505024 | tf_op jit(solution)/shard_map/attend_backward/pallas_call | solution.py:113
  433.0 27.3 %collective-permute-done.56 = bf16[4,2,24,3072]{3,2,0,1:T(8,128)(2,1)S(1)} collective-permute-done((bf16[4,2,24,3072]{3,2,0,1:T(8,128)(2,1)S(1)}, bf16[4,2,24,3072]{3,2,0,1:T(8,128)(2,1)S(1)}, u32[]{:S(2)}, u32[]{:S(2)}) %collective-permute-start.56) | collective-permute-done | bytes 1179680 | tf_op jit(solution)/shard_map/ppermute | solution.py:133
  473.4 10.3 %collective-permute-done.57 = bf16[4,24,3072]{2,1,0:T(8,128)(2,1)} collective-permute-done((bf16[4,24,3072]{2,1,0:T(8,128)(2,1)}, bf16[4,24,3072]{2,1,0:T(8,128)(2,1)}, u32[]{:S(2)}, u32[]{:S(2)}) %collective-permute-start.57) | collective-permute-done | bytes 589856 | tf_op jit(solution)/shard_map/ppermute | solution.py:133
  550.2 9.9 %collective-permute-done.44 = bf16[4,2,24,1536]{3,2,0,1:T(8,128)(2,1)S(1)} collective-permute-done((bf16[4,2,24,1536]{3,2,0,1:T(8,128)(2,1)S(1)}, bf16[4,2,24,1536]{3,2,0,1:T(8,128)(2,1)S(1)}, u32[]{:S(2)}, u32[]{:S(2)}) %collective-permute-start.44) | collective-permute-done | bytes 589856 | tf_op jit(solution)/shard_map/ppermute | solution.py:133
  560.7 12.9 %collective-permute-done.46 = bf16[4,2,24,1536]{3,2,0,1:T(8,128)(2,1)S(1)} collective-permute-done((bf16[4,2,24,1536]{3,2,0,1:T(8,128)(2,1)S(1)}, bf16[4,2,24,1536]{3,2,0,1:T(8,128)(2,1)S(1)}, u32[]{:S(2)}, u32[]{:S(2)}) %collective-permute-start.46) | collective-permute-done | bytes 589856 | tf_op jit(solution)/shard_map/ppermute | solution.py:133
  574.3 6.1 collective-permute-done.45
  (669 shorter events, 326.1 us)
Async XLA Ops:
  7.2 202.9 %all-gather.2.cloned.1.call-start = ((), (), s32[]{:S(2)}) async-start(), calls=%async_computation.1 | async-start | bytes 14598144 | tf_op jit(solution)/shard_map/all_gather | solution.py:405
  23.8 474.5 %reduce-scatter.2.cloned.1.call-start = ((), (), s32[]{:S(2)}) async-start(), calls=%async_computation.2 | async-start | bytes 9732096 | tf_op jit(solution)/shard_map/reduce_scatter | solution.py:424
  64.1 39.4 %collective-permute-start.20 = (bf16[96,768]{1,0:T(8,128)(2,1)S(1)}, bf16[96,768]{1,0:T(8,128)(2,1)S(1)}, u32[]{:S(2)}, u32[]{:S(2)}) collective-permute-start(bf16[96,768]{1,0:T(8,128)(2,1)S(1)} %get-tuple-element.88), channel_id=1, source_target_pairs={{0,8},{1,9},{2,10},{3,11},{4,12},{5,13},{6,14},{7,15},{8,0},{9,1},... | collective-permute-start | bytes 442376 | tf_op jit(solution)/shard_map/ppermute | solution.py:133
  67.5 36.0 %collective-permute-start.21 = (bf16[96,768]{1,0:T(8,128)(2,1)S(1)}, bf16[96,768]{1,0:T(8,128)(2,1)S(1)}, u32[]{:S(2)}, u32[]{:S(2)}) collective-permute-start(bf16[96,768]{1,0:T(8,128)(2,1)S(1)} %get-tuple-element.88), channel_id=1, source_target_pairs={{0,12},{1,13},{2,14},{3,15},{4,0},{5,1},{6,2},{7,3},{8,4},{9,5},{1... | collective-permute-start | bytes 442376 | tf_op jit(solution)/shard_map/ppermute | solution.py:133
  81.5 26.9 %collective-permute-start.5 = (bf16[512,768]{1,0:T(8,128)(2,1)S(1)}, bf16[512,768]{1,0:T(8,128)(2,1)S(1)}, u32[]{:S(2)}, u32[]{:S(2)}) collective-permute-start(bf16[512,768]{1,0:T(8,128)(2,1)S(1)} %copy-done.54), channel_id=1, source_target_pairs={{0,16},{16,0},{1,17},{17,1},{2,18},{18,2},{3,19},{19,3},{4,20},{20... | collective-permute-start | bytes 2359304 | tf_op jit(solution)/shard_map/ppermute | solution.py:133
  131.6 26.5 %collective-permute-start.25 = (bf16[4,96,768]{2,1,0:T(8,128)(2,1)S(1)}, bf16[4,96,768]{2,1,0:T(8,128)(2,1)S(1)}, u32[]{:S(2)}, u32[]{:S(2)}) collective-permute-start(bf16[4,96,768]{2,1,0:T(8,128)(2,1)S(1)} %bitcast_dynamic-update-slice_fusion), channel_id=1, source_target_pairs={{0,16},{16,0},{1,17},{17,1},{2,18},{18,2},{3,19},{19,3},{4,20},{20... | collective-permute-start | bytes 1769480 | tf_op jit(solution)/shard_map/ppermute | solution.py:133
  132.0 27.7 %collective-permute-start.24 = (bf16[4,24,3072]{2,1,0:T(8,128)(2,1)S(1)}, bf16[4,24,3072]{2,1,0:T(8,128)(2,1)S(1)}, u32[]{:S(2)}, u32[]{:S(2)}) collective-permute-start(bf16[4,24,3072]{2,1,0:T(8,128)(2,1)S(1)} %bitcast_dynamic-update-slice_fusion.4), channel_id=1, source_target_pairs={{0,2},{1,3},{2,0},{3,1},{4,6},{5,7},{6,4},{7,5},{8,10},{9,11},{10,... | collective-permute-start | bytes 1769480 | tf_op jit(solution)/shard_map/ppermute | solution.py:133
  135.0 25.8 %collective-permute-start.22 = (bf16[4,2,2,24,1536]{4,3,2,1,0:T(8,128)(2,1)S(1)}, bf16[4,2,2,24,1536]{4,3,2,1,0:T(8,128)(2,1)S(1)}, u32[]{:S(2)}, u32[]{:S(2)}) collective-permute-start(bf16[4,2,2,24,1536]{4,3,2,1,0:T(8,128)(2,1)S(1)} %copy.155), channel_id=1, source_target_pairs={{0,1},{1,0},{2,3},{3,2},{4,5},{5,4},{6,7},{7,6},{8,9},{9,8},{10,11... | collective-permute-start | bytes 3538952 | tf_op jit(solution)/shard_map/ppermute | solution.py:133
  135.0 25.0 %collective-permute-start.23 = (bf16[4,2,2,24,1536]{4,3,2,1,0:T(8,128)(2,1)S(1)}, bf16[4,2,2,24,1536]{4,3,2,1,0:T(8,128)(2,1)S(1)}, u32[]{:S(2)}, u32[]{:S(2)}) collective-permute-start(bf16[4,2,2,24,1536]{4,3,2,1,0:T(8,128)(2,1)S(1)} %pad_maximum_fusion.13), channel_id=1, source_target_pairs={{0,1},{1,0},{2,3},{3,2},{4,5},{5,4},{6,7},{7,6},{8,9},{9,8},{10,11... | collective-permute-start | bytes 3538952 | tf_op jit(solution)/shard_map/ppermute | solution.py:133
  383.4 37.9 %collective-permute-start.35 = (bf16[4,24,1536]{2,1,0:T(8,128)(2,1)}, bf16[4,24,1536]{2,1,0:T(8,128)(2,1)}, u32[]{:S(2)}, u32[]{:S(2)}) collective-permute-start(bf16[4,24,1536]{2,1,0:T(8,128)(2,1)} %dynamic-slice_bitcast_fusion.10), channel_id=1, source_target_pairs={{0,16},{16,0},{1,17},{17,1},{2,18},{18,2},{3,19},{19,3},{4,20},{20... | collective-permute-start | bytes 884744 | tf_op jit(solution)/shard_map/ppermute | solution.py:133
  384.5 38.0 %collective-permute-start.34 = (bf16[4,24,1536]{2,1,0:T(8,128)(2,1)}, bf16[4,24,1536]{2,1,0:T(8,128)(2,1)}, u32[]{:S(2)}, u32[]{:S(2)}) collective-permute-start(bf16[4,24,1536]{2,1,0:T(8,128)(2,1)} %dynamic-slice_bitcast_fusion.11), channel_id=1, source_target_pairs={{0,2},{1,3},{2,0},{3,1},{4,6},{5,7},{6,4},{7,5},{8,10},{9,11},{10,... | collective-permute-start | bytes 884744 | tf_op jit(solution)/shard_map/ppermute | solution.py:133
  389.7 34.7 %collective-permute-start.55 = (bf16[4,2,2,24,3072]{4,3,0,1,2:T(8,128)(2,1)}, bf16[4,2,2,24,3072]{4,3,0,1,2:T(8,128)(2,1)}, u32[]{:S(2)}, u32[]{:S(2)}) collective-permute-start(bf16[4,2,2,24,3072]{4,3,0,1,2:T(8,128)(2,1)} %bitcast.365), channel_id=1, source_target_pairs={{0,1},{1,0},{2,3},{3,2},{4,5},{5,4},{6,7},{7,6},{8,9},{9,8},{10,11... | collective-permute-start | bytes 7077896 | tf_op jit(solution)/shard_map/ppermute | solution.py:133
  396.7 33.9 %collective-permute-start.62 = (bf16[4,2,2,96,768]{4,3,0,2,1:T(8,128)(2,1)S(1)}, bf16[4,2,2,96,768]{4,3,0,2,1:T(8,128)(2,1)S(1)}, u32[]{:S(2)}, u32[]{:S(2)}) collective-permute-start(bf16[4,2,2,96,768]{4,3,0,2,1:T(8,128)(2,1)S(1)} %bitcast.411), channel_id=1, source_target_pairs={{0,1},{1,0},{2,3},{3,2},{4,5},{5,4},{6,7},{7,6},{8,9},{9,8},{10,11... | collective-permute-start | bytes 7077896 | tf_op jit(solution)/shard_map/ppermute | solution.py:133
  427.3 33.0 %collective-permute-start.56 = (bf16[4,2,24,3072]{3,2,0,1:T(8,128)(2,1)S(1)}, bf16[4,2,24,3072]{3,2,0,1:T(8,128)(2,1)S(1)}, u32[]{:S(2)}, u32[]{:S(2)}) collective-permute-start(bf16[4,2,24,3072]{3,2,0,1:T(8,128)(2,1)S(1)} %dynamic-slice_bitcast_fusion.1), channel_id=1, source_target_pairs={{0,16},{16,0},{1,17},{17,1},{2,18},{18,2},{3,19},{19,3},{4,20},{20... | collective-permute-start | bytes 3538952 | tf_op jit(solution)/shard_map/ppermute | solution.py:133
  432.7 37.6 %collective-permute-start.63 = (bf16[4,2,96,768]{3,2,0,1:T(8,128)(2,1)}, bf16[4,2,96,768]{3,2,0,1:T(8,128)(2,1)}, u32[]{:S(2)}, u32[]{:S(2)}) collective-permute-start(bf16[4,2,96,768]{3,2,0,1:T(8,128)(2,1)} %dynamic-slice_bitcast_fusion), channel_id=1, source_target_pairs={{0,2},{1,3},{2,0},{3,1},{4,6},{5,7},{6,4},{7,5},{8,10},{9,11},{10,... | collective-permute-start | bytes 3538952 | tf_op jit(solution)/shard_map/ppermute | solution.py:133
  485.8 28.4 %collective-permute-start.60 = (bf16[24,3072]{1,0:T(8,128)(2,1)}, bf16[24,3072]{1,0:T(8,128)(2,1)}, u32[]{:S(2)}, u32[]{:S(2)}) collective-permute-start(bf16[24,3072]{1,0:T(8,128)(2,1)} %get-tuple-element.243), channel_id=1, source_target_pairs={{0,12},{1,13},{2,14},{3,15},{4,0},{5,1},{6,2},{7,3},{8,4},{9,5},{1... | collective-permute-start | bytes 442376 | tf_op jit(solution)/shard_map/ppermute | solution.py:133
  489.8 25.3 %collective-permute-start.59 = (bf16[24,3072]{1,0:T(8,128)(2,1)}, bf16[24,3072]{1,0:T(8,128)(2,1)}, u32[]{:S(2)}, u32[]{:S(2)}) collective-permute-start(bf16[24,3072]{1,0:T(8,128)(2,1)} %get-tuple-element.244), channel_id=1, source_target_pairs={{0,8},{1,9},{2,10},{3,11},{4,12},{5,13},{6,14},{7,15},{8,0},{9,1},... | collective-permute-start | bytes 442376 | tf_op jit(solution)/shard_map/ppermute | solution.py:133
  494.6 34.7 %collective-permute-start.67 = (bf16[96,768]{1,0:T(8,128)(2,1)}, bf16[96,768]{1,0:T(8,128)(2,1)}, u32[]{:S(2)}, u32[]{:S(2)}) collective-permute-start(bf16[96,768]{1,0:T(8,128)(2,1)} %get-tuple-element.240), channel_id=1, source_target_pairs={{0,12},{1,13},{2,14},{3,15},{4,0},{5,1},{6,2},{7,3},{8,4},{9,5},{1... | collective-permute-start | bytes 442376 | tf_op jit(solution)/shard_map/ppermute | solution.py:133
  498.4 31.6 %collective-permute-start.66 = (bf16[96,768]{1,0:T(8,128)(2,1)}, bf16[96,768]{1,0:T(8,128)(2,1)}, u32[]{:S(2)}, u32[]{:S(2)}) collective-permute-start(bf16[96,768]{1,0:T(8,128)(2,1)} %get-tuple-element.241), channel_id=1, source_target_pairs={{0,8},{1,9},{2,10},{3,11},{4,12},{5,13},{6,14},{7,15},{8,0},{9,1},... | collective-permute-start | bytes 442376 | tf_op jit(solution)/shard_map/ppermute | solution.py:133
  516.4 28.7 %collective-permute-start.43 = (bf16[4,2,2,24,3072]{4,3,0,2,1:T(8,128)(2,1)}, bf16[4,2,2,24,3072]{4,3,0,2,1:T(8,128)(2,1)}, u32[]{:S(2)}, u32[]{:S(2)}) collective-permute-start(bf16[4,2,2,24,3072]{4,3,0,2,1:T(8,128)(2,1)} %bitcast.366), channel_id=1, source_target_pairs={{0,1},{1,0},{2,3},{3,2},{4,5},{5,4},{6,7},{7,6},{8,9},{9,8},{10,11... | collective-permute-start | bytes 7077896 | tf_op jit(solution)/shard_map/ppermute | solution.py:133
  525.9 64.7 %collective-permute-start.53 = (bf16[24,3072]{1,0:T(8,128)(2,1)}, bf16[24,3072]{1,0:T(8,128)(2,1)S(1)}, u32[]{:S(2)}, u32[]{:S(2)}) collective-permute-start(bf16[24,3072]{1,0:T(8,128)(2,1)} %get-tuple-element.246), channel_id=1, source_target_pairs={{0,12},{1,13},{2,14},{3,15},{4,0},{5,1},{6,2},{7,3},{8,4},{9,5},{1... | collective-permute-start | bytes 442376 | tf_op jit(solution)/shard_map/ppermute | solution.py:133
  534.4 57.0 %collective-permute-start.52 = (bf16[24,3072]{1,0:T(8,128)(2,1)}, bf16[24,3072]{1,0:T(8,128)(2,1)}, u32[]{:S(2)}, u32[]{:S(2)}) collective-permute-start(bf16[24,3072]{1,0:T(8,128)(2,1)} %get-tuple-element.247), channel_id=1, source_target_pairs={{0,8},{1,9},{2,10},{3,11},{4,12},{5,13},{6,14},{7,15},{8,0},{9,1},... | collective-permute-start | bytes 442376 | tf_op jit(solution)/shard_map/ppermute | solution.py:133
  536.2 57.4 %collective-permute-start.51 = (bf16[24,3072]{1,0:T(8,128)(2,1)}, bf16[24,3072]{1,0:T(8,128)(2,1)}, u32[]{:S(2)}, u32[]{:S(2)}) collective-permute-start(bf16[24,3072]{1,0:T(8,128)(2,1)} %get-tuple-element.245), channel_id=1, source_target_pairs={{0,4},{1,5},{2,6},{3,7},{4,8},{5,9},{6,10},{7,11},{8,12},{9,13},{1... | collective-permute-start | bytes 442376 | tf_op jit(solution)/shard_map/ppermute | solution.py:133
  543.3 47.3 %collective-permute-start.68 = (bf16[96,768]{1,0:T(8,128)(2,1)}, bf16[96,768]{1,0:T(8,128)(2,1)S(1)}, u32[]{:S(2)}, u32[]{:S(2)}) collective-permute-start(bf16[96,768]{1,0:T(8,128)(2,1)} %get-tuple-element.162), channel_id=1, source_target_pairs={{0,16},{16,0},{1,17},{17,1},{2,18},{18,2},{3,19},{19,3},{4,20},{20... | collective-permute-start | bytes 442376 | tf_op jit(solution)/shard_map/ppermute | solution.py:133
  (167 other events, 1501.7 us)
Sparse Core Ops, SparseCore 0:
  24.0 154.9 all-gather.1
  343.0 150.6 reduce-scatter.1

commit v4 on v3

--- a/solution.py
+++ b/solution.py
@@ -463,11 +463,14 @@
         first_part, up0 = main0[:, :cut], main0[:, cut:]
         first_part = spread_z(first_part)
         vectors = gather_vectors(packed)
-        first_part, up0, down0, traded = tie(first_part, up0, down0, traded)
         other = over_section(traded)
-        qk0 = third_stage(second_stage(first_part[..., : 2 * D], True), True)
-        vo0 = third_stage(second_stage(first_part[..., 2 * D :], False), False)
-        up0, down0 = spread_z(up0), spread_z(down0)
+        first_part, up0, down0, other = tie(first_part, up0, down0, other)
+        qk0 = second_stage(first_part[..., : 2 * D], True)
+        vo0 = second_stage(first_part[..., 2 * D :], False)
+        up0 = spread_z(up0)
+        qk0, vo0, up0, down0 = tie(qk0, vo0, up0, down0)
+        qk0, vo0 = third_stage(qk0, True), third_stage(vo0, False)
+        down0 = spread_z(down0)
         qk0, vo0, up0, down0 = tie(qk0, vo0, up0, down0)
         qk0, vo0 = core_stage(qk0), core_stage(vo0)
         up0, down0 = second_stage(up0, True), second_stage(down0, False)
@@ -503,8 +506,7 @@
     arrived_out = over_section(sent_out)
     mlp1 = backward_mlp(cotangent, before1, activated1, kept1[5], up1, down1)
     if direct:
-        total1 = mlp_packed(mlp1[0], mlp1[1])
-        mlp1, arrived_out, total1 = tie(mlp1, arrived_out, total1)
+        mlp1, arrived_out = tie(mlp1, arrived_out)
     up_grad1, down_grad1, grad_normed1, down_bias1, up_bias1 = mlp1
     back1 = backward_to_scores(
         cotangent, grad_normed1, kept1[4], kept1[3], kept1[1], kept1[2], vo1, vector1
@@ -525,26 +527,31 @@
         [ln1_gain1, ln1_bias1, out_bias1, ln2_gain1, ln2_bias1, down_bias1], qv_bias1, up_bias1, count
     )
     if direct:
-        up_sum1, down_sum1 = mlp_scattered(total1, 4 * D)
-        mid_low, part_grad1, small1 = tie(mid_low, part_grad1, small1)
+        up_sum1, down_sum1 = core_reduced(up_grad1), core_reduced(down_grad1)
+        mid_low, part_grad1, small1, up_sum1, down_sum1 = tie(
+            mid_low, part_grad1, small1, up_sum1, down_sum1
+        )
+        up_sum1, down_sum1 = wide_reduced(up_sum1, True), wide_reduced(down_sum1, False)
         part_sum1 = core_reduced(part_grad1)
-        qk_sum1 = wide_reduced(part_sum1[..., : 2 * D], True)
-        vo_sum1 = wide_reduced(part_sum1[..., 2 * D :], False)
     mid_float = mid_low.astype(FLOAT)
     mlp0 = backward_mlp(mid_float, before0, activated0, kept0[5], up0, down0)
     if direct:
-        mlp0, qk_sum1, vo_sum1, mid_float = tie(mlp0, qk_sum1, vo_sum1, mid_float)
+        total0 = mlp_packed(mlp0[0], mlp0[1])
+        mlp0, total0, up_sum1, down_sum1, part_sum1, mid_float = tie(
+            mlp0, total0, up_sum1, down_sum1, part_sum1, mid_float
+        )
+        up_sum0, down_sum0 = mlp_scattered(total0, 4 * D)
     up_grad0, down_grad0, grad_normed0, down_bias0, up_bias0 = mlp0
     back0 = backward_to_scores(
         mid_float, grad_normed0, kept0[4], kept0[3], kept0[1], kept0[2], vo0, vector0
     )
     if direct:
-        up_sum0, down_sum0 = core_reduced(up_grad0), core_reduced(down_grad0)
-        part_sum1 = jnp.concatenate(
-            [narrow_reduced(qk_sum1, True), narrow_reduced(vo_sum1, False)], axis=-1
+        up_sum1, down_sum1 = narrow_reduced(up_sum1, True), narrow_reduced(down_sum1, False)
+        qk_sum1 = wide_reduced(part_sum1[..., : 2 * D], True)
+        vo_sum1 = wide_reduced(part_sum1[..., 2 * D :], False)
+        back0, qk_sum1, vo_sum1, up_sum1, down_sum1 = tie(
+            back0, qk_sum1, vo_sum1, up_sum1, down_sum1
         )
-        up_sum0, down_sum0 = wide_reduced(up_sum0, True), wide_reduced(down_sum0, False)
-        back0, part_sum1 = tie(back0, part_sum1)
     residual0, out_grad0, grad_qk0, grad_v0, ln2_gain0, ln2_bias0, out_bias0 = back0
     part_grad0 = jnp.concatenate(
         [
@@ -555,11 +562,12 @@
         axis=1,
     )
     if direct:
-        part_grad0, up_sum1, down_sum1, part_sum1, residual0, grad_qk0, grad_v0 = tie(
-            part_grad0, up_sum1, down_sum1, part_sum1, residual0, grad_qk0, grad_v0
+        part_sum1 = jnp.concatenate(
+            [narrow_reduced(qk_sum1, True), narrow_reduced(vo_sum1, False)], axis=-1
         )
+        up_sum1, down_sum1 = reduce_z(up_sum1), reduce_z(down_sum1)
+        part_grad0, residual0, grad_qk0, grad_v0 = tie(part_grad0, residual0, grad_qk0, grad_v0)
         part_sum0 = core_reduced(part_grad0)
-        up_sum0, down_sum0 = narrow_reduced(up_sum0, True), narrow_reduced(down_sum0, False)
     in_low, ln1_gain0, ln1_bias0, qv_bias0 = backward_input(
         residual0, grad_qk0, grad_v0, hidden, qk0, vo0, vector0
     )
@@ -571,7 +579,6 @@
         part_sum1 = reduce_z(part_sum1)
         qk_sum0 = wide_reduced(part_sum0[..., : 2 * D], True)
         vo_sum0 = wide_reduced(part_sum0[..., 2 * D :], False)
-        up_sum0, down_sum0 = reduce_z(up_sum0), reduce_z(down_sum0)
         part_sum0 = jnp.concatenate(
             [narrow_reduced(qk_sum0, True), narrow_reduced(vo_sum0, False)], axis=-1
         )

time: 624 us -> 598 us (0.958)
  waiting for transfers between devices: 225 us -> 174 us
  starting transfers between devices: 80.2 us -> 100 us
  local copies, waits for them, and re-layouts: 72.1 us -> 81.4 us
    ppermute x69, waiting for transfers between devices: 225 us -> 174 us  [hop(): lax.ppermute(value, axis, [(source, target(source)) for source in range(c...]
    ppermute x69, starting transfers between devices: 80.1 us -> 100 us  [hop(): lax.ppermute(value, axis, [(source, target(source)) for source in range(c...]
    convert_element_type x16, other arithmetic: 15.3 us -> 23.9 us  [reduce_pair(): return (kept.astype(FLOAT) + exchange(sent).astype(FLOAT)).astype(LOW)]
    reduce_sum x1 -> x0, other arithmetic: 6.75 us -> none  [backward_mlp(): up_bias_grad = jnp.sum(grad_before, axis=0)]
    unnamed x257 -> x273, local copies, waits for them, and re-layouts: 22.6 us -> 23.2 us
  transfers between devices with their start and end apart: 71 -> 71, of which waited for: 32 -> 37; matrix products, arithmetic and copies ran while one was open for 24% -> 25% of each run, Pallas kernels for 4% -> 4%
where the time goes in v4:
time: 598 us; the launch traced here: 589 us
  waiting for transfers between devices  174 us (29%)
  starting transfers between devices  100 us (17%)
  other arithmetic  84.1 us (14%)
  local copies, waits for them, and re-layouts  81.4 us (14%)
  matrix products  81 us (14%)
  Pallas kernels  50.7 us (8%)
  between operations  17.1 us (3%)
    ppermute x69, waiting for transfers between devices, hop(): lax.ppermute(value, axis, [(source, target(source)) for source in range(c...  174 us
    ppermute x69, starting transfers between devices, hop(): lax.ppermute(value, axis, [(source, target(source)) for source in range(c...  100 us
    pallas_call x2, Pallas kernels, attention_backward(): pl.pallas_call(bwd_kernel, grid=(pairs,), in_specs=[first, second, first,...  35 us
    dot_general x10, matrix products, dot_nt(): lax.dot_general(a, b, (((1,), (1,)), ((), ())), preferred_element_type=FL...  31.6 us
    dot_general x10, matrix products, dot_tn(): lax.dot_general(a, b, (((0,), (0,)), ((), ())), preferred_element_type=FL...  24.3 us
    convert_element_type x16, other arithmetic, reduce_pair(): return (kept.astype(FLOAT) + exchange(sent).astype(FLOAT)).astype(LOW)  23.9 us
    unnamed x273, local copies, waits for them, and re-layouts  23.2 us
    pallas_call x2, Pallas kernels, attention_forward(): pl.pallas_call(fwd_kernel, grid=(pairs,), in_specs=[first, second, first]...  15.8 us
  transfers between devices with their start and end apart: 71, of which 37 were waited for; matrix products, arithmetic and copies ran while one was open for 25% of the time, Pallas kernels for 4%

profile of v4, /device:TPU:0, one launch (start us, length us, event | category | flops | bytes accessed | tf_op | source)
XLA Modules:
  0.0 589.0 jit_solution(7717724153698389359)
XLA Ops:
  14.2 7.6 %collective-permute-done.1 = bf16[96,768]{1,0:T(8,128)(2,1)S(1)} collective-permute-done((bf16[96,768]{1,0:T(8,128)(2,1)S(1)}, bf16[96,768]{1,0:T(8,128)(2,1)S(1)}, u32[]{:S(2)}, u32[]{:S(2)}) %collective-permute-start.1) | collective-permute-done | bytes 147488 | tf_op jit(solution)/shard_map/ppermute | solution.py:133
  73.2 8.4 %collective-permute-done.15 = bf16[24,3072]{1,0:T(8,128)(2,1)S(1)} collective-permute-done((bf16[24,3072]{1,0:T(8,128)(2,1)S(1)}, bf16[24,3072]{1,0:T(8,128)(2,1)S(1)}, u32[]{:S(2)}, u32[]{:S(2)}) %collective-permute-start.15) | collective-permute-done | bytes 147488 | tf_op jit(solution)/shard_map/ppermute | solution.py:133
  83.6 11.4 %collective-permute-start.19 = (bf16[96,768]{1,0:T(8,128)(2,1)S(1)}, bf16[96,768]{1,0:T(8,128)(2,1)S(1)}, u32[]{:S(2)}, u32[]{:S(2)}) collective-permute-start(bf16[96,768]{1,0:T(8,128)(2,1)S(1)} %get-tuple-element.99), channel_id=1, source_target_pairs={{0,4},{1,5},{2,6},{3,7},{4,8},{5,9},{6,10},{7,11},{8,12},{9,13},{1... | collective-permute-start | bytes 442376 | tf_op jit(solution)/shard_map/ppermute | solution.py:133
  106.0 16.5 %collective-permute-done.17 = bf16[4,2,24,1536]{3,2,0,1:T(8,128)(2,1)S(1)} collective-permute-done((bf16[4,2,24,1536]{3,2,0,1:T(8,128)(2,1)S(1)}, bf16[4,2,24,1536]{3,2,0,1:T(8,128)(2,1)S(1)}, u32[]{:S(2)}, u32[]{:S(2)}) %collective-permute-start.17) | collective-permute-done | bytes 589856 | tf_op jit(solution)/shard_map/ppermute | solution.py:133
  127.1 23.5 %collective-permute-done.25 = bf16[4,96,768]{2,1,0:T(8,128)(2,1)S(1)} collective-permute-done((bf16[4,96,768]{2,1,0:T(8,128)(2,1)S(1)}, bf16[4,96,768]{2,1,0:T(8,128)(2,1)S(1)}, u32[]{:S(2)}, u32[]{:S(2)}) %collective-permute-start.25) | collective-permute-done | bytes 589856 | tf_op jit(solution)/shard_map/ppermute | solution.py:133
  157.0 8.1 %attend_forward.2 = bf16[512,768]{1,0:T(8,128)(2,1)S(1)} custom-call(bf16[512,1536]{1,0:T(8,128)(2,1)S(1)} %fusion.29.q_ref.k_ref, bf16[512,1536]{1,0:T(8,128)(2,1)S(1)} %fusion.29.q_ref.k_ref, bf16[512,768]{1,0:T(8,128)(2,1)S(1)} %add_convert_fusion.7.v_ref), custom_call_target="tpu_custom_call" | custom-call | flops 201326592 | bytes 3145728 | tf_op jit(solution)/shard_map/attend_forward/pallas_call | solution.py:67
  168.0 7.5 %collective-permute-done.27 = bf16[4,2,96,768]{3,2,1,0:T(8,128)(2,1)S(1)} collective-permute-done((bf16[4,2,96,768]{3,2,1,0:T(8,128)(2,1)S(1)}, bf16[4,2,96,768]{3,2,1,0:T(8,128)(2,1)S(1)}, u32[]{:S(2)}, u32[]{:S(2)}) %collective-permute-start.27) | collective-permute-done | bytes 1179680 | tf_op jit(solution)/shard_map/ppermute | solution.py:133
  202.8 7.9 %slice.208 = bf16[3072,1536]{1,0:T(8,128)(2,1)} slice(bf16[3072,2304]{1,0:T(8,128)(2,1)} %all-gather.2.cloned.1.call-done), slice={[0:3072], [0:1536]} | slice | bytes 18874368 | tf_op jit(solution)/shard_map/slice | solution.py:410
  219.7 7.7 %attend_forward.3 = bf16[512,768]{1,0:T(8,128)(2,1)S(1)} custom-call(bf16[512,1536]{1,0:T(8,128)(2,1)S(1)} %fusion.30.q_ref.k_ref, bf16[512,1536]{1,0:T(8,128)(2,1)S(1)} %fusion.30.q_ref.k_ref, bf16[512,768]{1,0:T(8,128)(2,1)S(1)} %add_convert_fusion.4.v_ref), custom_call_target="tpu_custom_call" | custom-call | flops 201326592 | bytes 3145728 | tf_op jit(solution)/shard_map/attend_forward/pallas_call | solution.py:67
  228.7 6.5 %fusion.19 = (bf16[512,3072]{1,0:T(8,128)(2,1)S(1)}, f32[512,3072]{1,0:T(8,128)}) fusion(f32[3072]{0:T(1024)S(1)} %reshape.644, bf16[768,1536]{1,0:T(8,128)(2,1)S(1)} %bitcast.417, bf16[768,1536]{1,0:T(8,128)(2,1)S(1)} %bitcast.415, f32[512,768]{1,0:T(8,128)S(1)} %get-tuple-element.196, f32[768]{0:T(1024)S(1)} %reshape.643, f32[768]{0:T(1024)S(1)} %reshape.642, ...), kind=kOutput, calls=%fused_computation.25 | convolution fusion | flops 2443051008 | bytes 15751168 | tf_op jit(solution)/shard_map/dot_general | solution.py:318
  239.1 8.0 %fusion.157 = (f32[3072]{0:T(1024)S(1)}, bf16[512,3072]{1,0:T(8,128)(2,1)S(1)}) fusion(f32[512,3072]{1,0:T(8,128)} %get-tuple-element.117, bf16[3072,2304]{1,0:T(8,128)(2,1)S(1)} %bitcast.395, f32[512,768]{1,0:T(8,128)S(1)} %copy-done.20), kind=kOutput, calls=%fused_computation.433 | convolution fusion | flops 2449339392 | bytes 15740928 | tf_op jit(solution)/shard_map/dot_general | solution.py:22
  260.1 6.1 %fusion.28 = f32[512,768]{1,0:T(8,128)S(1)} fusion(bf16[768,1536]{1,0:T(8,128)(2,1)} %bitcast.418, bf16[768,1536]{1,0:T(8,128)(2,1)} %bitcast.416, bf16[512,3072]{1,0:T(8,128)(2,1)} %copy-done.111), kind=kOutput, calls=%fused_computation.53 | convolution fusion | flops 2425356288 | bytes 9437184 | tf_op jit(solution)/shard_map/dot_general | solution.py:22
  266.1 6.2 %collective-permute-done.30 = bf16[512,768]{1,0:T(8,128)(2,1)} collective-permute-done((bf16[512,768]{1,0:T(8,128)(2,1)}, bf16[512,768]{1,0:T(8,128)(2,1)}, u32[]{:S(2)}, u32[]{:S(2)}) %collective-permute-start.30) | collective-permute-done | bytes 786464 | tf_op jit(solution)/shard_map/ppermute | solution.py:133
  277.5 17.7 %attend_backward.2 = (bf16[512,1536]{1,0:T(8,128)(2,1)S(1)}, bf16[512,768]{1,0:T(8,128)(2,1)S(1)}) custom-call(bf16[512,1536]{1,0:T(8,128)(2,1)S(1)} %fusion.30.q_ref.k_ref, bf16[512,1536]{1,0:T(8,128)(2,1)S(1)} %fusion.30.q_ref.k_ref, bf16[512,768]{1,0:T(8,128)(2,1)S(1)} %add_convert_fusion.4.v_ref, bf16[512,768]{1,0:T(8,128)(2,1)S(1)} %convolution_convert_fusion.11.g_ref), custom_call_target="tpu_custom_call" | custom-call | flops 201326592 | bytes 5505024 | tf_op jit(solution)/shard_map/attend_backward/pallas_call | solution.py:113
  325.5 5.6 convolution_convert_fusion
  331.0 6.7 %fusion.142 = (f32[3072]{0:T(1024)S(1)}, bf16[512,3072]{1,0:T(8,128)(2,1)S(1)}) fusion(f32[512,3072]{1,0:T(8,128)S(1)} %bitcast.393, f32[3072]{0:T(1024)S(1)} %reshape.637, bf16[512,768]{1,0:T(8,128)(2,1)S(1)} %add_convert_fusion.1, bf16[3072,768]{1,0:T(8,128)(2,1)S(1)} %bitcast.399), kind=kOutput, calls=%fused_computation.421 | convolution fusion | flops 2450519040 | bytes 14966784 | tf_op jit(solution)/shard_map/dot_general | solution.py:22
  360.1 16.2 %collective-permute-done.34 = bf16[4,2,96,768]{3,2,0,1:T(8,128)(2,1)} collective-permute-done((bf16[4,2,96,768]{3,2,0,1:T(8,128)(2,1)}, bf16[4,2,96,768]{3,2,0,1:T(8,128)(2,1)}, u32[]{:S(2)}, u32[]{:S(2)}) %collective-permute-start.34) | collective-permute-done | bytes 1179680 | tf_op jit(solution)/shard_map/ppermute | solution.py:133
  398.2 17.3 %attend_backward.3 = (bf16[512,1536]{1,0:T(8,128)(2,1)S(1)}, bf16[512,768]{1,0:T(8,128)(2,1)S(1)}) custom-call(bf16[512,1536]{1,0:T(8,128)(2,1)S(1)} %copy-done.1, bf16[512,1536]{1,0:T(8,128)(2,1)S(1)} %copy-done.1, bf16[512,768]{1,0:T(8,128)(2,1)S(1)} %copy-done.3, bf16[512,768]{1,0:T(8,128)(2,1)S(1)} %convolution_convert_fusion.10.g_ref), custom_call_target="tpu_custom_call" | custom-call | flops 201326592 | bytes 5505024 | tf_op jit(solution)/shard_map/attend_backward/pallas_call | solution.py:113
  473.6 11.9 %collective-permute-done.55 = bf16[4,24,1536]{2,1,0:T(8,128)(2,1)S(1)} collective-permute-done((bf16[4,24,1536]{2,1,0:T(8,128)(2,1)S(1)}, bf16[4,24,1536]{2,1,0:T(8,128)(2,1)S(1)}, u32[]{:S(2)}, u32[]{:S(2)}) %collective-permute-start.55) | collective-permute-done | bytes 294944 | tf_op jit(solution)/shard_map/ppermute | solution.py:133
  494.9 7.7 %collective-permute-done.50 = bf16[4,2,24,1536]{3,2,0,1:T(8,128)(2,1)S(1)} collective-permute-done((bf16[4,2,24,1536]{3,2,0,1:T(8,128)(2,1)S(1)}, bf16[4,2,24,1536]{3,2,0,1:T(8,128)(2,1)S(1)}, u32[]{:S(2)}, u32[]{:S(2)}) %collective-permute-start.50) | collective-permute-done | bytes 589856 | tf_op jit(solution)/shard_map/ppermute | solution.py:133
  502.9 15.1 %collective-permute-done.48 = bf16[4,2,24,1536]{3,2,0,1:T(8,128)(2,1)S(1)} collective-permute-done((bf16[4,2,24,1536]{3,2,0,1:T(8,128)(2,1)S(1)}, bf16[4,2,24,1536]{3,2,0,1:T(8,128)(2,1)S(1)}, u32[]{:S(2)}, u32[]{:S(2)}) %collective-permute-start.48) | collective-permute-done | bytes 589856 | tf_op jit(solution)/shard_map/ppermute | solution.py:133
  518.4 6.3 %collective-permute-done.51 = bf16[4,24,1536]{2,1,0:T(8,128)(2,1)S(1)} collective-permute-done((bf16[4,24,1536]{2,1,0:T(8,128)(2,1)S(1)}, bf16[4,24,1536]{2,1,0:T(8,128)(2,1)S(1)}, u32[]{:S(2)}, u32[]{:S(2)}) %collective-permute-start.51) | collective-permute-done | bytes 294944 | tf_op jit(solution)/shard_map/ppermute | solution.py:133
  526.5 5.9 %collective-permute-done.49 = bf16[4,24,1536]{2,1,0:T(8,128)(2,1)S(1)} collective-permute-done((bf16[4,24,1536]{2,1,0:T(8,128)(2,1)S(1)}, bf16[4,24,1536]{2,1,0:T(8,128)(2,1)S(1)}, u32[]{:S(2)}, u32[]{:S(2)}) %collective-permute-start.49) | collective-permute-done | bytes 294944 | tf_op jit(solution)/shard_map/ppermute | solution.py:133
  542.2 7.0 %collective-permute-start.66 = (bf16[96,768]{1,0:T(8,128)(2,1)}, bf16[96,768]{1,0:T(8,128)(2,1)}, u32[]{:S(2)}, u32[]{:S(2)}) collective-permute-start(bf16[96,768]{1,0:T(8,128)(2,1)} %get-tuple-element.253), channel_id=1, source_target_pairs={{0,8},{1,9},{2,10},{3,11},{4,12},{5,13},{6,14},{7,15},{8,0},{9,1},... | collective-permute-start | bytes 442376 | tf_op jit(solution)/shard_map/ppermute | solution.py:133
  (687 shorter events, 329.1 us)
Async XLA Ops:
  7.2 195.0 %all-gather.2.cloned.1.call-start = ((), (), s32[]{:S(2)}) async-start(), calls=%async_computation.1 | async-start | bytes 14598144 | tf_op jit(solution)/shard_map/all_gather | solution.py:405
  23.8 542.9 %reduce-scatter.2.cloned.1.call-start = ((), (), s32[]{:S(2)}) async-start(), calls=%async_computation.2 | async-start | bytes 9732096 | tf_op jit(solution)/shard_map/reduce_scatter | solution.py:424
  97.5 25.4 %collective-permute-start.18 = (bf16[4,2,24,1536]{3,2,1,0:T(8,128)(2,1)S(1)}, bf16[4,2,24,1536]{3,2,1,0:T(8,128)(2,1)S(1)}, u32[]{:S(2)}, u32[]{:S(2)}) collective-permute-start(bf16[4,2,24,1536]{3,2,1,0:T(8,128)(2,1)S(1)} %pad_maximum_fusion.18), channel_id=1, source_target_pairs={{0,2},{1,3},{2,0},{3,1},{4,6},{5,7},{6,4},{7,5},{8,10},{9,11},{10,... | collective-permute-start | bytes 1769480 | tf_op jit(solution)/shard_map/ppermute | solution.py:133
  99.0 23.5 %collective-permute-start.17 = (bf16[4,2,24,1536]{3,2,0,1:T(8,128)(2,1)S(1)}, bf16[4,2,24,1536]{3,2,0,1:T(8,128)(2,1)S(1)}, u32[]{:S(2)}, u32[]{:S(2)}) collective-permute-start(bf16[4,2,24,1536]{3,2,0,1:T(8,128)(2,1)S(1)} %pad_maximum_fusion.17), channel_id=1, source_target_pairs={{0,16},{16,0},{1,17},{17,1},{2,18},{18,2},{3,19},{19,3},{4,20},{20... | collective-permute-start | bytes 1769480 | tf_op jit(solution)/shard_map/ppermute | solution.py:133
  123.1 27.5 %collective-permute-start.25 = (bf16[4,96,768]{2,1,0:T(8,128)(2,1)S(1)}, bf16[4,96,768]{2,1,0:T(8,128)(2,1)S(1)}, u32[]{:S(2)}, u32[]{:S(2)}) collective-permute-start(bf16[4,96,768]{2,1,0:T(8,128)(2,1)S(1)} %bitcast_dynamic-update-slice_fusion), channel_id=1, source_target_pairs={{0,16},{16,0},{1,17},{17,1},{2,18},{18,2},{3,19},{19,3},{4,20},{20... | collective-permute-start | bytes 1769480 | tf_op jit(solution)/shard_map/ppermute | solution.py:133
  126.0 25.5 %collective-permute-start.24 = (bf16[4,24,3072]{2,1,0:T(8,128)(2,1)S(1)}, bf16[4,24,3072]{2,1,0:T(8,128)(2,1)S(1)}, u32[]{:S(2)}, u32[]{:S(2)}) collective-permute-start(bf16[4,24,3072]{2,1,0:T(8,128)(2,1)S(1)} %bitcast_dynamic-update-slice_fusion.4), channel_id=1, source_target_pairs={{0,2},{1,3},{2,0},{3,1},{4,6},{5,7},{6,4},{7,5},{8,10},{9,11},{10,... | collective-permute-start | bytes 1769480 | tf_op jit(solution)/shard_map/ppermute | solution.py:133
  126.5 25.3 %collective-permute-start.23 = (bf16[4,2,2,24,1536]{4,3,2,1,0:T(8,128)(2,1)S(1)}, bf16[4,2,2,24,1536]{4,3,2,1,0:T(8,128)(2,1)S(1)}, u32[]{:S(2)}, u32[]{:S(2)}) collective-permute-start(bf16[4,2,2,24,1536]{4,3,2,1,0:T(8,128)(2,1)S(1)} %pad_maximum_fusion.13), channel_id=1, source_target_pairs={{0,1},{1,0},{2,3},{3,2},{4,5},{5,4},{6,7},{7,6},{8,9},{9,8},{10,11... | collective-permute-start | bytes 3538952 | tf_op jit(solution)/shard_map/ppermute | solution.py:133
  126.6 25.9 %collective-permute-start.22 = (bf16[4,2,2,24,1536]{4,3,2,1,0:T(8,128)(2,1)S(1)}, bf16[4,2,2,24,1536]{4,3,2,1,0:T(8,128)(2,1)S(1)}, u32[]{:S(2)}, u32[]{:S(2)}) collective-permute-start(bf16[4,2,2,24,1536]{4,3,2,1,0:T(8,128)(2,1)S(1)} %copy.159), channel_id=1, source_target_pairs={{0,1},{1,0},{2,3},{3,2},{4,5},{5,4},{6,7},{7,6},{8,9},{9,8},{10,11... | collective-permute-start | bytes 3538952 | tf_op jit(solution)/shard_map/ppermute | solution.py:133
  154.5 23.0 %collective-permute-start.26 = (bf16[4,2,24,3072]{3,2,0,1:T(8,128)(2,1)S(1)}, bf16[4,2,24,3072]{3,2,0,1:T(8,128)(2,1)S(1)}, u32[]{:S(2)}, u32[]{:S(2)}) collective-permute-start(bf16[4,2,24,3072]{3,2,0,1:T(8,128)(2,1)S(1)} %pad_maximum_fusion.14), channel_id=1, source_target_pairs={{0,16},{16,0},{1,17},{17,1},{2,18},{18,2},{3,19},{19,3},{4,20},{20... | collective-permute-start | bytes 3538952 | tf_op jit(solution)/shard_map/ppermute | solution.py:133
  346.5 34.0 %collective-permute-start.35 = (bf16[4,2,2,24,3072]{4,3,0,2,1:T(8,128)(2,1)}, bf16[4,2,2,24,3072]{4,3,0,2,1:T(8,128)(2,1)}, u32[]{:S(2)}, u32[]{:S(2)}) collective-permute-start(bf16[4,2,2,24,3072]{4,3,0,2,1:T(8,128)(2,1)} %bitcast.375), channel_id=1, source_target_pairs={{0,1},{1,0},{2,3},{3,2},{4,5},{5,4},{6,7},{7,6},{8,9},{9,8},{10,11... | collective-permute-start | bytes 7077896 | tf_op jit(solution)/shard_map/ppermute | solution.py:133
  347.7 28.7 %collective-permute-start.34 = (bf16[4,2,96,768]{3,2,0,1:T(8,128)(2,1)}, bf16[4,2,96,768]{3,2,0,1:T(8,128)(2,1)}, u32[]{:S(2)}, u32[]{:S(2)}) collective-permute-start(bf16[4,2,96,768]{3,2,0,1:T(8,128)(2,1)} %dynamic-slice_bitcast_fusion), channel_id=1, source_target_pairs={{0,2},{1,3},{2,0},{3,1},{4,6},{5,7},{6,4},{7,5},{8,10},{9,11},{10,... | collective-permute-start | bytes 3538952 | tf_op jit(solution)/shard_map/ppermute | solution.py:133
  350.6 28.2 %collective-permute-start.33 = (bf16[4,2,24,3072]{3,2,0,1:T(8,128)(2,1)S(1)}, bf16[4,2,24,3072]{3,2,0,1:T(8,128)(2,1)}, u32[]{:S(2)}, u32[]{:S(2)}) collective-permute-start(bf16[4,2,24,3072]{3,2,0,1:T(8,128)(2,1)S(1)} %dynamic-slice_bitcast_fusion.1), channel_id=1, source_target_pairs={{0,16},{16,0},{1,17},{17,1},{2,18},{18,2},{3,19},{19,3},{4,20},{20... | collective-permute-start | bytes 3538952 | tf_op jit(solution)/shard_map/ppermute | solution.py:133
  384.4 34.8 %collective-permute-start.39 = (bf16[4,96,768]{2,1,0:T(8,128)(2,1)}, bf16[4,96,768]{2,1,0:T(8,128)(2,1)}, u32[]{:S(2)}, u32[]{:S(2)}) collective-permute-start(bf16[4,96,768]{2,1,0:T(8,128)(2,1)} %dynamic-slice_bitcast_fusion.4), channel_id=1, source_target_pairs={{0,16},{16,0},{1,17},{17,1},{2,18},{18,2},{3,19},{19,3},{4,20},{20... | collective-permute-start | bytes 1769480 | tf_op jit(solution)/shard_map/ppermute | solution.py:133
  387.0 29.4 %collective-permute-start.38 = (bf16[4,24,3072]{2,1,0:T(8,128)(2,1)}, bf16[4,24,3072]{2,1,0:T(8,128)(2,1)}, u32[]{:S(2)}, u32[]{:S(2)}) collective-permute-start(bf16[4,24,3072]{2,1,0:T(8,128)(2,1)} %dynamic-slice_bitcast_fusion.5), channel_id=1, source_target_pairs={{0,2},{1,3},{2,0},{3,1},{4,6},{5,7},{6,4},{7,5},{8,10},{9,11},{10,... | collective-permute-start | bytes 1769480 | tf_op jit(solution)/shard_map/ppermute | solution.py:133
  389.7 31.7 %collective-permute-start.37 = (bf16[4,2,24,1536]{3,2,0,1:T(8,128)(2,1)}, bf16[4,2,24,1536]{3,2,0,1:T(8,128)(2,1)}, u32[]{:S(2)}, u32[]{:S(2)}) collective-permute-start(bf16[4,2,24,1536]{3,2,0,1:T(8,128)(2,1)} %dynamic-slice_bitcast_fusion.6), channel_id=1, source_target_pairs={{0,2},{1,3},{2,0},{3,1},{4,6},{5,7},{6,4},{7,5},{8,10},{9,11},{10,... | collective-permute-start | bytes 1769480 | tf_op jit(solution)/shard_map/ppermute | solution.py:133
  391.0 31.6 %collective-permute-start.36 = (bf16[4,2,24,1536]{3,2,0,1:T(8,128)(2,1)}, bf16[4,2,24,1536]{3,2,0,1:T(8,128)(2,1)}, u32[]{:S(2)}, u32[]{:S(2)}) collective-permute-start(bf16[4,2,24,1536]{3,2,0,1:T(8,128)(2,1)} %dynamic-slice_bitcast_fusion.7), channel_id=1, source_target_pairs={{0,16},{16,0},{1,17},{17,1},{2,18},{18,2},{3,19},{19,3},{4,20},{20... | collective-permute-start | bytes 1769480 | tf_op jit(solution)/shard_map/ppermute | solution.py:133
  425.7 47.8 %collective-permute-start.56 = (bf16[4,24,1536]{2,1,0:T(8,128)(2,1)}, bf16[4,24,1536]{2,1,0:T(8,128)(2,1)S(1)}, u32[]{:S(2)}, u32[]{:S(2)}) collective-permute-start(bf16[4,24,1536]{2,1,0:T(8,128)(2,1)} %dynamic-slice_bitcast_fusion.8), channel_id=1, source_target_pairs={{0,16},{16,0},{1,17},{17,1},{2,18},{18,2},{3,19},{19,3},{4,20},{20... | collective-permute-start | bytes 884744 | tf_op jit(solution)/shard_map/ppermute | solution.py:133
  433.7 51.9 %collective-permute-start.47 = (bf16[4,2,2,24,3072]{4,3,0,2,1:T(8,128)(2,1)}, bf16[4,2,2,24,3072]{4,3,0,2,1:T(8,128)(2,1)}, u32[]{:S(2)}, u32[]{:S(2)}) collective-permute-start(bf16[4,2,2,24,3072]{4,3,0,2,1:T(8,128)(2,1)} %bitcast.374), channel_id=1, source_target_pairs={{0,1},{1,0},{2,3},{3,2},{4,5},{5,4},{6,7},{7,6},{8,9},{9,8},{10,11... | collective-permute-start | bytes 7077896 | tf_op jit(solution)/shard_map/ppermute | solution.py:133
  472.8 87.1 %collective-permute-start.40 = (bf16[512,768]{1,0:T(8,128)(2,1)}, bf16[512,768]{1,0:T(8,128)(2,1)}, u32[]{:S(2)}, u32[]{:S(2)}) collective-permute-start(bf16[512,768]{1,0:T(8,128)(2,1)} %broadcast_select_fusion), channel_id=1, source_target_pairs={{0,16},{16,0},{1,17},{17,1},{2,18},{18,2},{3,19},{19,3},{4,20},{20... | collective-permute-start | bytes 2359304 | tf_op jit(solution)/shard_map/ppermute | solution.py:133
  490.3 44.0 %collective-permute-start.57 = (bf16[24,3072]{1,0:T(8,128)(2,1)S(1)}, bf16[24,3072]{1,0:T(8,128)(2,1)S(1)}, u32[]{:S(2)}, u32[]{:S(2)}) collective-permute-start(bf16[24,3072]{1,0:T(8,128)(2,1)S(1)} %get-tuple-element.257), channel_id=1, source_target_pairs={{0,4},{1,5},{2,6},{3,7},{4,8},{5,9},{6,10},{7,11},{8,12},{9,13},{1... | collective-permute-start | bytes 442376 | tf_op jit(solution)/shard_map/ppermute | solution.py:133
  491.2 45.6 %collective-permute-start.58 = (bf16[24,3072]{1,0:T(8,128)(2,1)S(1)}, bf16[24,3072]{1,0:T(8,128)(2,1)S(1)}, u32[]{:S(2)}, u32[]{:S(2)}) collective-permute-start(bf16[24,3072]{1,0:T(8,128)(2,1)S(1)} %get-tuple-element.258), channel_id=1, source_target_pairs={{0,8},{1,9},{2,10},{3,11},{4,12},{5,13},{6,14},{7,15},{8,0},{9,1},... | collective-permute-start | bytes 442376 | tf_op jit(solution)/shard_map/ppermute | solution.py:133
  493.0 46.9 %collective-permute-start.59 = (bf16[24,3072]{1,0:T(8,128)(2,1)S(1)}, bf16[24,3072]{1,0:T(8,128)(2,1)S(1)}, u32[]{:S(2)}, u32[]{:S(2)}) collective-permute-start(bf16[24,3072]{1,0:T(8,128)(2,1)S(1)} %get-tuple-element.259), channel_id=1, source_target_pairs={{0,12},{1,13},{2,14},{3,15},{4,0},{5,1},{6,2},{7,3},{8,4},{9,5},{1... | collective-permute-start | bytes 442376 | tf_op jit(solution)/shard_map/ppermute | solution.py:133
  540.0 27.9 %collective-permute-start.65 = (bf16[96,768]{1,0:T(8,128)(2,1)}, bf16[96,768]{1,0:T(8,128)(2,1)S(1)}, u32[]{:S(2)}, u32[]{:S(2)}) collective-permute-start(bf16[96,768]{1,0:T(8,128)(2,1)} %get-tuple-element.251), channel_id=1, source_target_pairs={{0,4},{1,5},{2,6},{3,7},{4,8},{5,9},{6,10},{7,11},{8,12},{9,13},{1... | collective-permute-start | bytes 442376 | tf_op jit(solution)/shard_map/ppermute | solution.py:133
  542.2 28.1 %collective-permute-start.66 = (bf16[96,768]{1,0:T(8,128)(2,1)}, bf16[96,768]{1,0:T(8,128)(2,1)}, u32[]{:S(2)}, u32[]{:S(2)}) collective-permute-start(bf16[96,768]{1,0:T(8,128)(2,1)} %get-tuple-element.253), channel_id=1, source_target_pairs={{0,8},{1,9},{2,10},{3,11},{4,12},{5,13},{6,14},{7,15},{8,0},{9,1},... | collective-permute-start | bytes 442376 | tf_op jit(solution)/shard_map/ppermute | solution.py:133
  (175 other events, 1607.6 us)
Sparse Core Ops, SparseCore 0:
  23.9 148.1 all-gather.1
  393.7 149.8 reduce-scatter.1

commit v5 on v4

--- a/solution.py
+++ b/solution.py
@@ -506,7 +506,7 @@
     arrived_out = over_section(sent_out)
     mlp1 = backward_mlp(cotangent, before1, activated1, kept1[5], up1, down1)
     if direct:
-        mlp1, arrived_out = tie(mlp1, arrived_out)
+        mlp1 = tie(*mlp1)
     up_grad1, down_grad1, grad_normed1, down_bias1, up_bias1 = mlp1
     back1 = backward_to_scores(
         cotangent, grad_normed1, kept1[4], kept1[3], kept1[1], kept1[2], vo1, vector1
@@ -528,8 +528,8 @@
     )
     if direct:
         up_sum1, down_sum1 = core_reduced(up_grad1), core_reduced(down_grad1)
-        mid_low, part_grad1, small1, up_sum1, down_sum1 = tie(
-            mid_low, part_grad1, small1, up_sum1, down_sum1
+        mid_low, part_grad1, small1, up_sum1, down_sum1, arrived_out = tie(
+            mid_low, part_grad1, small1, up_sum1, down_sum1, arrived_out
         )
         up_sum1, down_sum1 = wide_reduced(up_sum1, True), wide_reduced(down_sum1, False)
         part_sum1 = core_reduced(part_grad1)
@@ -537,9 +537,7 @@
     mlp0 = backward_mlp(mid_float, before0, activated0, kept0[5], up0, down0)
     if direct:
         total0 = mlp_packed(mlp0[0], mlp0[1])
-        mlp0, total0, up_sum1, down_sum1, part_sum1, mid_float = tie(
-            mlp0, total0, up_sum1, down_sum1, part_sum1, mid_float
-        )
+        mlp0, total0, part_sum1, mid_float = tie(mlp0, total0, part_sum1, mid_float)
         up_sum0, down_sum0 = mlp_scattered(total0, 4 * D)
     up_grad0, down_grad0, grad_normed0, down_bias0, up_bias0 = mlp0
     back0 = backward_to_scores(

time: 598 us -> 589 us (0.985)
  local copies, waits for them, and re-layouts: 81.4 us -> 72.9 us
  waiting for transfers between devices: 174 us -> 181 us
  other arithmetic: 84.1 us -> 77.2 us
    reshape x12, local copies, waits for them, and re-layouts: 7.86 us -> 0.91 us  [pack_vectors(): parts = [item.reshape(count, 1, -1) for item in singles]]
    ppermute x69, waiting for transfers between devices: 174 us -> 181 us  [hop(): lax.ppermute(value, axis, [(source, target(source)) for source in range(c...]
    unnamed x273 -> x275, local copies, waits for them, and re-layouts: 23.2 us -> 24.3 us
  transfers between devices with their start and end apart: 71 -> 71, of which waited for: 37 -> 36; matrix products, arithmetic and copies ran while one was open for 25% -> 22% of each run, Pallas kernels for 4% -> 4%
where the time goes in v5:
time: 589 us; the launch traced here: 581 us
  waiting for transfers between devices  181 us (31%)
  starting transfers between devices  100 us (17%)
  matrix products  81.7 us (14%)
  other arithmetic  77.2 us (13%)
  local copies, waits for them, and re-layouts  72.9 us (12%)
  Pallas kernels  51 us (9%)
  between operations  17.3 us (3%)
    ppermute x69, waiting for transfers between devices, hop(): lax.ppermute(value, axis, [(source, target(source)) for source in range(c...  181 us
    ppermute x69, starting transfers between devices, hop(): lax.ppermute(value, axis, [(source, target(source)) for source in range(c...  99.9 us
    pallas_call x2, Pallas kernels, attention_backward(): pl.pallas_call(bwd_kernel, grid=(pairs,), in_specs=[first, second, first,...  35.2 us
    dot_general x10, matrix products, dot_nt(): lax.dot_general(a, b, (((1,), (1,)), ((), ())), preferred_element_type=FL...  31.1 us
    dot_general x10, matrix products, dot_tn(): lax.dot_general(a, b, (((0,), (0,)), ((), ())), preferred_element_type=FL...  26 us
    unnamed x275, local copies, waits for them, and re-layouts  24.3 us
    convert_element_type x16, other arithmetic, reduce_pair(): return (kept.astype(FLOAT) + exchange(sent).astype(FLOAT)).astype(LOW)  22.4 us
    pallas_call x2, Pallas kernels, attention_forward(): pl.pallas_call(fwd_kernel, grid=(pairs,), in_specs=[first, second, first]...  15.8 us
  transfers between devices with their start and end apart: 71, of which 36 were waited for; matrix products, arithmetic and copies ran while one was open for 22% of the time, Pallas kernels for 4%

profile of v5, /device:TPU:0, one launch (start us, length us, event | category | flops | bytes accessed | tf_op | source)
XLA Modules:
  0.0 581.2 jit_solution(85518808961382460)
XLA Ops:
  14.2 7.6 %collective-permute-done.1 = bf16[96,768]{1,0:T(8,128)(2,1)S(1)} collective-permute-done((bf16[96,768]{1,0:T(8,128)(2,1)S(1)}, bf16[96,768]{1,0:T(8,128)(2,1)S(1)}, u32[]{:S(2)}, u32[]{:S(2)}) %collective-permute-start.1) | collective-permute-done | bytes 147488 | tf_op jit(solution)/shard_map/ppermute | solution.py:133
  73.2 8.4 %collective-permute-done.15 = bf16[24,3072]{1,0:T(8,128)(2,1)S(1)} collective-permute-done((bf16[24,3072]{1,0:T(8,128)(2,1)S(1)}, bf16[24,3072]{1,0:T(8,128)(2,1)S(1)}, u32[]{:S(2)}, u32[]{:S(2)}) %collective-permute-start.15) | collective-permute-done | bytes 147488 | tf_op jit(solution)/shard_map/ppermute | solution.py:133
  83.6 11.4 %collective-permute-start.19 = (bf16[96,768]{1,0:T(8,128)(2,1)S(1)}, bf16[96,768]{1,0:T(8,128)(2,1)S(1)}, u32[]{:S(2)}, u32[]{:S(2)}) collective-permute-start(bf16[96,768]{1,0:T(8,128)(2,1)S(1)} %get-tuple-element.97), channel_id=1, source_target_pairs={{0,4},{1,5},{2,6},{3,7},{4,8},{5,9},{6,10},{7,11},{8,12},{9,13},{1... | collective-permute-start | bytes 442376 | tf_op jit(solution)/shard_map/ppermute | solution.py:133
  106.0 16.5 %collective-permute-done.17 = bf16[4,2,24,1536]{3,2,0,1:T(8,128)(2,1)S(1)} collective-permute-done((bf16[4,2,24,1536]{3,2,0,1:T(8,128)(2,1)S(1)}, bf16[4,2,24,1536]{3,2,0,1:T(8,128)(2,1)S(1)}, u32[]{:S(2)}, u32[]{:S(2)}) %collective-permute-start.17) | collective-permute-done | bytes 589856 | tf_op jit(solution)/shard_map/ppermute | solution.py:133
  127.1 23.5 %collective-permute-done.25 = bf16[4,96,768]{2,1,0:T(8,128)(2,1)S(1)} collective-permute-done((bf16[4,96,768]{2,1,0:T(8,128)(2,1)S(1)}, bf16[4,96,768]{2,1,0:T(8,128)(2,1)S(1)}, u32[]{:S(2)}, u32[]{:S(2)}) %collective-permute-start.25) | collective-permute-done | bytes 589856 | tf_op jit(solution)/shard_map/ppermute | solution.py:133
  157.0 8.1 %attend_forward.2 = bf16[512,768]{1,0:T(8,128)(2,1)S(1)} custom-call(bf16[512,1536]{1,0:T(8,128)(2,1)S(1)} %fusion.29.q_ref.k_ref, bf16[512,1536]{1,0:T(8,128)(2,1)S(1)} %fusion.29.q_ref.k_ref, bf16[512,768]{1,0:T(8,128)(2,1)S(1)} %add_convert_fusion.7.v_ref), custom_call_target="tpu_custom_call" | custom-call | flops 201326592 | bytes 3145728 | tf_op jit(solution)/shard_map/attend_forward/pallas_call | solution.py:67
  168.0 7.5 %collective-permute-done.27 = bf16[4,2,96,768]{3,2,1,0:T(8,128)(2,1)S(1)} collective-permute-done((bf16[4,2,96,768]{3,2,1,0:T(8,128)(2,1)S(1)}, bf16[4,2,96,768]{3,2,1,0:T(8,128)(2,1)S(1)}, u32[]{:S(2)}, u32[]{:S(2)}) %collective-permute-start.27) | collective-permute-done | bytes 1179680 | tf_op jit(solution)/shard_map/ppermute | solution.py:133
  202.8 7.9 %slice.208 = bf16[3072,1536]{1,0:T(8,128)(2,1)} slice(bf16[3072,2304]{1,0:T(8,128)(2,1)} %all-gather.2.cloned.1.call-done), slice={[0:3072], [0:1536]} | slice | bytes 18874368 | tf_op jit(solution)/shard_map/slice | solution.py:410
  219.3 7.7 %attend_forward.3 = bf16[512,768]{1,0:T(8,128)(2,1)S(1)} custom-call(bf16[512,1536]{1,0:T(8,128)(2,1)S(1)} %fusion.30.q_ref.k_ref, bf16[512,1536]{1,0:T(8,128)(2,1)S(1)} %fusion.30.q_ref.k_ref, bf16[512,768]{1,0:T(8,128)(2,1)S(1)} %add_convert_fusion.4.v_ref), custom_call_target="tpu_custom_call" | custom-call | flops 201326592 | bytes 3145728 | tf_op jit(solution)/shard_map/attend_forward/pallas_call | solution.py:67
  228.3 6.5 %fusion.19 = (bf16[512,3072]{1,0:T(8,128)(2,1)S(1)}, f32[512,3072]{1,0:T(8,128)}) fusion(f32[3072]{0:T(1024)S(1)} %reshape.644, bf16[768,1536]{1,0:T(8,128)(2,1)S(1)} %bitcast.413, bf16[768,1536]{1,0:T(8,128)(2,1)S(1)} %bitcast.411, f32[512,768]{1,0:T(8,128)S(1)} %get-tuple-element.192, f32[768]{0:T(1024)S(1)} %reshape.643, f32[768]{0:T(1024)S(1)} %reshape.642, ...), kind=kOutput, calls=%fused_computation.25 | convolution fusion | flops 2443051008 | bytes 15751168 | tf_op jit(solution)/shard_map/dot_general | solution.py:318
  238.8 8.2 %fusion.157 = (f32[3072]{0:T(1024)S(1)}, bf16[512,3072]{1,0:T(8,128)(2,1)S(1)}) fusion(f32[512,3072]{1,0:T(8,128)} %get-tuple-element.115, bf16[3072,2304]{1,0:T(8,128)(2,1)S(1)} %bitcast.393, f32[512,768]{1,0:T(8,128)S(1)} %copy-done.24), kind=kOutput, calls=%fused_computation.433 | convolution fusion | flops 2449339392 | bytes 15740928 | tf_op jit(solution)/shard_map/dot_general | solution.py:22
  257.1 5.2 convolution_convert_fusion.2
  267.5 17.7 %attend_backward.2 = (bf16[512,1536]{1,0:T(8,128)(2,1)S(1)}, bf16[512,768]{1,0:T(8,128)(2,1)S(1)}) custom-call(bf16[512,1536]{1,0:T(8,128)(2,1)S(1)} %fusion.30.q_ref.k_ref, bf16[512,1536]{1,0:T(8,128)(2,1)S(1)} %fusion.30.q_ref.k_ref, bf16[512,768]{1,0:T(8,128)(2,1)S(1)} %add_convert_fusion.4.v_ref, bf16[512,768]{1,0:T(8,128)(2,1)S(1)} %convolution_convert_fusion.11.g_ref), custom_call_target="tpu_custom_call" | custom-call | flops 201326592 | bytes 5505024 | tf_op jit(solution)/shard_map/attend_backward/pallas_call | solution.py:113
  322.4 7.7 %fusion.142 = (f32[3072]{0:T(1024)S(1)}, bf16[512,3072]{1,0:T(8,128)(2,1)}) fusion(f32[512,3072]{1,0:T(8,128)S(1)} %bitcast.391, f32[3072]{0:T(1024)S(1)} %reshape.637, bf16[512,768]{1,0:T(8,128)(2,1)S(1)} %add_convert_fusion.1, bf16[3072,768]{1,0:T(8,128)(2,1)S(1)} %bitcast.397), kind=kOutput, calls=%fused_computation.421 | convolution fusion | flops 2450519040 | bytes 14966784 | tf_op jit(solution)/shard_map/dot_general | solution.py:22
  352.1 7.0 %collective-permute-done.38 = bf16[4,2,96,768]{3,2,0,1:T(8,128)(2,1)} collective-permute-done((bf16[4,2,96,768]{3,2,0,1:T(8,128)(2,1)}, bf16[4,2,96,768]{3,2,0,1:T(8,128)(2,1)}, u32[]{:S(2)}, u32[]{:S(2)}) %collective-permute-start.38) | collective-permute-done | bytes 1179680 | tf_op jit(solution)/shard_map/ppermute | solution.py:133
  393.0 17.5 %attend_backward.3 = (bf16[512,1536]{1,0:T(8,128)(2,1)S(1)}, bf16[512,768]{1,0:T(8,128)(2,1)S(1)}) custom-call(bf16[512,1536]{1,0:T(8,128)(2,1)S(1)} %copy-done.1, bf16[512,1536]{1,0:T(8,128)(2,1)S(1)} %copy-done.1, bf16[512,768]{1,0:T(8,128)(2,1)S(1)} %copy-done.3, bf16[512,768]{1,0:T(8,128)(2,1)S(1)} %convolution_convert_fusion.10.g_ref), custom_call_target="tpu_custom_call" | custom-call | flops 201326592 | bytes 5505024 | tf_op jit(solution)/shard_map/attend_backward/pallas_call | solution.py:113
  448.6 12.0 %collective-permute-done.55 = bf16[4,24,1536]{2,1,0:T(8,128)(2,1)S(1)} collective-permute-done((bf16[4,24,1536]{2,1,0:T(8,128)(2,1)S(1)}, bf16[4,24,1536]{2,1,0:T(8,128)(2,1)S(1)}, u32[]{:S(2)}, u32[]{:S(2)}) %collective-permute-start.55) | collective-permute-done | bytes 294944 | tf_op jit(solution)/shard_map/ppermute | solution.py:133
  469.7 7.9 %collective-permute-done.50 = bf16[4,2,24,1536]{3,2,0,1:T(8,128)(2,1)S(1)} collective-permute-done((bf16[4,2,24,1536]{3,2,0,1:T(8,128)(2,1)S(1)}, bf16[4,2,24,1536]{3,2,0,1:T(8,128)(2,1)S(1)}, u32[]{:S(2)}, u32[]{:S(2)}) %collective-permute-start.50) | collective-permute-done | bytes 589856 | tf_op jit(solution)/shard_map/ppermute | solution.py:133
  480.0 19.6 %collective-permute-done.48 = bf16[4,2,24,1536]{3,2,0,1:T(8,128)(2,1)S(1)} collective-permute-done((bf16[4,2,24,1536]{3,2,0,1:T(8,128)(2,1)S(1)}, bf16[4,2,24,1536]{3,2,0,1:T(8,128)(2,1)S(1)}, u32[]{:S(2)}, u32[]{:S(2)}) %collective-permute-start.48) | collective-permute-done | bytes 589856 | tf_op jit(solution)/shard_map/ppermute | solution.py:133
  501.2 5.1 collective-permute-done.51
  506.3 12.8 %collective-permute-done.49 = bf16[4,24,1536]{2,1,0:T(8,128)(2,1)S(1)} collective-permute-done((bf16[4,24,1536]{2,1,0:T(8,128)(2,1)S(1)}, bf16[4,24,1536]{2,1,0:T(8,128)(2,1)S(1)}, u32[]{:S(2)}, u32[]{:S(2)}) %collective-permute-start.49) | collective-permute-done | bytes 294944 | tf_op jit(solution)/shard_map/ppermute | solution.py:133
  530.9 5.6 collective-permute-start.66
  536.6 5.0 collective-permute-done.53
  542.3 9.2 %collective-permute-start.61 = (bf16[24,3072]{1,0:T(8,128)(2,1)}, bf16[24,3072]{1,0:T(8,128)(2,1)}, u32[]{:S(2)}, u32[]{:S(2)}) collective-permute-start(bf16[24,3072]{1,0:T(8,128)(2,1)} %get-tuple-element.250), channel_id=1, source_target_pairs={{0,4},{1,5},{2,6},{3,7},{4,8},{5,9},{6,10},{7,11},{8,12},{9,13},{1... | collective-permute-start | bytes 442376 | tf_op jit(solution)/shard_map/ppermute | solution.py:133
  (687 shorter events, 318.4 us)
Async XLA Ops:
  7.2 195.0 %all-gather.2.cloned.1.call-start = ((), (), s32[]{:S(2)}) async-start(), calls=%async_computation.1 | async-start | bytes 14598144 | tf_op jit(solution)/shard_map/all_gather | solution.py:405
  23.8 535.9 %reduce-scatter.2.cloned.1.call-start = ((), (), s32[]{:S(2)}) async-start(), calls=%async_computation.2 | async-start | bytes 9732096 | tf_op jit(solution)/shard_map/reduce_scatter | solution.py:424
  97.5 25.4 %collective-permute-start.18 = (bf16[4,2,24,1536]{3,2,1,0:T(8,128)(2,1)S(1)}, bf16[4,2,24,1536]{3,2,1,0:T(8,128)(2,1)S(1)}, u32[]{:S(2)}, u32[]{:S(2)}) collective-permute-start(bf16[4,2,24,1536]{3,2,1,0:T(8,128)(2,1)S(1)} %pad_maximum_fusion.18), channel_id=1, source_target_pairs={{0,2},{1,3},{2,0},{3,1},{4,6},{5,7},{6,4},{7,5},{8,10},{9,11},{10,... | collective-permute-start | bytes 1769480 | tf_op jit(solution)/shard_map/ppermute | solution.py:133
  99.0 23.5 %collective-permute-start.17 = (bf16[4,2,24,1536]{3,2,0,1:T(8,128)(2,1)S(1)}, bf16[4,2,24,1536]{3,2,0,1:T(8,128)(2,1)S(1)}, u32[]{:S(2)}, u32[]{:S(2)}) collective-permute-start(bf16[4,2,24,1536]{3,2,0,1:T(8,128)(2,1)S(1)} %pad_maximum_fusion.17), channel_id=1, source_target_pairs={{0,16},{16,0},{1,17},{17,1},{2,18},{18,2},{3,19},{19,3},{4,20},{20... | collective-permute-start | bytes 1769480 | tf_op jit(solution)/shard_map/ppermute | solution.py:133
  123.1 27.5 %collective-permute-start.25 = (bf16[4,96,768]{2,1,0:T(8,128)(2,1)S(1)}, bf16[4,96,768]{2,1,0:T(8,128)(2,1)S(1)}, u32[]{:S(2)}, u32[]{:S(2)}) collective-permute-start(bf16[4,96,768]{2,1,0:T(8,128)(2,1)S(1)} %bitcast_dynamic-update-slice_fusion), channel_id=1, source_target_pairs={{0,16},{16,0},{1,17},{17,1},{2,18},{18,2},{3,19},{19,3},{4,20},{20... | collective-permute-start | bytes 1769480 | tf_op jit(solution)/shard_map/ppermute | solution.py:133
  126.0 25.5 %collective-permute-start.24 = (bf16[4,24,3072]{2,1,0:T(8,128)(2,1)S(1)}, bf16[4,24,3072]{2,1,0:T(8,128)(2,1)S(1)}, u32[]{:S(2)}, u32[]{:S(2)}) collective-permute-start(bf16[4,24,3072]{2,1,0:T(8,128)(2,1)S(1)} %bitcast_dynamic-update-slice_fusion.4), channel_id=1, source_target_pairs={{0,2},{1,3},{2,0},{3,1},{4,6},{5,7},{6,4},{7,5},{8,10},{9,11},{10,... | collective-permute-start | bytes 1769480 | tf_op jit(solution)/shard_map/ppermute | solution.py:133
  126.5 25.3 %collective-permute-start.23 = (bf16[4,2,2,24,1536]{4,3,2,1,0:T(8,128)(2,1)S(1)}, bf16[4,2,2,24,1536]{4,3,2,1,0:T(8,128)(2,1)S(1)}, u32[]{:S(2)}, u32[]{:S(2)}) collective-permute-start(bf16[4,2,2,24,1536]{4,3,2,1,0:T(8,128)(2,1)S(1)} %pad_maximum_fusion.13), channel_id=1, source_target_pairs={{0,1},{1,0},{2,3},{3,2},{4,5},{5,4},{6,7},{7,6},{8,9},{9,8},{10,11... | collective-permute-start | bytes 3538952 | tf_op jit(solution)/shard_map/ppermute | solution.py:133
  126.6 25.9 %collective-permute-start.22 = (bf16[4,2,2,24,1536]{4,3,2,1,0:T(8,128)(2,1)S(1)}, bf16[4,2,2,24,1536]{4,3,2,1,0:T(8,128)(2,1)S(1)}, u32[]{:S(2)}, u32[]{:S(2)}) collective-permute-start(bf16[4,2,2,24,1536]{4,3,2,1,0:T(8,128)(2,1)S(1)} %copy.159), channel_id=1, source_target_pairs={{0,1},{1,0},{2,3},{3,2},{4,5},{5,4},{6,7},{7,6},{8,9},{9,8},{10,11... | collective-permute-start | bytes 3538952 | tf_op jit(solution)/shard_map/ppermute | solution.py:133
  152.9 22.5 %collective-permute-start.27 = (bf16[4,2,96,768]{3,2,1,0:T(8,128)(2,1)S(1)}, bf16[4,2,96,768]{3,2,1,0:T(8,128)(2,1)S(1)}, u32[]{:S(2)}, u32[]{:S(2)}) collective-permute-start(bf16[4,2,96,768]{3,2,1,0:T(8,128)(2,1)S(1)} %pad_maximum_fusion.15), channel_id=1, source_target_pairs={{0,2},{1,3},{2,0},{3,1},{4,6},{5,7},{6,4},{7,5},{8,10},{9,11},{10,... | collective-permute-start | bytes 3538952 | tf_op jit(solution)/shard_map/ppermute | solution.py:133
  154.5 23.0 %collective-permute-start.26 = (bf16[4,2,24,3072]{3,2,0,1:T(8,128)(2,1)S(1)}, bf16[4,2,24,3072]{3,2,0,1:T(8,128)(2,1)S(1)}, u32[]{:S(2)}, u32[]{:S(2)}) collective-permute-start(bf16[4,2,24,3072]{3,2,0,1:T(8,128)(2,1)S(1)} %pad_maximum_fusion.14), channel_id=1, source_target_pairs={{0,16},{16,0},{1,17},{17,1},{2,18},{18,2},{3,19},{19,3},{4,20},{20... | collective-permute-start | bytes 3538952 | tf_op jit(solution)/shard_map/ppermute | solution.py:133
  331.2 27.9 %collective-permute-start.38 = (bf16[4,2,96,768]{3,2,0,1:T(8,128)(2,1)}, bf16[4,2,96,768]{3,2,0,1:T(8,128)(2,1)}, u32[]{:S(2)}, u32[]{:S(2)}) collective-permute-start(bf16[4,2,96,768]{3,2,0,1:T(8,128)(2,1)} %dynamic-slice_bitcast_fusion), channel_id=1, source_target_pairs={{0,2},{1,3},{2,0},{3,1},{4,6},{5,7},{6,4},{7,5},{8,10},{9,11},{10,... | collective-permute-start | bytes 3538952 | tf_op jit(solution)/shard_map/ppermute | solution.py:133
  334.0 28.6 %collective-permute-start.36 = (bf16[4,2,24,3072]{3,2,0,1:T(8,128)(2,1)}, bf16[4,2,24,3072]{3,2,0,1:T(8,128)(2,1)}, u32[]{:S(2)}, u32[]{:S(2)}) collective-permute-start(bf16[4,2,24,3072]{3,2,0,1:T(8,128)(2,1)} %dynamic-slice_bitcast_fusion.1), channel_id=1, source_target_pairs={{0,16},{16,0},{1,17},{17,1},{2,18},{18,2},{3,19},{19,3},{4,20},{20... | collective-permute-start | bytes 3538952 | tf_op jit(solution)/shard_map/ppermute | solution.py:133
  337.6 41.3 %collective-permute-start.33 = (bf16[4,2,2,24,3072]{4,3,0,2,1:T(8,128)(2,1)}, bf16[4,2,2,24,3072]{4,3,0,2,1:T(8,128)(2,1)}, u32[]{:S(2)}, u32[]{:S(2)}) collective-permute-start(bf16[4,2,2,24,3072]{4,3,0,2,1:T(8,128)(2,1)} %bitcast.375), channel_id=1, source_target_pairs={{0,1},{1,0},{2,3},{3,2},{4,5},{5,4},{6,7},{7,6},{8,9},{9,8},{10,11... | collective-permute-start | bytes 7077896 | tf_op jit(solution)/shard_map/ppermute | solution.py:133
  382.6 27.9 %collective-permute-start.35 = (bf16[4,2,24,1536]{3,2,0,1:T(8,128)(2,1)}, bf16[4,2,24,1536]{3,2,0,1:T(8,128)(2,1)}, u32[]{:S(2)}, u32[]{:S(2)}) collective-permute-start(bf16[4,2,24,1536]{3,2,0,1:T(8,128)(2,1)} %dynamic-slice_bitcast_fusion.6), channel_id=1, source_target_pairs={{0,2},{1,3},{2,0},{3,1},{4,6},{5,7},{6,4},{7,5},{8,10},{9,11},{10,... | collective-permute-start | bytes 1769480 | tf_op jit(solution)/shard_map/ppermute | solution.py:133
  385.1 27.3 %collective-permute-start.34 = (bf16[4,2,24,1536]{3,2,0,1:T(8,128)(2,1)}, bf16[4,2,24,1536]{3,2,0,1:T(8,128)(2,1)}, u32[]{:S(2)}, u32[]{:S(2)}) collective-permute-start(bf16[4,2,24,1536]{3,2,0,1:T(8,128)(2,1)} %dynamic-slice_bitcast_fusion.7), channel_id=1, source_target_pairs={{0,16},{16,0},{1,17},{17,1},{2,18},{18,2},{3,19},{19,3},{4,20},{20... | collective-permute-start | bytes 1769480 | tf_op jit(solution)/shard_map/ppermute | solution.py:133
  415.8 31.8 %collective-permute-start.56 = (bf16[4,24,1536]{2,1,0:T(8,128)(2,1)}, bf16[4,24,1536]{2,1,0:T(8,128)(2,1)}, u32[]{:S(2)}, u32[]{:S(2)}) collective-permute-start(bf16[4,24,1536]{2,1,0:T(8,128)(2,1)} %dynamic-slice_bitcast_fusion.8), channel_id=1, source_target_pairs={{0,16},{16,0},{1,17},{17,1},{2,18},{18,2},{3,19},{19,3},{4,20},{20... | collective-permute-start | bytes 884744 | tf_op jit(solution)/shard_map/ppermute | solution.py:133
  423.7 37.0 %collective-permute-start.47 = (bf16[4,2,2,24,3072]{4,3,0,2,1:T(8,128)(2,1)}, bf16[4,2,2,24,3072]{4,3,0,2,1:T(8,128)(2,1)}, u32[]{:S(2)}, u32[]{:S(2)}) collective-permute-start(bf16[4,2,2,24,3072]{4,3,0,2,1:T(8,128)(2,1)} %bitcast.374), channel_id=1, source_target_pairs={{0,1},{1,0},{2,3},{3,2},{4,5},{5,4},{6,7},{7,6},{8,9},{9,8},{10,11... | collective-permute-start | bytes 7077896 | tf_op jit(solution)/shard_map/ppermute | solution.py:133
  446.7 106.2 %collective-permute-start.40 = (bf16[512,768]{1,0:T(8,128)(2,1)}, bf16[512,768]{1,0:T(8,128)(2,1)}, u32[]{:S(2)}, u32[]{:S(2)}) collective-permute-start(bf16[512,768]{1,0:T(8,128)(2,1)} %broadcast_select_fusion), channel_id=1, source_target_pairs={{0,16},{16,0},{1,17},{17,1},{2,18},{18,2},{3,19},{19,3},{4,20},{20... | collective-permute-start | bytes 2359304 | tf_op jit(solution)/shard_map/ppermute | solution.py:133
  464.7 55.3 %collective-permute-start.57 = (bf16[24,3072]{1,0:T(8,128)(2,1)S(1)}, bf16[24,3072]{1,0:T(8,128)(2,1)}, u32[]{:S(2)}, u32[]{:S(2)}) collective-permute-start(bf16[24,3072]{1,0:T(8,128)(2,1)S(1)} %get-tuple-element.253), channel_id=1, source_target_pairs={{0,4},{1,5},{2,6},{3,7},{4,8},{5,9},{6,10},{7,11},{8,12},{9,13},{1... | collective-permute-start | bytes 442376 | tf_op jit(solution)/shard_map/ppermute | solution.py:133
  465.3 54.7 %collective-permute-start.58 = (bf16[24,3072]{1,0:T(8,128)(2,1)S(1)}, bf16[24,3072]{1,0:T(8,128)(2,1)}, u32[]{:S(2)}, u32[]{:S(2)}) collective-permute-start(bf16[24,3072]{1,0:T(8,128)(2,1)S(1)} %get-tuple-element.254), channel_id=1, source_target_pairs={{0,8},{1,9},{2,10},{3,11},{4,12},{5,13},{6,14},{7,15},{8,0},{9,1},... | collective-permute-start | bytes 442376 | tf_op jit(solution)/shard_map/ppermute | solution.py:133
  466.8 58.8 %collective-permute-start.59 = (bf16[24,3072]{1,0:T(8,128)(2,1)}, bf16[24,3072]{1,0:T(8,128)(2,1)}, u32[]{:S(2)}, u32[]{:S(2)}) collective-permute-start(bf16[24,3072]{1,0:T(8,128)(2,1)} %get-tuple-element.255), channel_id=1, source_target_pairs={{0,12},{1,13},{2,14},{3,15},{4,0},{5,1},{6,2},{7,3},{8,4},{9,5},{1... | collective-permute-start | bytes 442376 | tf_op jit(solution)/shard_map/ppermute | solution.py:133
  525.6 35.3 %collective-permute-start.65 = (bf16[96,768]{1,0:T(8,128)(2,1)}, bf16[96,768]{1,0:T(8,128)(2,1)}, u32[]{:S(2)}, u32[]{:S(2)}) collective-permute-start(bf16[96,768]{1,0:T(8,128)(2,1)} %get-tuple-element.247), channel_id=1, source_target_pairs={{0,4},{1,5},{2,6},{3,7},{4,8},{5,9},{6,10},{7,11},{8,12},{9,13},{1... | collective-permute-start | bytes 442376 | tf_op jit(solution)/shard_map/ppermute | solution.py:133
  530.9 32.4 %collective-permute-start.66 = (bf16[96,768]{1,0:T(8,128)(2,1)}, bf16[96,768]{1,0:T(8,128)(2,1)}, u32[]{:S(2)}, u32[]{:S(2)}) collective-permute-start(bf16[96,768]{1,0:T(8,128)(2,1)} %get-tuple-element.249), channel_id=1, source_target_pairs={{0,8},{1,9},{2,10},{3,11},{4,12},{5,13},{6,14},{7,15},{8,0},{9,1},... | collective-permute-start | bytes 442376 | tf_op jit(solution)/shard_map/ppermute | solution.py:133
  542.3 22.8 %collective-permute-start.61 = (bf16[24,3072]{1,0:T(8,128)(2,1)}, bf16[24,3072]{1,0:T(8,128)(2,1)}, u32[]{:S(2)}, u32[]{:S(2)}) collective-permute-start(bf16[24,3072]{1,0:T(8,128)(2,1)} %get-tuple-element.250), channel_id=1, source_target_pairs={{0,4},{1,5},{2,6},{3,7},{4,8},{5,9},{6,10},{7,11},{8,12},{9,13},{1... | collective-permute-start | bytes 442376 | tf_op jit(solution)/shard_map/ppermute | solution.py:133
  (176 other events, 1679.6 us)
Sparse Core Ops, SparseCore 0:
  23.9 148.1 all-gather.1
  391.5 166.5 reduce-scatter.1
